TPU v7x, 128 devices: a whole 4x4x4 slice. The times are simulated.
128 devices in a mesh: dp: 8 (over y, core), seq: 16 (over x, z).
Axes of the slice: x: 4, y: 4, z: 4, core: 2. Of those that a mesh axis runs over, the one named last changes fastest.
Arguments:
- nodes: bfloat16 [8, 2048, 1024], P('dp', 'seq'), may hold values from -6 to 6
- w_qkv: bfloat16 [1024, 3072], replicated, as said below
- w_out: bfloat16 [1024, 1024], replicated, may hold values from -0.1875 to 0.1875
- cotangent: bfloat16 [8, 2048, 1024], P('dp', 'seq'), may hold values from -6 to 6
- order: int32 [8, 2048], P('dp'), may hold values from 0 to 2047, each once within a row
- block_list: int32 [8, 32, 8], P('dp'), may hold values from 0 to 31, as said below
- block_count: int32 [8, 32], P('dp'), may hold values from 1 to 8, as said below
Outputs:
- mixed: bfloat16 [8, 2048, 1024], P('dp', 'seq')
- grad_nodes: bfloat16 [8, 2048, 1024], P('dp', 'seq')
- grad_qkv: float32 [1024, 3072], P(('dp', 'seq'))
- grad_out: float32 [1024, 1024], P(('dp', 'seq'))
Inputs may be any that keep to these rules, and one draw needn't show every extreme that they name: Columns of w_qkv are ordered by head, then query, key, value, then the head's 64 features. `block_list`: each row lists 8 different key blocks, the first being the query block itself; only the first block_count entries are used. `block_count`: in every batch some query block uses all 8 entries.
All inputs are finite; a program needn't handle non-finite values.
Results may differ from a plain program's by a relative error of at most 0.017.
Values may be sent and summed in bfloat16 or wider, within the bound.
No kernel may reach another device: no remote copies, remote signals or barrier semaphores. Data moves between devices by JAX's collectives and lax.ppermute only.
A program may use at most 128 MiB of HBM per device.

v0:
```python
import math

import jax
import jax.numpy as jnp
from jax import lax
from jax.sharding import PartitionSpec as P

H = 16
HD = 64
D = 1024
BLK = 64
MAXB = 8
GROUP = 8


EPS = 1e-05


def fetch_blocks(source, chosen):
    gathered = source[chosen]
    return gathered.reshape(chosen.shape[0], chosen.shape[1] * source.shape[1], source.shape[2])


def block_probs(queries, keyed, tally, scale):
    scores = jnp.einsum("gqe,gke->gqk", queries, keyed, preferred_element_type=jnp.float32) * scale
    usable = jnp.arange(MAXB)[None, :] < tally[:, None]
    usable = jnp.repeat(usable, BLK, axis=1)[:, None, :]
    scores = jnp.where(usable, scores, jnp.float32(-1e30))
    highest = jnp.max(scores, axis=-1, keepdims=True)
    expo = jnp.exp(scores - highest)
    return expo / jnp.sum(expo, axis=-1, keepdims=True)


def head_forward(queries, keys_all, values_all, picked, counted):
    nblk = picked.shape[0]
    width = queries.shape[1]
    scale = 1.0 / math.sqrt(width)
    key_table = keys_all.reshape(nblk, BLK, width)
    value_table = values_all.reshape(nblk, BLK, width)
    query_groups = queries.reshape(nblk // GROUP, GROUP, BLK, width)

    def per_group(packed_in):
        query_block, chosen, tally = packed_in
        keyed = fetch_blocks(key_table, chosen)
        valued = fetch_blocks(value_table, chosen)
        probs_low = block_probs(query_block, keyed, tally, scale).astype(jnp.bfloat16)
        result = jnp.einsum("gqk,gke->gqe", probs_low, valued, preferred_element_type=jnp.float32)
        return result.astype(jnp.bfloat16)

    outputs = lax.map(
        per_group,
        (
            query_groups,
            picked.reshape(nblk // GROUP, GROUP, MAXB),
            counted.reshape(nblk // GROUP, GROUP),
        ),
    )
    return outputs.reshape(nblk * BLK, width)


def head_backward(queries, keys_all, values_all, grad_in, picked, counted):
    nblk = picked.shape[0]
    width = queries.shape[1]
    scale = 1.0 / math.sqrt(width)
    key_table = keys_all.reshape(nblk, BLK, width)
    value_table = values_all.reshape(nblk, BLK, width)
    query_groups = queries.reshape(nblk // GROUP, GROUP, BLK, width)
    grad_groups = grad_in.reshape(nblk // GROUP, GROUP, BLK, width)

    def per_group(carry, packed_in):
        key_acc, value_acc = carry
        query_block, grad_block, chosen, tally = packed_in
        keyed = fetch_blocks(key_table, chosen)
        valued = fetch_blocks(value_table, chosen)
        probs = block_probs(query_block, keyed, tally, scale)
        probs_low = probs.astype(jnp.bfloat16)
        grad_probs = jnp.einsum(
            "gqe,gke->gqk", grad_block, valued, preferred_element_type=jnp.float32
        )
        delta = jnp.sum(grad_probs * probs, axis=-1, keepdims=True)
        grad_scores = (probs * (grad_probs - delta) * scale).astype(jnp.bfloat16)
        grad_query = jnp.einsum(
            "gqk,gke->gqe", grad_scores, keyed, preferred_element_type=jnp.float32
        ).astype(jnp.bfloat16)
        key_part = jnp.einsum(
            "gqk,gqe->gke", grad_scores, query_block, preferred_element_type=jnp.float32
        )
        value_part = jnp.einsum(
            "gqk,gqe->gke", probs_low, grad_block, preferred_element_type=jnp.float32
        )
        flat = chosen.reshape(-1)
        key_acc = key_acc.at[flat].add(key_part.reshape(-1, BLK, width))
        value_acc = value_acc.at[flat].add(value_part.reshape(-1, BLK, width))
        return ((key_acc, value_acc), grad_query)

    start_acc = jnp.zeros((nblk, BLK, width), jnp.float32)
    (key_acc, value_acc), grad_queries = lax.scan(
        per_group,
        (start_acc, start_acc),
        (
            query_groups,
            grad_groups,
            picked.reshape(nblk // GROUP, GROUP, MAXB),
            counted.reshape(nblk // GROUP, GROUP),
        ),
    )
    grad_queries = grad_queries.reshape(nblk * BLK, width)
    grad_keys = key_acc.reshape(nblk * BLK, width).astype(jnp.bfloat16)
    grad_values = value_acc.reshape(nblk * BLK, width).astype(jnp.bfloat16)
    return jnp.concatenate([grad_queries, grad_keys, grad_values], axis=1)


def attend_all(clustered, picked, counted):
    width = clustered.shape[2] // 3
    per_head = jnp.moveaxis(clustered, 1, 0)

    def single(head_rows):
        return head_forward(
            head_rows[:, :width],
            head_rows[:, width : 2 * width],
            head_rows[:, 2 * width :],
            picked,
            counted,
        )

    return jnp.moveaxis(lax.map(single, per_head), 0, 1)


def attend_back(clustered, grad_cluster, picked, counted):
    width = clustered.shape[2] // 3
    per_head = (jnp.moveaxis(clustered, 1, 0), jnp.moveaxis(grad_cluster, 1, 0))

    def single(pair):
        head_rows, head_grad = pair
        return head_backward(
            head_rows[:, :width],
            head_rows[:, width : 2 * width],
            head_rows[:, 2 * width :],
            head_grad,
            picked,
            counted,
        )

    return jnp.moveaxis(lax.map(single, per_head), 0, 1)


def shards(nodes, w_qkv, w_out, cotangent, order, block_list, block_count):
    contract_rows = (((0,), (0,)), ((), ()))
    contract_cols = (((1,), (1,)), ((), ()))
    features = nodes[0]
    upstream = cotangent[0]
    ordering = order[0]
    picked = block_list[0]
    counted = block_count[0]
    local_rows = features.shape[0]
    wide_in = features.astype(jnp.float32)
    inv_rms = lax.rsqrt(jnp.mean(wide_in * wide_in, axis=-1, keepdims=True) + EPS)
    normed = (wide_in * inv_rms).astype(jnp.bfloat16)
    packed_local = (
        jnp.dot(normed, w_qkv, preferred_element_type=jnp.float32)
        .astype(jnp.bfloat16)
        .reshape(1, local_rows, H, 3 * HD)
    )
    head_packed = lax.all_to_all(packed_local, "seq", split_axis=2, concat_axis=1, tiled=True)
    all_nodes = head_packed.shape[1]
    inverse = (
        jnp.zeros((all_nodes,), jnp.int32).at[ordering].set(jnp.arange(all_nodes, dtype=jnp.int32))
    )
    clustered = head_packed[0][ordering]
    attn_heads = attend_all(clustered, picked, counted)[inverse]
    attn = lax.all_to_all(attn_heads[None], "seq", split_axis=1, concat_axis=2, tiled=True)[
        0
    ].reshape(local_rows, D)
    mixed = (wide_in + jnp.dot(attn, w_out, preferred_element_type=jnp.float32)).astype(
        jnp.bfloat16
    )
    projected = lax.dot_general(upstream, w_out, contract_cols, preferred_element_type=jnp.float32)
    head_grad = lax.all_to_all(
        projected.astype(jnp.bfloat16).reshape(1, local_rows, H, HD),
        "seq",
        split_axis=2,
        concat_axis=1,
        tiled=True,
    )
    grad_heads = attend_back(clustered, head_grad[0][ordering], picked, counted)[inverse]
    grad_packed = lax.all_to_all(grad_heads[None], "seq", split_axis=1, concat_axis=2, tiled=True)[
        0
    ].reshape(local_rows, 3 * D)
    grad_normed = lax.dot_general(
        grad_packed, w_qkv, contract_cols, preferred_element_type=jnp.float32
    )
    inner = jnp.mean(grad_normed * wide_in, axis=-1, keepdims=True)
    grad_features = (
        upstream.astype(jnp.float32)
        + inv_rms * grad_normed
        - wide_in * inv_rms * inv_rms * inv_rms * inner
    ).astype(jnp.bfloat16)
    part_qkv = lax.dot_general(
        normed, grad_packed, contract_rows, preferred_element_type=jnp.float32
    )
    part_out = lax.dot_general(attn, upstream, contract_rows, preferred_element_type=jnp.float32)
    summed = lax.psum_scatter(
        jnp.concatenate([part_qkv, part_out], axis=1),
        ("dp", "seq"),
        scatter_dimension=0,
        tiled=True,
    )
    return (mixed[None], grad_features[None], summed[:, : 3 * D], summed[:, 3 * D :])


def solution(mesh):
    return jax.shard_map(
        shards,
        mesh=mesh,
        in_specs=(
            P("dp", "seq", None),
            P(),
            P(),
            P("dp", "seq", None),
            P("dp", None),
            P("dp", None, None),
            P("dp", None),
        ),
        out_specs=(
            P("dp", "seq", None),
            P("dp", "seq", None),
            P(("dp", "seq"), None),
            P(("dp", "seq"), None),
        ),
        check_vma=False,
    )
```

profile of v0, /device:TPU:0, one launch (start us, length us, event | category | flops | bytes accessed | tf_op | source)
XLA Modules:
  0.0 1094.1 jit_solution(13564174745725181313)
XLA Ops:
  11.4 8.0 all-to-all-start.2
  20.9 3.8 convolution_convert_fusion.2
  25.9 2.0 all-to-all-done.2
  27.9 5.3 all-to-all-start
  33.2 8.2 scatter_custom_fusion.2
  41.7 8.0 gather_fusion.6
  51.2 9.0 gather_fusion.4
  60.2 2.4 fusion.80
  63.5 41.6 %while.40 = (s32[]{:T(128)}, bf16[4,8,64,64]{3,2,1,0:T(8,128)(2,1)}, s32[4,8]{1,0:T(4,128)S(1)}, bf16[4,8,64,64]{3,2,1,0:T(8,128)(2,1)}, s32[4,8,8]{2,1,0:T(8,12...) while((s32[]{:T(128)}, bf16[4,8,64,64]{3,2,1,0:T(8,128)(2,1)}, ...), condition=%wide.region_4.5_spmd, body=%wide.region_1.4_spmd.sunk | while | flops 68979456 | bytes 12871785 | solution.py:50
  65.5 1.8 fusion.133
  70.3 3.6 fusion.135
  75.9 1.8 fusion.133
  80.7 3.6 fusion.135
  91.1 3.6 fusion.135
  96.7 1.8 fusion.133
  101.5 3.6 fusion.135
  105.1 8.7 gather_fusion.5
  113.8 2.6 copy.121
  116.9 13.4 %reduce.4 = bf16[2048,64]{1,0:T(8,128)(2,1)} reduce(bf16[2048,1,1,64]{3,2,1,0:T(2,128)(2,1)} %bitcast.229, bf16[]{:T(256)} %broadcast.187), dimensions={1,2}, to_apply=%bitcast.155.reduce_sub_computation | reduce | bytes 524290
  130.3 2.1 reshape.360
  132.4 7.2 all-to-all-start.1
  142.9 194.6 %while.41 = (s32[]{:T(128)}, f32[32,64,64]{2,1,0:T(8,128)}, f32[32,64,64]{2,1,0:T(8,128)}, bf16[4,8,64,64]{3,2,1,0:T(8,128)(2,1)}, s32[4,8,8]{2,1,0:T(8,128)S(1)...) while((s32[]{:T(128)}, f32[32,64,64]{2,1,0:T(8,128)}, ...), condition=%wide.region_12.13_spmd, body=%wide.region_6.0_spmd.sunk | while | flops 173839296 | bytes 33206156 | solution.py:97
  145.0 2.8 fusion.151
  149.5 2.8 fusion.149
  153.5 5.9 fusion.155
  159.5 7.1 fusion.153
  166.6 10.3 scatter_fusion
  176.9 4.3 fusion.154
  181.2 10.3 scatter_fusion.1
  193.7 2.8 fusion.151
  198.2 2.8 fusion.149
  202.2 5.9 fusion.155
  208.1 7.1 fusion.153
  215.2 10.3 scatter_fusion
  225.6 4.3 fusion.154
  229.9 10.3 scatter_fusion.1
  242.3 2.8 fusion.151
  246.8 2.8 fusion.149
  250.9 5.9 fusion.155
  256.8 7.1 fusion.153
  263.9 10.3 scatter_fusion
  274.2 4.3 fusion.154
  278.5 10.3 scatter_fusion.1
  291.0 2.8 fusion.151
  295.4 2.8 fusion.149
  299.5 5.9 fusion.155
  305.4 7.1 fusion.153
  312.5 10.4 scatter_fusion
  322.9 4.3 fusion.154
  327.2 10.4 scatter_fusion.1
  339.8 9.0 gather_fusion.7
  348.7 4.3 copy.120
  353.1 12.7 %reduce.5 = bf16[2048,192]{1,0:T(8,128)(2,1)S(1)} reduce(bf16[2048,1,1,192]{3,2,1,0:T(2,128)(2,1)} %bitcast.223, bf16[]{:T(256)} %broadcast.187), dimensions={1,2}, to_apply=%bitcast.154.reduce_sub_computation | reduce | bytes 1572866
  365.7 2.1 reshape.362
  367.8 7.2 all-to-all-start.3
  375.3 2.2 reshape.361
  380.3 3.6 fusion.70
  383.8 3.9 all-to-all-done.3
  387.7 5.9 reshape.363
  393.7 4.5 copy.101
  398.5 1.9 fusion.66
  400.7 6.0 pad_maximum_fusion
  407.9 5.1 fusion.63
  414.0 670.4 %reduce-scatter.2.cloned.1.call-done = f32[8,4096]{1,0:T(8,128)} async-done(((f32[1024,4096]{1,0:T(8,128)}), f32[8,4096]{1,0:T(8,128)}) %reduce-scatter.2.cloned.1.call-update) | async-done | bytes 131088 | tf_op jit(solution)/shard_map/reduce_scatter | solution.py:202
  (160 shorter events, 66.1 us)
Async XLA Ops:
  7.2 1.6 copy-start
  7.2 12.2 %copy-start.5 = (bf16[1,128,1024]{2,1,0:T(8,128)(2,1)S(1)}, bf16[1,128,1024]{2,1,0:T(8,128)(2,1)}, u32[]{:S(2)}) copy-start(bf16[1,128,1024]{2,1,0:T(8,128)(2,1)} %param.11) | copy-start | bytes 786436
  7.2 12.8 %copy-start.10 = (s32[1,32]{1,0:T(1,128)S(1)}, s32[1,32]{1,0:T(1,128)}, u32[]{:S(2)}) copy-start(s32[1,32]{1,0:T(1,128)} %param.17) | copy-start | bytes 388
  7.2 13.6 %copy-start.9 = (s32[1,32,8]{1,2,0:T(8,128)S(1)}, s32[1,32,8]{1,2,0:T(8,128)}, u32[]{:S(2)}) copy-start(s32[1,32,8]{1,2,0:T(8,128)} %param.16) | copy-start | bytes 3076
  11.4 16.5 %all-to-all-start.2 = ((bf16[1,128,16,64]{1,3,0,2:T(8,128)(2,1)}), bf16[1,128,16,64]{1,3,0,2:T(8,128)(2,1)S(1)}, u32[]{:S(2)}, u32[]{:S(2)}) async-start(bf16[1,128,16,64]{1,3,0,2:T(8,128)(2,1)} %bitcast.35), calls=%async_computation.2 | async-start | bytes 524288 | tf_op jit(solution)/shard_map/all_to_all | solution.py:178
  24.7 8.5 copy-start.8
  27.9 21.8 %all-to-all-start = ((bf16[1,128,16,192]{1,3,0,2:T(8,128)(2,1)}), bf16[1,128,16,192]{1,3,0,2:T(8,128)(2,1)}, u32[]{:S(2)}, u32[]{:S(2)}) async-start(bf16[1,128,16,192]{1,3,0,2:T(8,128)(2,1)} %bitcast.231), calls=%async_computation | async-start | bytes 1572864 | tf_op jit(solution)/shard_map/all_to_all | solution.py:164
  67.3 1.0 copy-start.3
  77.7 1.0 copy-start.3
  88.1 1.0 copy-start.3
  98.5 1.0 copy-start.3
  132.4 235.4 %all-to-all-start.1 = ((bf16[16,2,4096]{2,1,0:T(2,128)(2,1)}), bf16[16,2,4096]{2,1,0:T(2,128)(2,1)}, u32[]{:S(2)}, u32[]{:S(2)}) async-start(bf16[16,2,4096]{2,1,0:T(2,128)(2,1)} %reshape.360), calls=%async_computation.1 | async-start | bytes 524288 | tf_op jit(solution)/shard_map/all_to_all | solution.py:171
  149.5 2.8 copy-start.2
  198.2 2.8 copy-start.2
  246.8 2.8 copy-start.2
  295.4 2.8 copy-start.2
  337.5 1.5 copy-start.1
  337.5 1.7 copy-start.7
  367.8 19.9 %all-to-all-start.3 = ((bf16[16,2,12288]{2,1,0:T(2,128)(2,1)}), bf16[16,2,12288]{2,1,0:T(2,128)(2,1)}, u32[]{:S(2)}, u32[]{:S(2)}) async-start(bf16[16,2,12288]{2,1,0:T(2,128)(2,1)} %reshape.362), calls=%async_computation.3 | async-start | bytes 1572864 | tf_op jit(solution)/shard_map/all_to_all | solution.py:186
  375.0 709.4 %reduce-scatter.2.cloned.1.call-start = ((), (), s32[]{:S(2)}) async-start(), calls=%async_computation.5 | async-start | bytes 16908288 | tf_op jit(solution)/shard_map/reduce_scatter | solution.py:202
  398.5 2.2 copy-start.4
  407.9 5.1 copy-start.6
Sparse Core Ops, SparseCore 0:
  406.9 677.4 reduce-scatter.1
where the time goes:
time: 1100 us; the launch traced here: 1090 us
  waiting for transfers between devices  676 us (61%)
  matrix products  131 us (12%)
  other arithmetic  125 us (11%)
  local copies, waits for them, and re-layouts  120 us (11%)
  starting transfers between devices  28 us (3%)
  between operations  14.3 us (1%)
    reduce_scatter x1, waiting for transfers between devices, shards(): lax.psum_scatter(jnp.concatenate([part_qkv, part_out], axis=1), ('dp', 's...  670 us
    scatter-add x4, other arithmetic, per_group(): key_acc = key_acc.at[flat].add(key_part.reshape(-1, BLK, width))  41.4 us
    scatter-add x4, other arithmetic, per_group(): value_acc = value_acc.at[flat].add(value_part.reshape(-1, BLK, width))  41.3 us
    reshape x4, matrix products, per_group(): key_acc = key_acc.at[flat].add(key_part.reshape(-1, BLK, width))  28.4 us
    gather x16, local copies, waits for them, and re-layouts, fetch_blocks(): gathered = source[chosen]  26.9 us
    unnamed x3, other arithmetic  26.7 us
    dot_general x4, matrix products, per_group(): jnp.einsum('gqk,gke->gqe', grad_scores, keyed, preferred_element_type=jnp...  23.7 us
  transfers between devices with their start and end apart: 5, of which 3 were waited for; matrix products, arithmetic and copies ran while one was open for 24% of the time, Pallas kernels for 0%

commit v1 on v0

v1 whole, which is shorter than its diff:
```python
import functools
import math

import jax
import jax.numpy as jnp
from jax import lax
from jax.experimental import pallas as pl
from jax.experimental.pallas import tpu as pltpu
from jax.sharding import PartitionSpec as P

H = 16
HD = 64
D = 1024
BLK = 64
MAXB = 8
NODES = 2048
NBLK = 32
WIDE = 4 * HD
TILE = 256
EPS = 1e-05
SCALE = 1.0 / math.sqrt(HD)


def contract(a, b, da, db):
    return lax.dot_general(a, b, (((da,), (db,)), ((), ())), preferred_element_type=jnp.float32)


def attention_kernel(list_ref, count_ref, order_ref, rows_ref, out_ref, qg_ref, kv_ref, acc_ref, res_ref):
    low_lanes = lax.broadcasted_iota(jnp.int32, (TILE, 2 * HD), 1) < HD

    def to_cluster(t, carry):
        start = pl.multiple_of(t * TILE, TILE)
        ordered = jnp.broadcast_to(order_ref[:, pl.ds(start, TILE)], (128, TILE))
        position = jnp.transpose(ordered.astype(jnp.float32)).astype(jnp.int32)
        lanes = lax.broadcasted_iota(jnp.int32, (TILE, 128), 1)
        pick = jnp.concatenate(
            [(position == lanes + 128 * c).astype(jnp.float32).astype(jnp.bfloat16) for c in range(NODES // 128)],
            axis=1,
        )
        moved = contract(pick, rows_ref[...], 1, 0)
        first, second = moved[:, : 2 * HD], moved[:, 2 * HD :]
        qg_ref[pl.ds(start, TILE), :] = jnp.where(low_lanes, first, second).astype(jnp.bfloat16)
        kv_ref[pl.ds(start, TILE), :] = jnp.where(
            low_lanes, pltpu.roll(first, HD, 1), pltpu.roll(second, HD, 1)
        ).astype(jnp.bfloat16)
        return carry

    lax.fori_loop(0, NODES // TILE, to_cluster, 0)
    acc_ref[...] = jnp.zeros_like(acc_ref)
    block_low = lax.broadcasted_iota(jnp.int32, (BLK, 2 * HD), 1) < HD
    key_slot = lax.broadcasted_iota(jnp.int32, (BLK, MAXB * BLK), 1) // BLK

    def per_block(b, carry):
        start = pl.multiple_of(b * BLK, BLK)
        qg = qg_ref[pl.ds(start, BLK), :].astype(jnp.float32)
        keys_at = [pl.multiple_of(list_ref[b, j] * BLK, BLK) for j in range(MAXB)]
        kv = jnp.concatenate([kv_ref[pl.ds(at, BLK), :] for at in keys_at], axis=0)
        zero = jnp.zeros_like(qg)
        split = jnp.concatenate(
            [jnp.where(block_low, qg, zero), jnp.where(block_low, zero, qg)], axis=0
        ).astype(jnp.bfloat16)
        both = contract(split, kv, 1, 1)
        scores = jnp.where(key_slot < count_ref[b], both[:BLK] * SCALE, jnp.float32(-1e30))
        expo = jnp.exp(scores - jnp.max(scores, axis=1, keepdims=True))
        probs = expo * (1.0 / jnp.sum(expo, axis=1, keepdims=True))
        grad_probs = both[BLK:]
        delta = jnp.sum(grad_probs * probs, axis=1, keepdims=True)
        grad_scores = probs * (grad_probs - delta) * SCALE
        stacked = jnp.concatenate([grad_scores, probs], axis=0).astype(jnp.bfloat16)
        crossed = contract(stacked, kv, 1, 0)
        res_ref[pl.ds(start, BLK), :] = jnp.where(block_low, crossed[:BLK], crossed[BLK:])
        parts = contract(stacked, split, 0, 0)
        for j in range(MAXB):
            acc_ref[pl.ds(keys_at[j], BLK), :] += parts[j * BLK : (j + 1) * BLK]
        return carry

    lax.fori_loop(0, NBLK, per_block, 0)

    def assemble(t, carry):
        start = pl.multiple_of(t * TILE, TILE)
        dqo = res_ref[pl.ds(start, TILE), :]
        turned = pltpu.roll(acc_ref[pl.ds(start, TILE), :], HD, 1)
        qg_ref[pl.ds(start, TILE), :] = jnp.where(low_lanes, dqo, turned).astype(jnp.bfloat16)
        kv_ref[pl.ds(start, TILE), :] = jnp.where(low_lanes, turned, dqo).astype(jnp.bfloat16)
        return carry

    lax.fori_loop(0, NODES // TILE, assemble, 0)

    def to_nodes(t, carry):
        start = pl.multiple_of(t * TILE, TILE)
        node = lax.broadcasted_iota(jnp.int32, (TILE, NODES), 0) + start
        pick = (node == order_ref[...]).astype(jnp.float32).astype(jnp.bfloat16)
        out_ref[pl.ds(start, TILE), : 2 * HD] = contract(pick, qg_ref[...], 1, 0).astype(jnp.bfloat16)
        out_ref[pl.ds(start, TILE), 2 * HD :] = contract(pick, kv_ref[...], 1, 0).astype(jnp.bfloat16)
        return carry

    lax.fori_loop(0, NODES // TILE, to_nodes, 0)


def attention(picked, counted, order, rows):
    return pl.pallas_call(
        attention_kernel,
        out_shape=jax.ShapeDtypeStruct((NODES, WIDE), jnp.bfloat16),
        in_specs=[
            pl.BlockSpec(memory_space=pltpu.SMEM),
            pl.BlockSpec(memory_space=pltpu.SMEM),
            pl.BlockSpec(memory_space=pltpu.VMEM),
            pl.BlockSpec(memory_space=pltpu.VMEM),
        ],
        out_specs=pl.BlockSpec(memory_space=pltpu.VMEM),
        scratch_shapes=[
            pltpu.VMEM((NODES, 2 * HD), jnp.bfloat16),
            pltpu.VMEM((NODES, 2 * HD), jnp.bfloat16),
            pltpu.VMEM((NODES, 2 * HD), jnp.float32),
            pltpu.VMEM((NODES, 2 * HD), jnp.float32),
        ],
        compiler_params=pltpu.CompilerParams(vmem_limit_bytes=40 * 1024 * 1024),
        cost_estimate=pl.CostEstimate(flops=10_000_000_000, bytes_accessed=4_000_000, transcendentals=1_000_000),
        name="clustered_attention",
    )(picked, counted, order, rows)


def shards(nodes, w_qkv, w_out, cotangent, order, block_list, block_count):
    features = nodes[0]
    upstream = cotangent[0]
    rows = features.shape[0]
    wide_in = features.astype(jnp.float32)
    inv_rms = lax.rsqrt(jnp.mean(wide_in * wide_in, axis=-1, keepdims=True) + EPS)
    normed = (wide_in * inv_rms).astype(jnp.bfloat16)
    all_normed = lax.all_gather(normed, "seq", axis=0, tiled=True)
    all_upstream = lax.all_gather(upstream, "seq", axis=0, tiled=True)
    packed = contract(normed, w_qkv, 1, 0).astype(jnp.bfloat16).reshape(rows, H, 3 * HD)
    projected = contract(upstream, w_out, 1, 1).astype(jnp.bfloat16).reshape(rows, H, HD)
    sent = jnp.concatenate([packed, projected], axis=2).transpose(1, 0, 2)
    head_rows = lax.all_to_all(sent, "seq", 0, 0, tiled=True).reshape(NODES, WIDE)
    head_out = attention(block_list[0], block_count[0], order, head_rows)

    part_qkv = contract(all_normed, head_out[:, : 3 * HD], 0, 0)
    part_out = contract(head_out[:, 3 * HD :], all_upstream, 0, 0)
    parts = jnp.concatenate(
        [part_qkv.reshape(8, 128 * 3 * HD), part_out.reshape(8, 8 * D)], axis=1
    ).astype(jnp.bfloat16).reshape(8, 128, WIDE)
    batches = lax.all_to_all(parts, "dp", 0, 0, tiled=True)
    total = jnp.sum(batches.astype(jnp.float32), axis=0).reshape(128 * WIDE)
    head_qkv = total[: 128 * 3 * HD].reshape(H, 8, 3 * HD)
    head_rows_out = total[128 * 3 * HD :].reshape(8, D)
    grad_qkv = lax.all_to_all(head_qkv, "seq", 0, 0, tiled=True).transpose(1, 0, 2).reshape(8, 3 * D)
    moves = [(i * H + h, h * 8 + i) for i in range(8) for h in range(H)]
    grad_out = lax.ppermute(head_rows_out, ("dp", "seq"), moves)

    back = lax.all_to_all(head_out.reshape(H, rows, WIDE), "seq", 0, 0, tiled=True).transpose(1, 0, 2)
    grad_packed = back[:, :, : 3 * HD].reshape(rows, 3 * D)
    attn = back[:, :, 3 * HD :].reshape(rows, D)
    mixed = (wide_in + contract(attn, w_out, 1, 0)).astype(jnp.bfloat16)
    grad_normed = contract(grad_packed, w_qkv, 1, 1)
    inner = jnp.mean(grad_normed * wide_in, axis=-1, keepdims=True)
    grad_nodes = (
        upstream.astype(jnp.float32)
        + inv_rms * grad_normed
        - wide_in * inv_rms * inv_rms * inv_rms * inner
    ).astype(jnp.bfloat16)
    return mixed[None], grad_nodes[None], grad_qkv, grad_out


def solution(mesh):
    return jax.shard_map(
        shards,
        mesh=mesh,
        in_specs=(
            P("dp", "seq", None),
            P(),
            P(),
            P("dp", "seq", None),
            P("dp", None),
            P("dp", None, None),
            P("dp", None),
        ),
        out_specs=(
            P("dp", "seq", None),
            P("dp", "seq", None),
            P(("dp", "seq"), None),
            P(("dp", "seq"), None),
        ),
        check_vma=False,
    )
```

time: 1100 us -> 184 us (0.17)
  the two profiles are of different devices: /device:TPU:0 before, /device:TPU:7 now
where the time goes in v1:
time: 184 us; the launch traced here: 183 us
  waiting for transfers between devices  47.2 us (26%)
  Pallas kernels  34.3 us (19%)
  starting transfers between devices  22.9 us (12%)
  blocking collectives  22.4 us (12%)
  matrix products  20.2 us (11%)
  between operations  14.2 us (8%)
  local copies, waits for them, and re-layouts  13.7 us (7%)
  other arithmetic  8.14 us (4%)
    pallas_call x1, Pallas kernels, attention(): pl.pallas_call(attention_kernel, out_shape=jax.ShapeDtypeStruct((NODES, W...  34.3 us
    all_to_all x1, blocking collectives, shards(): lax.all_to_all(head_out.reshape(H, rows, WIDE), 'seq', 0, 0, tiled=True)  22.4 us
    dot_general x6, matrix products, contract(): lax.dot_general(a, b, (((da,), (db,)), ((), ())), preferred_element_type=...  20.2 us
    all_gather x1, waiting for transfers between devices, shards(): all_normed = lax.all_gather(normed, 'seq', axis=0, tiled=True)  16.6 us
    all_to_all x1, waiting for transfers between devices, shards(): lax.all_to_all(sent, 'seq', 0, 0, tiled=True).reshape(NODES, WIDE)  16.1 us
    all_to_all x1, waiting for transfers between devices, shards(): batches = lax.all_to_all(parts, 'dp', 0, 0, tiled=True)  8.63 us
    all_to_all x1, starting transfers between devices, shards(): lax.all_to_all(sent, 'seq', 0, 0, tiled=True).reshape(NODES, WIDE)  7.71 us
    ppermute x1, waiting for transfers between devices, shards(): grad_out = lax.ppermute(head_rows_out, ('dp', 'seq'), moves)  5.16 us
  transfers between devices with their start and end apart: 6, of which 4 were waited for; matrix products, arithmetic and copies ran while one was open for 15% of the time, Pallas kernels for 19%

profile of v1, /device:TPU:7, one launch (start us, length us, event | category | flops | bytes accessed | tf_op | source)
XLA Modules:
  0.0 183.1 jit_solution(6813781331837060432)
XLA Ops:
  7.2 0.0 copy-start
  7.2 0.0 all-gather.6.cloned.1.call-start
  7.2 0.7 all-gather.6.cloned.1.call-update
  7.9 0.0 all-gather.4.cloned.1.call-start
  8.0 1.1 fusion.14
  9.1 1.8 fusion.9
  10.8 0.0 all-gather.4.cloned.1.call-update
  10.8 0.0 copy-done
  10.9 1.8 convolution_convert_fusion.2
  12.6 0.2 copy.31
  12.8 3.9 %convolution_convert_fusion = bf16[128,3072]{1,0:T(8,128)(2,1)S(1)} fusion(bf16[128,1024]{1,0:T(8,128)(2,1)} %fusion.9, bf16[1024,3072]{1,0:T(8,128)(2,1)} %param.8), kind=kOutput, calls=%fused_computation.2 | convolution fusion | flops 805699584 | bytes 7340032 | tf_op jit(solution)/shard_map/dot_general | solution.py:25
  16.7 0.0 copy-start.8
  16.7 0.0 copy-start.2
  16.7 0.0 copy-start.3
  16.7 1.2 copy.30
  17.9 2.3 %maximum_bitcast_fusion = bf16[16,128,256]{1,2,0:T(8,128)(2,1)} fusion(bf16[128,16,64]{0,2,1:T(8,128)(2,1)S(1)} %bitcast.51, bf16[128,16,192]{0,2,1:T(8,128)(2,1)} %bitcast.47), kind=kLoop, calls=%fused_computation.10 | loop fusion | flops 2097152 | bytes 2097152 | tf_op jit(solution)/shard_map/transpose | solution.py:134
  20.2 7.7 %all-to-all-start = ((bf16[16,128,256]{1,2,0:T(8,128)(2,1)}), bf16[16,128,256]{1,2,0:T(8,128)(2,1)S(1)}, u32[]{:S(2)}, u32[]{:S(2)}) async-start(bf16[16,128,256]{1,2,0:T(8,128)(2,1)} %maximum_bitcast_fusion), calls=%async_computation | async-start | bytes 2097152 | tf_op jit(solution)/shard_map/all_to_all | solution.py:135
  27.9 0.0 copy-done.8
  27.9 0.1 copy.29
  28.0 16.1 %all-to-all-done = bf16[16,128,256]{1,2,0:T(8,128)(2,1)S(1)} async-done(((bf16[16,128,256]{1,2,0:T(8,128)(2,1)}), bf16[16,128,256]{1,2,0:T(8,128)(2,1)S(1)}, u32[]{:S(2)}, u32[]{:S(2)}) %all-to-all-start) | async-done | bytes 1048608 | tf_op jit(solution)/shard_map/all_to_all | solution.py:135
  44.1 1.4 copy.32
  45.5 0.0 copy-done.2
  45.5 0.0 copy-done.3
  45.5 0.0 copy-start.1
  45.5 1.2 copy-done.1
  46.7 34.3 %clustered_attention.1 = bf16[2048,256]{1,0:T(8,128)(2,1)S(1)} custom-call(s32[32,8]{1,0:T(8,128)S(1)} %bitcast.43, s32[32]{0:T(128)S(1)} %bitcast.44, s32[1,2048]{1,0:T(1,128)S(1)} %copy-done.2, bf16[2048,256]{1,0:T(8,128)(2,1)S(1)} %bitcast.42), custom_call_target="tpu_custom_call" | custom-call | flops 10000000000 | bytes 4000000 | tf_op jit(solution)/shard_map/clustered_attention/pallas_call | solution.py:101
  81.0 0.0 copy-start.4
  81.0 1.4 copy.33
  82.4 22.4 %all_to_all.20 = bf16[16,128,256]{1,2,0:T(8,128)(2,1)S(1)} all-to-all(bf16[16,128,256]{1,2,0:T(8,128)(2,1)} %copy.33), channel_id=1, replica_groups=mesh['dp'=8,'seq'=16] {'seq'}, dimensions={0} | all-to-all | bytes 2097152 | tf_op jit(solution)/shard_map/all_to_all | solution.py:151
  104.8 0.7 slice.26
  105.5 0.1 slice.27
  105.6 0.0 copy-done.4
  105.6 5.8 %fusion.15 = (f32[128]{0:T(128)S(1)}, f32[128,1024]{1,0:T(8,128)}) fusion(bf16[1,128,1024]{2,1,0:T(8,128)(2,1)S(1)} %copy-done.4, bf16[128,3072]{0,1:T(8,128)(2,1)S(1)} %bitcast.48, bf16[1024,3072]{1,0:T(8,128)(2,1)} %param.8), kind=kOutput, calls=%fused_computation.22 | convolution fusion | flops 805699456 | bytes 7864832 | tf_op jit(solution)/shard_map/dot_general | solution.py:25
  111.4 0.0 all-gather.6.cloned.1.call-done
  111.4 3.6 %fusion.4 = bf16[64,1024]{1,0:T(8,128)(2,1)S(1)} fusion(bf16[1,2048,1024]{2,1,0:T(8,128)(2,1)} %all-gather.6.cloned.1.call-done, bf16[2048,256]{1,0:T(8,128)(2,1)S(1)} %clustered_attention.1), kind=kOutput, calls=%fused_computation.8 | convolution fusion | flops 268500992 | bytes 4849664 | tf_op jit(solution)/shard_map/dot_general | solution.py:25
  115.0 0.7 reshape.72
  115.7 16.6 %all-gather.4.cloned.1.call-done = bf16[2048,1024]{1,0:T(8,128)(2,1)} async-done(((bf16[128,1024]{1,0:T(8,128)(2,1)}), bf16[2048,1024]{1,0:T(8,128)(2,1)}) %all-gather.4.cloned.1.call-update) | async-done | bytes 4194320 | tf_op jit(solution)/shard_map/all_gather | solution.py:130
  132.3 4.0 %convolution_convert_fusion.1 = bf16[1024,192]{0,1:T(8,128)(2,1)} fusion(bf16[2048,1024]{1,0:T(8,128)(2,1)} %all-gather.4.cloned.1.call-done, bf16[2048,256]{1,0:T(8,128)(2,1)S(1)} %clustered_attention.1), kind=kOutput, calls=%fused_computation.3 | convolution fusion | flops 805502976 | bytes 5636096 | tf_op jit(solution)/shard_map/dot_general | solution.py:25
  136.3 0.0 copy-start.5
  136.3 0.0 copy-start.6
  136.3 2.1 %copy.34 = bf16[1024,192]{1,0:T(8,128)(2,1)} copy(bf16[1024,192]{0,1:T(8,128)(2,1)} %convolution_convert_fusion.1) | data formatting | bytes 786432 | tf_op jit(solution)/shard_map/convert.4
  138.4 1.7 reshape.71
  140.0 0.9 pad_maximum_fusion
  141.0 0.0 copy-start.7
  141.0 0.9 copy.35
  141.9 5.0 %all-to-all-start.2 = ((bf16[8,128,256]{2,1,0:T(8,128)(2,1)}), bf16[8,128,256]{2,1,0:T(8,128)(2,1)}, u32[]{:S(2)}, u32[]{:S(2)}) async-start(bf16[8,128,256]{2,1,0:T(8,128)(2,1)} %copy.35), calls=%async_computation.2 | async-start | bytes 1048576 | tf_op jit(solution)/shard_map/all_to_all | solution.py:143
  146.9 0.0 copy-done.5
  146.9 0.0 copy-done.6
  146.9 0.9 fusion.17
  147.8 8.6 %all-to-all-done.2 = bf16[8,128,256]{2,1,0:T(8,128)(2,1)} async-done(((bf16[8,128,256]{2,1,0:T(8,128)(2,1)}), bf16[8,128,256]{2,1,0:T(8,128)(2,1)}, u32[]{:S(2)}, u32[]{:S(2)}) %all-to-all-start.2) | async-done | bytes 524320 | tf_op jit(solution)/shard_map/all_to_all | solution.py:143
  156.4 1.1 convert_reduce_fusion
  157.6 0.7 reshape.73
  158.3 5.2 %all-to-all-start.3 = ((f32[16,8,192]{2,1,0:T(8,128)}), f32[16,8,192]{2,1,0:T(8,128)S(1)}, u32[]{:S(2)}, u32[]{:S(2)}) async-start(f32[16,8,192]{2,1,0:T(8,128)} %reshape.73), calls=%async_computation.3 | async-start | bytes 262144 | tf_op jit(solution)/shard_map/all_to_all | solution.py:147
  163.5 5.0 %collective-permute-start = (f32[8,1024]{1,0:T(8,128)S(1)}, f32[8,1024]{1,0:T(8,128)S(1)}, u32[]{:S(2)}, u32[]{:S(2)}) collective-permute-start(f32[8,1024]{1,0:T(8,128)S(1)} %reshape.75), channel_id=1, source_target_pairs={{0,0},{1,8},{2,16},{3,24},{4,32},{5,40},{6,48},{7,56},{8,64},{9,72... | collective-permute-start | bytes 98312 | tf_op jit(solution)/shard_map/ppermute | solution.py:149
  168.5 0.0 copy-done.7
  168.5 1.2 fusion.3
  169.7 5.2 %collective-permute-done = f32[8,1024]{1,0:T(8,128)S(1)} collective-permute-done((f32[8,1024]{1,0:T(8,128)S(1)}, f32[8,1024]{1,0:T(8,128)S(1)}, u32[]{:S(2)}, u32[]{:S(2)}) %collective-permute-start) | collective-permute-done | bytes 32800 | tf_op jit(solution)/shard_map/ppermute | solution.py:149
  174.9 0.0 all-to-all-done.3
  174.9 0.7 reshape.74
  175.7 0.6 copy.38
  (6 shorter events, 0.1 us)
Async XLA Ops:
  7.2 3.7 %copy-start = (bf16[1024,1024]{1,0:T(8,128)(2,1)S(1)}, bf16[1024,1024]{1,0:T(8,128)(2,1)}, u32[]{:S(2)}) copy-start(bf16[1024,1024]{1,0:T(8,128)(2,1)} %param.9) | copy-start | bytes 6291460
  7.2 104.3 %all-gather.6.cloned.1.call-start = ((), (), s32[]{:S(2)}) async-start(), calls=%async_computation.5 | async-start | bytes 4456448 | tf_op jit(solution)/shard_map/all_gather | solution.py:131
  7.9 124.4 %all-gather.4.cloned.1.call-start = ((), (), s32[]{:S(2)}) async-start(), calls=%async_computation.4 | async-start | bytes 4456448 | tf_op jit(solution)/shard_map/all_gather | solution.py:130
  16.7 11.2 %copy-start.8 = (s32[1,32,8]{1,2,0:T(8,128)S(1)}, s32[1,32,8]{1,2,0:T(8,128)}, u32[]{:S(2)}) copy-start(s32[1,32,8]{1,2,0:T(8,128)} %param.12) | copy-start | bytes 3076
  16.7 28.7 %copy-start.2 = (s32[1,2048]{1,0:T(1,128)S(1)}, s32[1,2048]{1,0:T(1,128)}, u32[]{:S(2)}) copy-start(s32[1,2048]{1,0:T(1,128)} %order_ref.1) | copy-start | bytes 24580
  16.7 28.7 %copy-start.3 = (s32[1,32]{1,0:T(1,128)S(1)}, s32[1,32]{1,0:T(1,128)}, u32[]{:S(2)}) copy-start(s32[1,32]{1,0:T(1,128)} %param.13) | copy-start | bytes 388
  20.2 23.9 %all-to-all-start = ((bf16[16,128,256]{1,2,0:T(8,128)(2,1)}), bf16[16,128,256]{1,2,0:T(8,128)(2,1)S(1)}, u32[]{:S(2)}, u32[]{:S(2)}) async-start(bf16[16,128,256]{1,2,0:T(8,128)(2,1)} %maximum_bitcast_fusion), calls=%async_computation | async-start | bytes 2097152 | tf_op jit(solution)/shard_map/all_to_all | solution.py:135
  45.5 1.2 copy-start.1
  81.0 24.6 %copy-start.4 = (bf16[1,128,1024]{2,1,0:T(8,128)(2,1)S(1)}, bf16[1,128,1024]{2,1,0:T(8,128)(2,1)}, u32[]{:S(2)}) copy-start(bf16[1,128,1024]{2,1,0:T(8,128)(2,1)} %param.7) | copy-start | bytes 786436
  136.3 10.6 %copy-start.5 = (bf16[1,128,1024]{2,1,0:T(8,128)(2,1)S(1)}, bf16[1,128,1024]{2,1,0:T(8,128)(2,1)}, u32[]{:S(2)}) copy-start(bf16[1,128,1024]{2,1,0:T(8,128)(2,1)} %param.10) | copy-start | bytes 786436
  136.3 10.6 %copy-start.6 = (f32[128,1024]{1,0:T(8,128)S(1)}, f32[128,1024]{1,0:T(8,128)}, u32[]{:S(2)}) copy-start(f32[128,1024]{1,0:T(8,128)} %get-tuple-element.5) | copy-start | bytes 1572868
  141.0 27.5 %copy-start.7 = (bf16[128,16,64]{0,2,1:T(8,128)(2,1)S(1)}, bf16[128,16,64]{0,2,1:T(8,128)(2,1)}, u32[]{:S(2)}) copy-start(bf16[128,16,64]{0,2,1:T(8,128)(2,1)} %slice.26) | copy-start | bytes 786436
  141.9 14.5 %all-to-all-start.2 = ((bf16[8,128,256]{2,1,0:T(8,128)(2,1)}), bf16[8,128,256]{2,1,0:T(8,128)(2,1)}, u32[]{:S(2)}, u32[]{:S(2)}) async-start(bf16[8,128,256]{2,1,0:T(8,128)(2,1)} %copy.35), calls=%async_computation.2 | async-start | bytes 1048576 | tf_op jit(solution)/shard_map/all_to_all | solution.py:143
  158.3 16.5 %all-to-all-start.3 = ((f32[16,8,192]{2,1,0:T(8,128)}), f32[16,8,192]{2,1,0:T(8,128)S(1)}, u32[]{:S(2)}, u32[]{:S(2)}) async-start(f32[16,8,192]{2,1,0:T(8,128)} %reshape.73), calls=%async_computation.3 | async-start | bytes 262144 | tf_op jit(solution)/shard_map/all_to_all | solution.py:147
  163.5 11.4 %collective-permute-start = (f32[8,1024]{1,0:T(8,128)S(1)}, f32[8,1024]{1,0:T(8,128)S(1)}, u32[]{:S(2)}, u32[]{:S(2)}) collective-permute-start(f32[8,1024]{1,0:T(8,128)S(1)} %reshape.75), channel_id=1, source_target_pairs={{0,0},{1,8},{2,16},{3,24},{4,32},{5,40},{6,48},{7,56},{8,64},{9,72... | collective-permute-start | bytes 98312 | tf_op jit(solution)/shard_map/ppermute | solution.py:149
Sparse Core Ops, SparseCore 0:
  10.2 61.1 all-gather.5
  74.0 58.2 all-gather.3

commit v2 on v1

v2 whole, which is shorter than its diff:
```python
import math

import jax
import jax.numpy as jnp
from jax import lax
from jax.experimental import pallas as pl
from jax.experimental.pallas import tpu as pltpu
from jax.sharding import PartitionSpec as P

H = 16
HD = 64
D = 1024
BLK = 64
MAXB = 8
NODES = 2048
NBLK = 32
WIDE = 4 * HD
TILE = 2048
PAIRS = 2
STEPS = (8, 4)
DP = 8
SEQ = 16
ROWS = 128
CHUNK = 512
HALF = ROWS // 2
VMEM_BYTES = 60 * 1024 * 1024
EPS = 1e-05
SCALE = 1.0 / math.sqrt(HD)


def contract(a, b, da, db):
    return lax.dot_general(a, b, (((da,), (db,)), ((), ())), preferred_element_type=jnp.float32)


def attention_kernel(
    list_ref, count_ref, ranked_ref, bounds_ref, order_ref, rows_ref, after_ref, out_ref, attn_ref, grads_ref, qg_ref, kv_ref, acc_ref, done_ref, both_ref
):
    low_lanes = lax.broadcasted_iota(jnp.int32, (TILE, 2 * HD), 1) < HD
    one, none = jnp.ones((TILE, 128), jnp.bfloat16), jnp.zeros((TILE, 128), jnp.bfloat16)

    def to_cluster(t, carry):
        start = pl.multiple_of(t * TILE, TILE)
        ordered = jnp.broadcast_to(order_ref[:, pl.ds(start, TILE)], (128, TILE))
        position = jnp.transpose(ordered.astype(jnp.float32)).astype(jnp.int32)
        lanes = lax.broadcasted_iota(jnp.int32, (TILE, 128), 1)
        within = (position % 128 == lanes).astype(jnp.float32).astype(jnp.bfloat16)
        tile_of = (position // 128).astype(jnp.float32).astype(jnp.bfloat16)
        pick = jnp.concatenate(
            [jnp.where(tile_of == jnp.bfloat16(c), within, none) for c in range(NODES // 128)], axis=1
        )
        moved = contract(pick, rows_ref[...], 1, 0)
        first, second = moved[:, : 2 * HD], moved[:, 2 * HD :]
        qg_ref[pl.ds(start, TILE), :] = jnp.where(low_lanes, first * SCALE, second).astype(jnp.bfloat16)
        kv_ref[pl.ds(start, TILE), :] = jnp.where(
            low_lanes, pltpu.roll(first, HD, 1), pltpu.roll(second, HD, 1)
        ).astype(jnp.bfloat16)
        return carry

    lax.fori_loop(0, NODES // TILE, to_cluster, 0)
    acc_ref[...] = jnp.zeros_like(acc_ref)
    block_low = lax.broadcasted_iota(jnp.int32, (BLK, 2 * HD), 1) < HD
    pair_low = lax.broadcasted_iota(jnp.int32, (1, 2 * BLK), 1) < BLK

    def folded(parts, op):
        total = parts[0]
        for part in parts[1:]:
            total = op(total, part)
        return total

    def pair(at, slot, used):
        blocks = (ranked_ref[at], ranked_ref[at + 1])
        starts = [pl.multiple_of(b * BLK, BLK) for b in blocks]
        qg = [qg_ref[pl.ds(s, BLK), :].astype(jnp.float32) for s in starts]
        keys_at = [[pl.multiple_of(list_ref[b, j] * BLK, BLK) for j in range(used)] for b in blocks]
        kv = jnp.concatenate(
            [jnp.concatenate([kv_ref[pl.ds(key, BLK), :] for key in keys], axis=0) for keys in keys_at], axis=1
        )
        zero = jnp.zeros_like(qg[0])
        q0, q1 = (jnp.where(block_low, x, zero) for x in qg)
        g0, g1 = (jnp.where(block_low, zero, x) for x in qg)
        split = jnp.concatenate(
            [
                jnp.concatenate([q0, zero, g0, zero], axis=0),
                jnp.concatenate([zero, q1, zero, g1], axis=0),
            ],
            axis=1,
        ).astype(jnp.bfloat16)
        both_ref[slot, : used * BLK, :] = contract(kv, split, 1, 1)
        counts = jnp.where(pair_low, count_ref[blocks[0]], count_ref[blocks[1]])
        scores = [
            jnp.where(j < counts, both_ref[slot, j * BLK : (j + 1) * BLK, : 2 * BLK], jnp.float32(-1e30))
            for j in range(used)
        ]
        highest = jnp.max(folded(scores, jnp.maximum), axis=0, keepdims=True)
        expo = [jnp.exp(s - highest) for s in scores]
        inverse = 1.0 / jnp.sum(folded(expo, jnp.add), axis=0, keepdims=True)
        grads = [both_ref[slot, j * BLK : (j + 1) * BLK, 2 * BLK :] for j in range(used)]
        probs = [e * inverse for e in expo]
        delta = jnp.sum(folded([g * p for g, p in zip(grads, probs)], jnp.add), axis=0, keepdims=True)
        mixed = jnp.concatenate(
            [
                jnp.concatenate([(p * (g - delta)).astype(jnp.bfloat16), p.astype(jnp.bfloat16)], axis=1)
                for g, p in zip(grads, probs)
            ],
            axis=0,
        )
        crossed = contract(mixed, kv, 0, 0)
        for s, dq, o in (
            (starts[0], crossed[:64, :128], crossed[128:192, :128]),
            (starts[1], crossed[64:128, 128:], crossed[192:, 128:]),
        ):
            done_ref[pl.ds(s, BLK), : 2 * HD] = (dq * SCALE).astype(jnp.bfloat16)
            done_ref[pl.ds(s, BLK), 2 * HD :] = o.astype(jnp.bfloat16)
        return keys_at, contract(mixed, split, 1, 0)

    def grouped(used):
        def per_group(i, carry):
            found = [pair((i * PAIRS + u) * 2, u, used) for u in range(PAIRS)]
            for keys_at, parts in found:
                for c in range(2):
                    for j in range(used):
                        acc_ref[pl.ds(keys_at[c][j], BLK), :] += parts[
                            j * BLK : (j + 1) * BLK, c * 128 : (c + 1) * 128
                        ]
            return carry

        return per_group

    for step, used in enumerate(STEPS):
        lax.fori_loop(bounds_ref[step], bounds_ref[step + 1], grouped(used), 0)

    def assemble(t, carry):
        start = pl.multiple_of(t * TILE, TILE)
        turned = pltpu.roll(acc_ref[pl.ds(start, TILE), :], HD, 1).astype(jnp.bfloat16)
        rows = pl.ds(start, TILE)
        done_ref[rows, : 2 * HD] = jnp.where(low_lanes, done_ref[rows, : 2 * HD], turned)
        done_ref[rows, 2 * HD :] = jnp.where(low_lanes, turned, done_ref[rows, 2 * HD :])
        return carry

    lax.fori_loop(0, NODES // TILE, assemble, 0)
    row = lax.broadcasted_iota(jnp.int32, (128, NODES), 0).astype(jnp.float32).astype(jnp.bfloat16)
    full, empty = jnp.ones_like(row), jnp.zeros_like(row)

    def to_nodes(t, carry):
        start = pl.multiple_of(t * TILE, TILE)
        offsets = [
            jnp.clip(order_ref[...] - start - 128 * c, -1, 128).astype(jnp.float32).astype(jnp.bfloat16)
            for c in range(TILE // 128)
        ]
        pick = jnp.concatenate([jnp.where(row == offset, full, empty) for offset in offsets], axis=0)
        moved = contract(pick, done_ref[...], 1, 0)
        out_ref[pl.ds(start, TILE), :] = moved.astype(jnp.bfloat16)
        for c in range(TILE // ROWS):
            place = t * (TILE // ROWS) + c
            top, bottom = moved[c * ROWS : c * ROWS + HALF], moved[c * ROWS + HALF : (c + 1) * ROWS]
            late_top, late_bottom = top[:, 2 * HD :], bottom[:, 2 * HD :]
            attn_ref[place] = jnp.where(block_low, pltpu.roll(late_top, HD, 1), late_bottom).astype(jnp.bfloat16)
            grads_ref[place] = jnp.concatenate(
                [top[:, : 2 * HD], jnp.where(block_low, late_top, pltpu.roll(late_bottom, HD, 1)), bottom[:, : 2 * HD]],
                axis=1,
            ).astype(jnp.bfloat16)
        return carry

    lax.fori_loop(0, NODES // TILE, to_nodes, 0)


def ranking(counted):
    index = jnp.arange(NBLK)
    ahead = (counted[None, :] > counted[:, None]) | (
        (counted[None, :] == counted[:, None]) & (index[None, :] < index[:, None])
    )
    rank = jnp.sum(ahead.astype(jnp.int32), axis=1)
    ranked = jnp.sum(jnp.where(rank[None, :] == index[:, None], index[None, :], 0), axis=1)
    above = jnp.stack([jnp.sum((counted > limit).astype(jnp.int32)) for limit in STEPS[1:] + (0,)])
    group = 2 * PAIRS
    bounds = jnp.concatenate([jnp.zeros((1,), jnp.int32), (above + group - 1) // group])
    return ranked.astype(jnp.int32), bounds.astype(jnp.int32)


def attention(picked, counted, order, rows, after):
    ranked, bounds = ranking(counted)
    smem = pl.BlockSpec(memory_space=pltpu.SMEM)
    vmem = pl.BlockSpec(memory_space=pltpu.VMEM)
    return pl.pallas_call(
        attention_kernel,
        out_shape=(
            jax.ShapeDtypeStruct((NODES, WIDE), jnp.bfloat16),
            jax.ShapeDtypeStruct((SEQ, HALF, 2 * HD), jnp.bfloat16),
            jax.ShapeDtypeStruct((SEQ, HALF, 6 * HD), jnp.bfloat16),
        ),
        in_specs=[smem, smem, smem, smem, vmem, vmem, pl.BlockSpec(memory_space=pl.ANY)],
        out_specs=(vmem, vmem, vmem),
        scratch_shapes=[
            pltpu.VMEM((NODES, 2 * HD), jnp.bfloat16),
            pltpu.VMEM((NODES, 2 * HD), jnp.bfloat16),
            pltpu.VMEM((NODES, 2 * HD), jnp.float32),
            pltpu.VMEM((NODES, WIDE), jnp.bfloat16),
            pltpu.VMEM((PAIRS, MAXB * BLK, 4 * BLK), jnp.float32),
        ],
        compiler_params=pltpu.CompilerParams(vmem_limit_bytes=VMEM_BYTES),
        cost_estimate=pl.CostEstimate(flops=10_000_000_000, bytes_accessed=4_000_000, transcendentals=1_000_000),
        name="clustered_attention",
    )(picked, counted, ranked, bounds, order, rows, after)


def project_kernel(features_ref, upstream_ref, w_qkv_ref, w_out_ref, sent_ref, normed_ref):
    @pl.when(pl.program_id(0) == 0)
    def _():
        wide = features_ref[...].astype(jnp.float32)
        inv_rms = lax.rsqrt(jnp.mean(wide * wide, axis=-1, keepdims=True) + EPS)
        normed_ref[...] = (wide * inv_rms).astype(jnp.bfloat16)

    packed = contract(normed_ref[...], w_qkv_ref[...], 1, 0)
    grads = contract(upstream_ref[...], w_out_ref[...], 1, 1)
    for k in range(2):
        sent_ref[k] = jnp.concatenate(
            [packed[:, k * 3 * HD : (k + 1) * 3 * HD], grads[:, k * HD : (k + 1) * HD]], axis=1
        ).astype(jnp.bfloat16)


def project(features, upstream, w_qkv, w_out):
    whole = pl.BlockSpec((ROWS, D), lambda i: (0, 0))
    return pl.pallas_call(
        project_kernel,
        grid=(H // 2,),
        out_shape=(
            jax.ShapeDtypeStruct((H, ROWS, WIDE), jnp.bfloat16),
            jax.ShapeDtypeStruct((ROWS, D), jnp.bfloat16),
        ),
        in_specs=[
            whole,
            whole,
            pl.BlockSpec((D, 6 * HD), lambda i: (0, i)),
            pl.BlockSpec((2 * HD, D), lambda i: (i, 0)),
        ],
        out_specs=(pl.BlockSpec((2, ROWS, WIDE), lambda i: (i, 0, 0)), whole),
        compiler_params=pltpu.CompilerParams(vmem_limit_bytes=VMEM_BYTES),
        cost_estimate=pl.CostEstimate(flops=2 * ROWS * D * 4 * D, bytes_accessed=9_500_000, transcendentals=ROWS),
        name="project",
    )(features, upstream, w_qkv, w_out)


def node_rows(one, two):
    halves = [jnp.concatenate([one[:, lanes], two[:, lanes]], axis=1) for lanes in (slice(0, HD), slice(HD, 2 * HD))]
    return jnp.concatenate(halves, axis=0)


def finish_kernel(features_ref, upstream_ref, attn_ref, grads_ref, w_qkv_ref, w_out_ref, mixed_ref, grad_ref, mixed_acc, grad_acc):
    step = pl.program_id(0)

    @pl.when(step == 0)
    def _():
        mixed_acc[...] = features_ref[...].astype(jnp.float32)
        grad_acc[...] = jnp.zeros_like(grad_acc)

    attn, grads = node_rows(attn_ref[0], attn_ref[1]), []
    for k in range(2):
        block = grads_ref[k]
        first, values, second = block[:, : 2 * HD], block[:, 2 * HD : 4 * HD], block[:, 4 * HD :]
        grads.append(
            jnp.concatenate(
                [
                    jnp.concatenate([first, values[:, :HD]], axis=1),
                    jnp.concatenate([second, values[:, HD:]], axis=1),
                ],
                axis=0,
            )
        )
    grads = jnp.concatenate(grads, axis=1)
    mixed_acc[...] += contract(attn, w_out_ref[...], 1, 0)
    grad_acc[...] += contract(grads, w_qkv_ref[...], 1, 1)

    @pl.when(step == pl.num_programs(0) - 1)
    def _():
        wide = features_ref[...].astype(jnp.float32)
        inv_rms = lax.rsqrt(jnp.mean(wide * wide, axis=-1, keepdims=True) + EPS)
        grad_normed = grad_acc[...]
        inner = jnp.mean(grad_normed * wide, axis=-1, keepdims=True)
        mixed_ref[...] = mixed_acc[...].astype(jnp.bfloat16)
        grad_ref[...] = (
            upstream_ref[...].astype(jnp.float32)
            + inv_rms * grad_normed
            - wide * inv_rms * inv_rms * inv_rms * inner
        ).astype(jnp.bfloat16)


def finish(features, upstream, attn, grads, w_qkv, w_out):
    whole = pl.BlockSpec((ROWS, D), lambda i: (0, 0))
    return pl.pallas_call(
        finish_kernel,
        grid=(H // 2,),
        out_shape=(jax.ShapeDtypeStruct((ROWS, D), jnp.bfloat16),) * 2,
        in_specs=[
            whole,
            whole,
            pl.BlockSpec((2, HALF, 2 * HD), lambda i: (i, 0, 0)),
            pl.BlockSpec((2, HALF, 6 * HD), lambda i: (i, 0, 0)),
            pl.BlockSpec((D, 6 * HD), lambda i: (0, i)),
            pl.BlockSpec((2 * HD, D), lambda i: (i, 0)),
        ],
        out_specs=(whole, whole),
        scratch_shapes=[pltpu.VMEM((ROWS, D), jnp.float32)] * 2,
        compiler_params=pltpu.CompilerParams(vmem_limit_bytes=VMEM_BYTES),
        cost_estimate=pl.CostEstimate(flops=2 * ROWS * D * 4 * D, bytes_accessed=10_000_000, transcendentals=ROWS),
        name="finish",
    )(features, upstream, attn, grads, w_qkv, w_out)


CORES = 2
CHIPS = DP // CORES
SHARE = ROWS + 3 * HD


def place():
    me = lax.axis_index("dp")
    return me // CORES, me % CORES


def stacked(blocks, after):
    def kernel(*refs):
        for k in range(len(blocks)):
            refs[-1][k * ROWS : (k + 1) * ROWS] = refs[k][...]

    vmem = pl.BlockSpec(memory_space=pltpu.VMEM)
    return pl.pallas_call(
        kernel,
        out_shape=jax.ShapeDtypeStruct((len(blocks) * ROWS, D), jnp.bfloat16),
        in_specs=[vmem] * len(blocks) + [pl.BlockSpec(memory_space=pl.ANY)],
        out_specs=vmem,
        compiler_params=pltpu.CompilerParams(vmem_limit_bytes=VMEM_BYTES),
        cost_estimate=pl.CostEstimate(flops=0, bytes_accessed=4 * D * ROWS * len(blocks), transcendentals=0),
        name="stacked",
    )(*blocks, after)


def weight_qkv_kernel(out_ref, nodes_ref, sent_ref):
    total = None
    for t in range(NODES // CHUNK):
        rows = slice(t * CHUNK, (t + 1) * CHUNK)
        wide = nodes_ref[rows, :].astype(jnp.float32)
        inv_rms = lax.rsqrt(jnp.mean(wide * wide, axis=-1, keepdims=True) + EPS)
        part = contract(out_ref[rows, : 3 * HD], (wide * inv_rms).astype(jnp.bfloat16), 0, 0)
        total = part if total is None else total + part
    for i in range(DP):
        sent_ref[i] = total[:, i * ROWS : (i + 1) * ROWS].astype(jnp.bfloat16)


def weight_qkv(head_out, all_nodes):
    vmem = pl.BlockSpec(memory_space=pltpu.VMEM)
    return pl.pallas_call(
        weight_qkv_kernel,
        out_shape=jax.ShapeDtypeStruct((DP, 3 * HD, ROWS), jnp.bfloat16),
        in_specs=[vmem, vmem],
        out_specs=vmem,
        compiler_params=pltpu.CompilerParams(vmem_limit_bytes=VMEM_BYTES),
        cost_estimate=pl.CostEstimate(flops=2 * NODES * D * 3 * HD, bytes_accessed=6_000_000, transcendentals=0),
        name="weight_qkv",
    )(head_out, all_nodes)


def shares_kernel(attn_ref, qkv_ref, grads_ref, own_ref, sent_ref, through_ref):
    _, core = place()
    for chip in range(CHIPS):
        for ref, c in ((own_ref, core), (sent_ref, 1 - core)):
            i = chip * CORES + c
            ref[chip, :HALF] = attn_ref[2 * i]
            ref[chip, HALF:ROWS] = attn_ref[2 * i + 1]
            ref[chip, ROWS:] = qkv_ref[i]


def shares(attn, part_qkv, grads):
    vmem = pl.BlockSpec(memory_space=pltpu.VMEM)
    anywhere = pl.BlockSpec(memory_space=pl.ANY)
    share = jax.ShapeDtypeStruct((CHIPS, SHARE, ROWS), jnp.bfloat16)
    return pl.pallas_call(
        shares_kernel,
        out_shape=(share, share, jax.ShapeDtypeStruct(grads.shape, grads.dtype)),
        in_specs=[vmem, vmem, anywhere],
        out_specs=(vmem, vmem, anywhere),
        input_output_aliases={2: 2},
        compiler_params=pltpu.CompilerParams(vmem_limit_bytes=VMEM_BYTES),
        name="shares",
    )(attn, part_qkv, grads)


def chips_kernel(own_ref, other_ref, *sent_refs):
    y, core = place()
    for step, ref in enumerate(sent_refs):
        chip = (y + step) % CHIPS
        own, other = own_ref[chip], other_ref[chip]
        first = core == 0
        ref[:ROWS] = jnp.where(first, own[:ROWS], other[:ROWS])
        ref[ROWS : 2 * ROWS] = jnp.where(first, other[:ROWS], own[:ROWS])
        ref[2 * ROWS :] = (own[ROWS:].astype(jnp.float32) + other[ROWS:].astype(jnp.float32)).astype(jnp.bfloat16)


def over_dp(own, sent):
    other = lax.ppermute(sent, "dp", [(i, i ^ 1) for i in range(DP)])
    vmem = pl.BlockSpec(memory_space=pltpu.VMEM)
    shape = jax.ShapeDtypeStruct((ROWS + SHARE, ROWS), jnp.bfloat16)
    parts = pl.pallas_call(
        chips_kernel,
        out_shape=(shape,) * CHIPS,
        in_specs=[vmem, vmem],
        out_specs=(vmem,) * CHIPS,
        compiler_params=pltpu.CompilerParams(vmem_limit_bytes=VMEM_BYTES),
        name="chips",
    )(own, other)
    return parts[0], *(lax.ppermute(parts[step], "dp", chip_shift(step)) for step in (1, 2, 3))


def chip_shift(step):
    return [(i, (i + step * CORES) % DP) for i in range(DP)]


def batches_of(block, after):
    moved = [lax.ppermute(block, "dp", chip_shift(step)) for step in (1, 2, 3)]
    mine = stacked((block, *moved), after)
    return mine, lax.ppermute(mine, "dp", [(i, i ^ 1) for i in range(DP)])


def weight_out_kernel(*refs):
    parts, (mine_ref, other_ref, sent_ref) = refs[:CHIPS], refs[CHIPS:]
    _, core = place()
    total, mine, other = None, [], []
    for ref in parts:
        qkv = ref[2 * ROWS :].astype(jnp.float32)
        total = qkv if total is None else total + qkv
        attn = [node_rows(ref[c * ROWS : c * ROWS + HALF], ref[c * ROWS + HALF : (c + 1) * ROWS]) for c in range(CORES)]
        mine.append(jnp.where(core == 0, attn[0], attn[1]))
        other.append(jnp.where(core == 0, attn[1], attn[0]))
    out = contract(jnp.concatenate(mine, axis=0), mine_ref[...], 0, 0)
    out += contract(jnp.concatenate(other, axis=0), other_ref[...], 0, 0)
    qkv = jnp.transpose(total)
    nothing = jnp.zeros((8, HD), jnp.float32)
    for s in range(SEQ):
        rows = slice(s * 8, (s + 1) * 8)
        sent_ref[s] = jnp.concatenate(
            [
                jnp.concatenate([out[rows, : D // 2], out[rows, D // 2 :]], axis=0),
                jnp.concatenate(
                    [qkv[rows, : 2 * HD], jnp.concatenate([qkv[rows, 2 * HD :], nothing], axis=1)], axis=0
                ),
            ],
            axis=1,
        ).astype(jnp.bfloat16)


def weight_out(parts, mine, other):
    vmem = pl.BlockSpec(memory_space=pltpu.VMEM)
    return pl.pallas_call(
        weight_out_kernel,
        out_shape=jax.ShapeDtypeStruct((SEQ, 16, D // 2 + 2 * HD), jnp.bfloat16),
        in_specs=[vmem] * (CHIPS + 2),
        out_specs=vmem,
        compiler_params=pltpu.CompilerParams(vmem_limit_bytes=VMEM_BYTES),
        cost_estimate=pl.CostEstimate(flops=2 * DP * ROWS * D * ROWS, bytes_accessed=3_000_000, transcendentals=0),
        name="weight_out",
    )(*parts, mine, other)


def fold_kernel(parts_ref, qkv_ref, out_ref):
    total = parts_ref[0, :, : D // 2].astype(jnp.float32)
    for s in range(1, SEQ):
        total = total + parts_ref[s, :, : D // 2].astype(jnp.float32)
    out_ref[:, : D // 2] = total[:8]
    out_ref[:, D // 2 :] = total[8:]
    for h in range(H):
        part = parts_ref[h, :, D // 2 :].astype(jnp.float32)
        qkv_ref[:, h * 3 * HD : (h + 1) * 3 * HD] = jnp.concatenate([part[:8], part[8:, :HD]], axis=1)


def fold(parts):
    vmem = pl.BlockSpec(memory_space=pltpu.VMEM)
    return pl.pallas_call(
        fold_kernel,
        out_shape=(
            jax.ShapeDtypeStruct((8, 3 * D), jnp.float32),
            jax.ShapeDtypeStruct((8, D), jnp.float32),
        ),
        in_specs=[vmem],
        out_specs=(vmem, vmem),
        name="fold",
    )(parts)


def shards(nodes, w_qkv, w_out, cotangent, order, block_list, block_count):
    features, upstream = nodes[0], cotangent[0]
    all_nodes = lax.all_gather(features, "seq", axis=0, tiled=True)
    sent, _ = project(features, upstream, w_qkv, w_out)
    head_rows = lax.all_to_all(sent, "seq", 0, 0, tiled=True).reshape(NODES, WIDE)
    upstreams = batches_of(upstream, sent)
    head_out, attn_sent, grads_sent = attention(block_list[0], block_count[0], order, head_rows, upstreams[0])
    attn = lax.all_to_all(attn_sent, "seq", 0, 0, tiled=True)

    own, sent, grads_sent = shares(attn, weight_qkv(head_out, all_nodes), grads_sent)
    grads = lax.all_to_all(grads_sent, "seq", 0, 0, tiled=True)
    parts = weight_out(over_dp(own, sent), *upstreams)
    grad_qkv, grad_out = fold(lax.all_to_all(parts, "seq", 0, 0, tiled=True))

    mixed, grad_nodes = finish(features, upstream, attn, grads, w_qkv, w_out)
    return mixed[None], grad_nodes[None], grad_qkv, grad_out


def solution(mesh):
    return jax.shard_map(
        shards,
        mesh=mesh,
        in_specs=(
            P("dp", "seq", None),
            P(),
            P(),
            P("dp", "seq", None),
            P("dp", None),
            P("dp", None, None),
            P("dp", None),
        ),
        out_specs=(
            P("dp", "seq", None),
            P("dp", "seq", None),
            P(("dp", "seq"), None),
            P(("dp", "seq"), None),
        ),
        check_vma=False,
    )
```

time: 184 us -> 130 us (0.71)
  the two profiles are of different devices: /device:TPU:7 before, /device:TPU:0 now
where the time goes in v2:
time: 130 us; the launch traced here: 128 us
  Pallas kernels  49.5 us (38%)
  starting transfers between devices  38 us (29%)
  waiting for transfers between devices  17.4 us (13%)
  between operations  14.2 us (11%)
  local copies, waits for them, and re-layouts  5.89 us (5%)
  other arithmetic  3.47 us (3%)
    pallas_call x1, Pallas kernels, attention(): pl.pallas_call(attention_kernel, out_shape=(jax.ShapeDtypeStruct((NODES,...  15.7 us
    pallas_call x1, Pallas kernels, finish(): pl.pallas_call(finish_kernel, grid=(H // 2,), out_shape=(jax.ShapeDtypeSt...  9.26 us
    pallas_call x1, Pallas kernels, project(): pl.pallas_call(project_kernel, grid=(H // 2,), out_shape=(jax.ShapeDtypeS...  8.61 us
    all_to_all x1, starting transfers between devices, shards(): lax.all_to_all(sent, 'seq', 0, 0, tiled=True).reshape(NODES, WIDE)  7.96 us
    all_to_all x1, starting transfers between devices, shards(): grad_qkv, grad_out = fold(lax.all_to_all(parts, 'seq', 0, 0, tiled=True))  7.03 us
    ppermute x3, starting transfers between devices, over_dp(): lax.ppermute(parts[step], 'dp', chip_shift(step))  6.29 us
    all_to_all x1, starting transfers between devices, shards(): attn = lax.all_to_all(attn_sent, 'seq', 0, 0, tiled=True)  5.94 us
    ppermute x3, starting transfers between devices, batches_of(): moved = [lax.ppermute(block, 'dp', chip_shift(step)) for step in (1, 2, 3)]  5.89 us
  transfers between devices with their start and end apart: 13, of which 7 were waited for; matrix products, arithmetic and copies ran while one was open for 3% of the time, Pallas kernels for 37%

profile of v2, /device:TPU:0, one launch (start us, length us, event | category | flops | bytes accessed | tf_op | source)
XLA Modules:
  0.0 128.4 jit_solution(14848956638818934881)
XLA Ops:
  7.2 0.0 all-gather.3.cloned.1.call-start
  7.2 0.7 all-gather.3.cloned.1.call-update
  7.9 0.0 copy-start.1
  7.9 0.0 copy-start.14
  7.9 0.0 copy-start.13
  7.9 8.6 %project.1 = (bf16[16,128,256]{2,1,0:T(8,128)(2,1)}, bf16[128,1024]{1,0:T(8,128)(2,1)}) custom-call(bf16[128,1024]{1,0:T(8,128)(2,1)} %bitcast.19, bf16[128,1024]{1,0:T(8,128)(2,1)} %bitcast.13, bf16[1024,3072]{1,0:T(8,128)(2,1)} %w_qkv_ref.3, bf16[1024,1024]{1,0:T(8,128)(2,1)} %w_out_ref.3), custom_call_target="tpu_custom_call" | custom-call | flops 1073741824 | bytes 9500000 | tf_op jit(solution)/shard_map/project/pallas_call | solution.py:223
  16.5 8.0 %all-to-all-start = ((bf16[16,128,256]{2,1,0:T(8,128)(2,1)}), bf16[16,128,256]{2,1,0:T(8,128)(2,1)S(1)}, u32[]{:S(2)}, u32[]{:S(2)}) async-start(bf16[16,128,256]{2,1,0:T(8,128)(2,1)} %get-tuple-element.19.refs_4_), calls=%async_computation | async-start | bytes 2097152 | tf_op jit(solution)/shard_map/all_to_all | solution.py:491
  24.5 0.0 copy-done.1
  24.5 1.6 %collective-permute-start = (bf16[128,1024]{1,0:T(8,128)(2,1)S(1)}, bf16[128,1024]{1,0:T(8,128)(2,1)S(1)}, u32[]{:S(2)}, u32[]{:S(2)}) collective-permute-start(bf16[128,1024]{1,0:T(8,128)(2,1)S(1)} %bitcast.16), channel_id=1, source_target_pairs={{0,32},{16,48},{32,64},{48,80},{64,96},{80,112},{96,0},{112,16},{1... | collective-permute-start | bytes 786440 | tf_op jit(solution)/shard_map/ppermute | solution.py:417
  26.2 2.9 %collective-permute-start.1 = (bf16[128,1024]{1,0:T(8,128)(2,1)S(1)}, bf16[128,1024]{1,0:T(8,128)(2,1)S(1)}, u32[]{:S(2)}, u32[]{:S(2)}) collective-permute-start(bf16[128,1024]{1,0:T(8,128)(2,1)S(1)} %bitcast.17), channel_id=1, source_target_pairs={{0,64},{16,80},{32,96},{48,112},{64,0},{80,16},{96,32},{112,48},{1... | collective-permute-start | bytes 786440 | tf_op jit(solution)/shard_map/ppermute | solution.py:417
  29.1 1.3 %collective-permute-start.2 = (bf16[128,1024]{1,0:T(8,128)(2,1)S(1)}, bf16[128,1024]{1,0:T(8,128)(2,1)S(1)}, u32[]{:S(2)}, u32[]{:S(2)}) collective-permute-start(bf16[128,1024]{1,0:T(8,128)(2,1)S(1)} %bitcast.18), channel_id=1, source_target_pairs={{0,96},{16,112},{32,0},{48,16},{64,32},{80,48},{96,64},{112,80},{1... | collective-permute-start | bytes 786440 | tf_op jit(solution)/shard_map/ppermute | solution.py:417
  30.4 0.0 copy-done.14
  30.4 0.6 fusion.2
  31.1 1.4 %and_select_fusion = s32[2]{0:T(128)S(1)} fusion(s32[1]{0:T(128)} %bitcast.5, s32[1]{0:T(128)} %bitcast.4), kind=kLoop, calls=%fused_computation.6 | loop fusion | flops 34 | bytes 16 | tf_op jit(solution)/shard_map/jit(floor_divide)/jit(_where)/select_n | solution.py:176
  32.4 0.6 pad_add_fusion.bounds_ref
  33.1 0.0 copy-done.13
  33.1 0.7 copy.13
  33.8 0.2 convert_reduce_fusion
  33.9 0.6 select_reduce_fusion.ranked_ref
  34.6 0.0 collective-permute-done.refs_1_
  34.6 0.0 copy-start.7
  34.6 5.8 %collective-permute-done.1.refs_2_ = bf16[128,1024]{1,0:T(8,128)(2,1)S(1)} collective-permute-done((bf16[128,1024]{1,0:T(8,128)(2,1)S(1)}, bf16[128,1024]{1,0:T(8,128)(2,1)S(1)}, u32[]{:S(2)}, u32[]{:S(2)}) %collective-permute-start.1) | collective-permute-done | bytes 262176 | tf_op jit(solution)/shard_map/ppermute | solution.py:417
  40.4 0.0 copy-start.8
  40.4 0.0 collective-permute-done.2.refs_3_
  40.4 0.0 copy-done.7
  40.4 0.7 copy-done.8
  41.1 0.0 copy-start.9
  41.1 0.7 copy-done.9
  41.8 2.3 %stacked.1.after_ref.refs_4_ = bf16[512,1024]{1,0:T(8,128)(2,1)} custom-call(bf16[128,1024]{1,0:T(8,128)(2,1)} %bitcast.14, bf16[128,1024]{1,0:T(8,128)(2,1)} %copy-done.7, bf16[128,1024]{1,0:T(8,128)(2,1)} %copy-done.8, bf16[128,1024]{1,0:T(8,128)(2,1)} %copy-done.9, bf16[16,128,256]{2,1,0:T(8,128)(2,1)} %get-tuple-element.19.refs_4_), custom_call_target="tpu_custom_call" | custom-call | bytes 2097152 | tf_op jit(solution)/shard_map/stacked/pallas_call | solution.py:325
  44.1 0.0 collective-permute-start.7
  44.1 1.0 all-to-all-done
  45.1 0.0 copy-start.4
  45.1 1.0 copy-done.4
  46.1 15.7 %clustered_attention.1 = (bf16[2048,256]{1,0:T(8,128)(2,1)}, bf16[16,64,128]{2,1,0:T(8,128)(2,1)}, bf16[16,64,384]{2,1,0:T(8,128)(2,1)}) custom-call(s32[32,8]{1,0:T(8,128)} %bitcast.22, s32[32]{0:T(128)} %bitcast.25, s32[32]{0:T(128)} %select_reduce_fusion.ranked_ref, s32[3]{0:T(128)} %pad_add_fusion.bounds_ref, s32[1,2048]{1,0:T(1,128)} %order_ref.1, ...), custom_call_target="tpu_custom_call" | custom-call | flops 10000000000 | bytes 4000000 | tf_op jit(solution)/shard_map/clustered_attention/pallas_call | solution.py:184
  61.7 5.9 %all-to-all-start.1 = ((bf16[16,64,128]{2,1,0:T(8,128)(2,1)}), bf16[16,64,128]{2,1,0:T(8,128)(2,1)S(1)}, u32[]{:S(2)}, u32[]{:S(2)}) async-start(bf16[16,64,128]{2,1,0:T(8,128)(2,1)} %get-tuple-element.20), calls=%async_computation.1 | async-start | bytes 524288 | tf_op jit(solution)/shard_map/all_to_all | solution.py:494
  67.7 3.7 %all-gather.3.cloned.1.call-done = bf16[1,2048,1024]{2,1,0:T(8,128)(2,1)} async-done(((bf16[1,128,1024]{2,1,0:T(8,128)(2,1)}), bf16[1,2048,1024]{2,1,0:T(8,128)(2,1)}) %all-gather.3.cloned.1.call-update) | async-done | bytes 4194320 | tf_op jit(solution)/shard_map/all_gather | solution.py:489
  71.4 5.1 %weight_qkv.1.qkv_ref = bf16[8,192,128]{2,1,0:T(8,128)(2,1)} custom-call(bf16[2048,256]{1,0:T(8,128)(2,1)} %get-tuple-element.21.out_ref, bf16[2048,1024]{1,0:T(8,128)(2,1)} %bitcast.12), custom_call_target="tpu_custom_call" | custom-call | flops 805306368 | bytes 6000000 | tf_op jit(solution)/shard_map/weight_qkv/pallas_call | solution.py:350
  76.4 0.6 all-to-all-done.1.attn_ref
  77.1 0.7 copy-done.2
  77.8 2.0 %shares.1 = (bf16[4,320,128]{2,1,0:T(8,128)(2,1)}, bf16[4,320,128]{2,1,0:T(8,128)(2,1)}, bf16[16,64,384]{2,1,0:T(8,128)(2,1)}) custom-call(bf16[16,64,128]{2,1,0:T(8,128)(2,1)} %copy-done.2, bf16[8,192,128]{2,1,0:T(8,128)(2,1)} %weight_qkv.1.qkv_ref, bf16[16,64,384]{2,1,0:T(8,128)(2,1)} %get-tuple-element.22.grads_ref), custom_call_target="tpu_custom_call", output_to_operand_aliasing={{2}: (2, {})} | custom-call | tf_op jit(solution)/shard_map/shares/pallas_call | solution.py:375
  79.7 4.6 %all-to-all-start.2 = ((bf16[16,64,384]{2,1,0:T(8,128)(2,1)}), bf16[16,64,384]{2,1,0:T(8,128)(2,1)S(1)}, u32[]{:S(2)}, u32[]{:S(2)}) async-start(bf16[16,64,384]{2,1,0:T(8,128)(2,1)} %get-tuple-element.23), calls=%async_computation.2 | async-start | bytes 1572864 | tf_op jit(solution)/shard_map/all_to_all | solution.py:497
  84.4 0.3 collective-permute-start.3
  84.6 1.8 %collective-permute-done.3.other_ref = bf16[4,320,128]{2,1,0:T(8,128)(2,1)S(1)} collective-permute-done((bf16[4,320,128]{2,1,0:T(8,128)(2,1)}, bf16[4,320,128]{2,1,0:T(8,128)(2,1)S(1)}, u32[]{:S(2)}, u32[]{:S(2)}) %collective-permute-start.3) | collective-permute-done | bytes 327712 | tf_op jit(solution)/shard_map/ppermute | solution.py:398
  86.5 0.7 copy-done.6
  87.2 1.9 %chips.1 = (bf16[448,128]{1,0:T(8,128)(2,1)}, bf16[448,128]{1,0:T(8,128)(2,1)}, bf16[448,128]{1,0:T(8,128)(2,1)}, bf16[448,128]{1,0:T(8,128)(2,1)}) custom-call(bf16[4,320,128]{2,1,0:T(8,128)(2,1)} %get-tuple-element.26.own_ref, bf16[4,320,128]{2,1,0:T(8,128)(2,1)} %copy-done.6), custom_call_target="tpu_custom_call" | custom-call | tf_op jit(solution)/shard_map/chips/pallas_call | solution.py:401
  89.1 1.5 %collective-permute-start.4 = (bf16[448,128]{1,0:T(8,128)(2,1)}, bf16[448,128]{1,0:T(8,128)(2,1)S(1)}, u32[]{:S(2)}, u32[]{:S(2)}) collective-permute-start(bf16[448,128]{1,0:T(8,128)(2,1)} %get-tuple-element.29), channel_id=1, source_target_pairs={{0,32},{16,48},{32,64},{48,80},{64,96},{80,112},{96,0},{112,16},{1... | collective-permute-start | bytes 344072 | tf_op jit(solution)/shard_map/ppermute | solution.py:409
  90.5 2.7 %collective-permute-start.5 = (bf16[448,128]{1,0:T(8,128)(2,1)}, bf16[448,128]{1,0:T(8,128)(2,1)S(1)}, u32[]{:S(2)}, u32[]{:S(2)}) collective-permute-start(bf16[448,128]{1,0:T(8,128)(2,1)} %get-tuple-element.30), channel_id=1, source_target_pairs={{0,64},{16,80},{32,96},{48,112},{64,0},{80,16},{96,32},{112,48},{1... | collective-permute-start | bytes 344072 | tf_op jit(solution)/shard_map/ppermute | solution.py:409
  93.3 2.1 %collective-permute-start.6 = (bf16[448,128]{1,0:T(8,128)(2,1)}, bf16[448,128]{1,0:T(8,128)(2,1)S(1)}, u32[]{:S(2)}, u32[]{:S(2)}) collective-permute-start(bf16[448,128]{1,0:T(8,128)(2,1)} %get-tuple-element.31), channel_id=1, source_target_pairs={{0,96},{16,112},{32,0},{48,16},{64,32},{80,48},{96,64},{112,80},{1... | collective-permute-start | bytes 344072 | tf_op jit(solution)/shard_map/ppermute | solution.py:409
  95.3 0.0 collective-permute-done.7.refs_5_
  95.4 0.3 collective-permute-done.4.refs_1_
  95.7 3.4 %collective-permute-done.5.refs_2_ = bf16[448,128]{1,0:T(8,128)(2,1)S(1)} collective-permute-done((bf16[448,128]{1,0:T(8,128)(2,1)}, bf16[448,128]{1,0:T(8,128)(2,1)S(1)}, u32[]{:S(2)}, u32[]{:S(2)}) %collective-permute-start.5) | collective-permute-done | bytes 114720 | tf_op jit(solution)/shard_map/ppermute | solution.py:409
  99.1 0.0 collective-permute-done.6.refs_3_
  99.1 0.0 copy-done.5
  99.1 0.0 copy-done.10
  99.1 0.6 copy-done.11
  99.8 0.1 copy-done.12
  99.8 3.1 %weight_out.1 = bf16[16,16,640]{2,1,0:T(8,128)(2,1)} custom-call(bf16[448,128]{1,0:T(8,128)(2,1)} %get-tuple-element.28.refs_0_, bf16[448,128]{1,0:T(8,128)(2,1)} %copy-done.10, bf16[448,128]{1,0:T(8,128)(2,1)} %copy-done.11, bf16[448,128]{1,0:T(8,128)(2,1)} %copy-done.12, bf16[512,1024]{1,0:T(8,128)(2,1)} %stacked.1.after_ref.refs_4_, ...), custom_call_target="tpu_custom_call" | custom-call | flops 268435456 | bytes 3000000 | tf_op jit(solution)/shard_map/weight_out/pallas_call | solution.py:451
  102.9 0.0 all-to-all-done.2.grads_ref
  102.9 7.0 %all-to-all-start.3 = ((bf16[16,16,640]{2,1,0:T(8,128)(2,1)}), bf16[16,16,640]{2,1,0:T(8,128)(2,1)S(1)}, u32[]{:S(2)}, u32[]{:S(2)}) async-start(bf16[16,16,640]{2,1,0:T(8,128)(2,1)} %weight_out.1), calls=%async_computation.3 | async-start | bytes 655360 | tf_op jit(solution)/shard_map/all_to_all | solution.py:499
  109.9 0.0 copy-done
  109.9 9.3 %finish.1 = (bf16[128,1024]{1,0:T(8,128)(2,1)}, bf16[128,1024]{1,0:T(8,128)(2,1)}) custom-call(bf16[128,1024]{1,0:T(8,128)(2,1)} %bitcast.20, bf16[128,1024]{1,0:T(8,128)(2,1)} %bitcast.15, bf16[16,64,128]{2,1,0:T(8,128)(2,1)} %copy-done.2, bf16[16,64,384]{2,1,0:T(8,128)(2,1)} %copy-done, bf16[1024,3072]{1,0:T(8,128)(2,1)} %w_qkv_ref.3, ...), custom_call_target="tpu_custom_call" | custom-call | flops 1073741824 | bytes 10000000 | tf_op jit(solution)/shard_map/finish/pallas_call | solution.py:289
  119.2 0.0 all-to-all-done.3.parts_ref
  119.2 0.7 copy-done.3
  119.9 1.7 %fold.1 = (f32[8,3072]{1,0:T(8,128)}, f32[8,1024]{1,0:T(8,128)}) custom-call(bf16[16,16,640]{2,1,0:T(8,128)(2,1)} %copy-done.3), custom_call_target="tpu_custom_call" | custom-call | tf_op jit(solution)/shard_map/fold/pallas_call | solution.py:475
  (8 shorter events, 0.0 us)
Async XLA Ops:
  7.2 64.2 %all-gather.3.cloned.1.call-start = ((), (), s32[]{:S(2)}) async-start(), calls=%async_computation.4 | async-start | bytes 4456448 | tf_op jit(solution)/shard_map/all_gather | solution.py:489
  7.9 16.6 %copy-start.1 = (bf16[1,128,1024]{2,1,0:T(8,128)(2,1)S(1)}, bf16[1,128,1024]{2,1,0:T(8,128)(2,1)}, u32[]{:S(2)}) copy-start(bf16[1,128,1024]{2,1,0:T(8,128)(2,1)} %param.10) | copy-start | bytes 786436
  7.9 22.5 %copy-start.14 = (s32[1,32]{1,0:T(1,128)S(1)}, s32[1,32]{1,0:T(1,128)}, u32[]{:S(2)}) copy-start(s32[1,32]{1,0:T(1,128)} %param.13) | copy-start | bytes 388
  7.9 25.2 %copy-start.13 = (s32[1,32,8]{1,2,0:T(8,128)S(1)}, s32[1,32,8]{1,2,0:T(8,128)}, u32[]{:S(2)}) copy-start(s32[1,32,8]{1,2,0:T(8,128)} %param.12) | copy-start | bytes 3076
  16.5 28.6 %all-to-all-start = ((bf16[16,128,256]{2,1,0:T(8,128)(2,1)}), bf16[16,128,256]{2,1,0:T(8,128)(2,1)S(1)}, u32[]{:S(2)}, u32[]{:S(2)}) async-start(bf16[16,128,256]{2,1,0:T(8,128)(2,1)} %get-tuple-element.19.refs_4_), calls=%async_computation | async-start | bytes 2097152 | tf_op jit(solution)/shard_map/all_to_all | solution.py:491
  24.5 10.1 %collective-permute-start = (bf16[128,1024]{1,0:T(8,128)(2,1)S(1)}, bf16[128,1024]{1,0:T(8,128)(2,1)S(1)}, u32[]{:S(2)}, u32[]{:S(2)}) collective-permute-start(bf16[128,1024]{1,0:T(8,128)(2,1)S(1)} %bitcast.16), channel_id=1, source_target_pairs={{0,32},{16,48},{32,64},{48,80},{64,96},{80,112},{96,0},{112,16},{1... | collective-permute-start | bytes 786440 | tf_op jit(solution)/shard_map/ppermute | solution.py:417
  26.2 14.3 %collective-permute-start.1 = (bf16[128,1024]{1,0:T(8,128)(2,1)S(1)}, bf16[128,1024]{1,0:T(8,128)(2,1)S(1)}, u32[]{:S(2)}, u32[]{:S(2)}) collective-permute-start(bf16[128,1024]{1,0:T(8,128)(2,1)S(1)} %bitcast.17), channel_id=1, source_target_pairs={{0,64},{16,80},{32,96},{48,112},{64,0},{80,16},{96,32},{112,48},{1... | collective-permute-start | bytes 786440 | tf_op jit(solution)/shard_map/ppermute | solution.py:417
  29.1 11.4 %collective-permute-start.2 = (bf16[128,1024]{1,0:T(8,128)(2,1)S(1)}, bf16[128,1024]{1,0:T(8,128)(2,1)S(1)}, u32[]{:S(2)}, u32[]{:S(2)}) collective-permute-start(bf16[128,1024]{1,0:T(8,128)(2,1)S(1)} %bitcast.18), channel_id=1, source_target_pairs={{0,96},{16,112},{32,0},{48,16},{64,32},{80,48},{96,64},{112,80},{1... | collective-permute-start | bytes 786440 | tf_op jit(solution)/shard_map/ppermute | solution.py:417
  34.6 5.9 %copy-start.7 = (bf16[128,1024]{1,0:T(8,128)(2,1)}, bf16[128,1024]{1,0:T(8,128)(2,1)S(1)}, u32[]{:S(2)}) copy-start(bf16[128,1024]{1,0:T(8,128)(2,1)S(1)} %collective-permute-done.refs_1_) | copy-start | bytes 786436
  40.4 0.7 copy-start.8
  41.1 0.7 copy-start.9
  44.1 51.3 %collective-permute-start.7 = (bf16[512,1024]{1,0:T(8,128)(2,1)}, bf16[512,1024]{1,0:T(8,128)(2,1)S(1)}, u32[]{:S(2)}, u32[]{:S(2)}) collective-permute-start(bf16[512,1024]{1,0:T(8,128)(2,1)} %stacked.1.after_ref.refs_4_), channel_id=1, source_target_pairs={{0,16},{16,0},{32,48},{48,32},{64,80},{80,64},{96,112},{112,96},{1... | collective-permute-start | bytes 3145736 | tf_op jit(solution)/shard_map/ppermute | solution.py:419
  45.1 1.0 copy-start.4
  61.7 15.3 %all-to-all-start.1 = ((bf16[16,64,128]{2,1,0:T(8,128)(2,1)}), bf16[16,64,128]{2,1,0:T(8,128)(2,1)S(1)}, u32[]{:S(2)}, u32[]{:S(2)}) async-start(bf16[16,64,128]{2,1,0:T(8,128)(2,1)} %get-tuple-element.20), calls=%async_computation.1 | async-start | bytes 524288 | tf_op jit(solution)/shard_map/all_to_all | solution.py:494
  77.1 0.7 copy-start.2
  79.7 23.1 %all-to-all-start.2 = ((bf16[16,64,384]{2,1,0:T(8,128)(2,1)}), bf16[16,64,384]{2,1,0:T(8,128)(2,1)S(1)}, u32[]{:S(2)}, u32[]{:S(2)}) async-start(bf16[16,64,384]{2,1,0:T(8,128)(2,1)} %get-tuple-element.23), calls=%async_computation.2 | async-start | bytes 1572864 | tf_op jit(solution)/shard_map/all_to_all | solution.py:497
  84.4 2.1 %collective-permute-start.3 = (bf16[4,320,128]{2,1,0:T(8,128)(2,1)}, bf16[4,320,128]{2,1,0:T(8,128)(2,1)S(1)}, u32[]{:S(2)}, u32[]{:S(2)}) collective-permute-start(bf16[4,320,128]{2,1,0:T(8,128)(2,1)} %get-tuple-element.27), channel_id=1, source_target_pairs={{0,16},{16,0},{32,48},{48,32},{64,80},{80,64},{96,112},{112,96},{1... | collective-permute-start | bytes 983048 | tf_op jit(solution)/shard_map/ppermute | solution.py:398
  86.5 0.7 copy-start.6
  89.1 6.6 %collective-permute-start.4 = (bf16[448,128]{1,0:T(8,128)(2,1)}, bf16[448,128]{1,0:T(8,128)(2,1)S(1)}, u32[]{:S(2)}, u32[]{:S(2)}) collective-permute-start(bf16[448,128]{1,0:T(8,128)(2,1)} %get-tuple-element.29), channel_id=1, source_target_pairs={{0,32},{16,48},{32,64},{48,80},{64,96},{80,112},{96,0},{112,16},{1... | collective-permute-start | bytes 344072 | tf_op jit(solution)/shard_map/ppermute | solution.py:409
  90.5 8.6 %collective-permute-start.5 = (bf16[448,128]{1,0:T(8,128)(2,1)}, bf16[448,128]{1,0:T(8,128)(2,1)S(1)}, u32[]{:S(2)}, u32[]{:S(2)}) collective-permute-start(bf16[448,128]{1,0:T(8,128)(2,1)} %get-tuple-element.30), channel_id=1, source_target_pairs={{0,64},{16,80},{32,96},{48,112},{64,0},{80,16},{96,32},{112,48},{1... | collective-permute-start | bytes 344072 | tf_op jit(solution)/shard_map/ppermute | solution.py:409
  93.3 5.8 %collective-permute-start.6 = (bf16[448,128]{1,0:T(8,128)(2,1)}, bf16[448,128]{1,0:T(8,128)(2,1)S(1)}, u32[]{:S(2)}, u32[]{:S(2)}) collective-permute-start(bf16[448,128]{1,0:T(8,128)(2,1)} %get-tuple-element.31), channel_id=1, source_target_pairs={{0,96},{16,112},{32,0},{48,16},{64,32},{80,48},{96,64},{112,80},{1... | collective-permute-start | bytes 344072 | tf_op jit(solution)/shard_map/ppermute | solution.py:409
  95.4 3.8 %copy-start.5 = (bf16[512,1024]{1,0:T(8,128)(2,1)}, bf16[512,1024]{1,0:T(8,128)(2,1)S(1)}, u32[]{:S(2)}) copy-start(bf16[512,1024]{1,0:T(8,128)(2,1)S(1)} %collective-permute-done.7.refs_5_) | copy-start | bytes 3145732
  95.7 3.5 %copy-start.10 = (bf16[448,128]{1,0:T(8,128)(2,1)}, bf16[448,128]{1,0:T(8,128)(2,1)S(1)}, u32[]{:S(2)}) copy-start(bf16[448,128]{1,0:T(8,128)(2,1)S(1)} %collective-permute-done.4.refs_1_) | copy-start | bytes 344068
  99.1 0.6 copy-start.11
  99.1 0.7 copy-start.12
  102.9 7.0 %copy-start = (bf16[16,64,384]{2,1,0:T(8,128)(2,1)}, bf16[16,64,384]{2,1,0:T(8,128)(2,1)S(1)}, u32[]{:S(2)}) copy-start(bf16[16,64,384]{2,1,0:T(8,128)(2,1)S(1)} %all-to-all-done.2.grads_ref) | copy-start | bytes 2359300
  102.9 16.3 %all-to-all-start.3 = ((bf16[16,16,640]{2,1,0:T(8,128)(2,1)}), bf16[16,16,640]{2,1,0:T(8,128)(2,1)S(1)}, u32[]{:S(2)}, u32[]{:S(2)}) async-start(bf16[16,16,640]{2,1,0:T(8,128)(2,1)} %weight_out.1), calls=%async_computation.3 | async-start | bytes 655360 | tf_op jit(solution)/shard_map/all_to_all | solution.py:499
  119.2 0.7 copy-start.3
Sparse Core Ops, SparseCore 0:
  10.1 61.1 all-gather.2

commit v3 on v2

--- a/solution.py
+++ b/solution.py
@@ -23,6 +23,8 @@
 ROWS = 128
 CHUNK = 512
 HALF = ROWS // 2
+STEP = 8
+FEW = 2
 VMEM_BYTES = 60 * 1024 * 1024
 EPS = 1e-05
 SCALE = 1.0 / math.sqrt(HD)
@@ -212,7 +214,7 @@
 
     packed = contract(normed_ref[...], w_qkv_ref[...], 1, 0)
     grads = contract(upstream_ref[...], w_out_ref[...], 1, 1)
-    for k in range(2):
+    for k in range(FEW):
         sent_ref[k] = jnp.concatenate(
             [packed[:, k * 3 * HD : (k + 1) * 3 * HD], grads[:, k * HD : (k + 1) * HD]], axis=1
         ).astype(jnp.bfloat16)
@@ -222,7 +224,7 @@
     whole = pl.BlockSpec((ROWS, D), lambda i: (0, 0))
     return pl.pallas_call(
         project_kernel,
-        grid=(H // 2,),
+        grid=(H // FEW,),
         out_shape=(
             jax.ShapeDtypeStruct((H, ROWS, WIDE), jnp.bfloat16),
             jax.ShapeDtypeStruct((ROWS, D), jnp.bfloat16),
@@ -230,18 +232,18 @@
         in_specs=[
             whole,
             whole,
-            pl.BlockSpec((D, 6 * HD), lambda i: (0, i)),
-            pl.BlockSpec((2 * HD, D), lambda i: (i, 0)),
+            pl.BlockSpec((D, 3 * FEW * HD), lambda i: (0, i)),
+            pl.BlockSpec((FEW * HD, D), lambda i: (i, 0)),
         ],
-        out_specs=(pl.BlockSpec((2, ROWS, WIDE), lambda i: (i, 0, 0)), whole),
+        out_specs=(pl.BlockSpec((FEW, ROWS, WIDE), lambda i: (i, 0, 0)), whole),
         compiler_params=pltpu.CompilerParams(vmem_limit_bytes=VMEM_BYTES),
         cost_estimate=pl.CostEstimate(flops=2 * ROWS * D * 4 * D, bytes_accessed=9_500_000, transcendentals=ROWS),
         name="project",
     )(features, upstream, w_qkv, w_out)
 
 
-def node_rows(one, two):
-    halves = [jnp.concatenate([one[:, lanes], two[:, lanes]], axis=1) for lanes in (slice(0, HD), slice(HD, 2 * HD))]
+def node_rows(*heads):
+    halves = [jnp.concatenate([h[:, lanes] for h in heads], axis=1) for lanes in (slice(0, HD), slice(HD, 2 * HD))]
     return jnp.concatenate(halves, axis=0)
 
 
@@ -253,20 +255,13 @@
         mixed_acc[...] = features_ref[...].astype(jnp.float32)
         grad_acc[...] = jnp.zeros_like(grad_acc)
 
-    attn, grads = node_rows(attn_ref[0], attn_ref[1]), []
-    for k in range(2):
+    attn = node_rows(*(attn_ref[k] for k in range(STEP)))
+    first, second = [], []
+    for k in range(STEP):
         block = grads_ref[k]
-        first, values, second = block[:, : 2 * HD], block[:, 2 * HD : 4 * HD], block[:, 4 * HD :]
-        grads.append(
-            jnp.concatenate(
-                [
-                    jnp.concatenate([first, values[:, :HD]], axis=1),
-                    jnp.concatenate([second, values[:, HD:]], axis=1),
-                ],
-                axis=0,
-            )
-        )
-    grads = jnp.concatenate(grads, axis=1)
+        first += [block[:, : 2 * HD], block[:, 2 * HD : 3 * HD]]
+        second += [block[:, 4 * HD :], block[:, 3 * HD : 4 * HD]]
+    grads = jnp.concatenate([jnp.concatenate(first, axis=1), jnp.concatenate(second, axis=1)], axis=0)
     mixed_acc[...] += contract(attn, w_out_ref[...], 1, 0)
     grad_acc[...] += contract(grads, w_qkv_ref[...], 1, 1)
 
@@ -288,15 +283,15 @@
     whole = pl.BlockSpec((ROWS, D), lambda i: (0, 0))
     return pl.pallas_call(
         finish_kernel,
-        grid=(H // 2,),
+        grid=(H // STEP,),
         out_shape=(jax.ShapeDtypeStruct((ROWS, D), jnp.bfloat16),) * 2,
         in_specs=[
             whole,
             whole,
-            pl.BlockSpec((2, HALF, 2 * HD), lambda i: (i, 0, 0)),
-            pl.BlockSpec((2, HALF, 6 * HD), lambda i: (i, 0, 0)),
-            pl.BlockSpec((D, 6 * HD), lambda i: (0, i)),
-            pl.BlockSpec((2 * HD, D), lambda i: (i, 0)),
+            pl.BlockSpec((STEP, HALF, 2 * HD), lambda i: (i, 0, 0)),
+            pl.BlockSpec((STEP, HALF, 6 * HD), lambda i: (i, 0, 0)),
+            pl.BlockSpec((D, 3 * STEP * HD), lambda i: (0, i)),
+            pl.BlockSpec((STEP * HD, D), lambda i: (i, 0)),
         ],
         out_specs=(whole, whole),
         scratch_shapes=[pltpu.VMEM((ROWS, D), jnp.float32)] * 2,
@@ -308,12 +303,6 @@
 
 CORES = 2
 CHIPS = DP // CORES
-SHARE = ROWS + 3 * HD
-
-
-def place():
-    me = lax.axis_index("dp")
-    return me // CORES, me % CORES
 
 
 def stacked(blocks, after):
@@ -333,7 +322,7 @@
     )(*blocks, after)
 
 
-def weight_qkv_kernel(out_ref, nodes_ref, sent_ref):
+def weight_qkv_kernel(out_ref, nodes_ref, grads_ref, sent_ref, through_ref):
     total = None
     for t in range(NODES // CHUNK):
         rows = slice(t * CHUNK, (t + 1) * CHUNK)
@@ -345,67 +334,51 @@
         sent_ref[i] = total[:, i * ROWS : (i + 1) * ROWS].astype(jnp.bfloat16)
 
 
-def weight_qkv(head_out, all_nodes):
-    vmem = pl.BlockSpec(memory_space=pltpu.VMEM)
+def weight_qkv(head_out, all_nodes, grads):
+    vmem = pl.BlockSpec(memory_space=pltpu.VMEM)
+    anywhere = pl.BlockSpec(memory_space=pl.ANY)
     return pl.pallas_call(
         weight_qkv_kernel,
-        out_shape=jax.ShapeDtypeStruct((DP, 3 * HD, ROWS), jnp.bfloat16),
-        in_specs=[vmem, vmem],
-        out_specs=vmem,
+        out_shape=(
+            jax.ShapeDtypeStruct((DP, 3 * HD, ROWS), jnp.bfloat16),
+            jax.ShapeDtypeStruct(grads.shape, grads.dtype),
+        ),
+        in_specs=[vmem, vmem, anywhere],
+        out_specs=(vmem, anywhere),
+        input_output_aliases={2: 1},
         compiler_params=pltpu.CompilerParams(vmem_limit_bytes=VMEM_BYTES),
         cost_estimate=pl.CostEstimate(flops=2 * NODES * D * 3 * HD, bytes_accessed=6_000_000, transcendentals=0),
         name="weight_qkv",
-    )(head_out, all_nodes)
-
-
-def shares_kernel(attn_ref, qkv_ref, grads_ref, own_ref, sent_ref, through_ref):
-    _, core = place()
-    for chip in range(CHIPS):
-        for ref, c in ((own_ref, core), (sent_ref, 1 - core)):
-            i = chip * CORES + c
-            ref[chip, :HALF] = attn_ref[2 * i]
-            ref[chip, HALF:ROWS] = attn_ref[2 * i + 1]
-            ref[chip, ROWS:] = qkv_ref[i]
-
-
-def shares(attn, part_qkv, grads):
-    vmem = pl.BlockSpec(memory_space=pltpu.VMEM)
-    anywhere = pl.BlockSpec(memory_space=pl.ANY)
-    share = jax.ShapeDtypeStruct((CHIPS, SHARE, ROWS), jnp.bfloat16)
-    return pl.pallas_call(
-        shares_kernel,
-        out_shape=(share, share, jax.ShapeDtypeStruct(grads.shape, grads.dtype)),
-        in_specs=[vmem, vmem, anywhere],
-        out_specs=(vmem, vmem, anywhere),
-        input_output_aliases={2: 2},
-        compiler_params=pltpu.CompilerParams(vmem_limit_bytes=VMEM_BYTES),
-        name="shares",
-    )(attn, part_qkv, grads)
-
-
-def chips_kernel(own_ref, other_ref, *sent_refs):
-    y, core = place()
+    )(head_out, all_nodes, grads)
+
+
+def chips_kernel(attn_ref, qkv_ref, other_attn_ref, other_qkv_ref, *sent_refs):
+    me = lax.axis_index("dp")
+    y, core = me // CORES, me % CORES
+    first = core == 0
     for step, ref in enumerate(sent_refs):
-        chip = (y + step) % CHIPS
-        own, other = own_ref[chip], other_ref[chip]
-        first = core == 0
-        ref[:ROWS] = jnp.where(first, own[:ROWS], other[:ROWS])
-        ref[ROWS : 2 * ROWS] = jnp.where(first, other[:ROWS], own[:ROWS])
-        ref[2 * ROWS :] = (own[ROWS:].astype(jnp.float32) + other[ROWS:].astype(jnp.float32)).astype(jnp.bfloat16)
-
-
-def over_dp(own, sent):
-    other = lax.ppermute(sent, "dp", [(i, i ^ 1) for i in range(DP)])
-    vmem = pl.BlockSpec(memory_space=pltpu.VMEM)
-    shape = jax.ShapeDtypeStruct((ROWS + SHARE, ROWS), jnp.bfloat16)
+        i = ((y + step) % CHIPS) * CORES + core
+        for k in range(2):
+            own, other = attn_ref[2 * i + k], other_attn_ref[2 * i + k]
+            ref[k * HALF : (k + 1) * HALF] = jnp.where(first, own, other)
+            ref[ROWS + k * HALF : ROWS + (k + 1) * HALF] = jnp.where(first, other, own)
+        total = qkv_ref[i].astype(jnp.float32) + other_qkv_ref[i].astype(jnp.float32)
+        ref[2 * ROWS :] = total.astype(jnp.bfloat16)
+
+
+def over_dp(attn, part_qkv):
+    pairs = [(i, i ^ 1) for i in range(DP)]
+    vmem = pl.BlockSpec(memory_space=pltpu.VMEM)
+    shape = jax.ShapeDtypeStruct((2 * ROWS + 3 * HD, ROWS), jnp.bfloat16)
     parts = pl.pallas_call(
         chips_kernel,
         out_shape=(shape,) * CHIPS,
-        in_specs=[vmem, vmem],
+        in_specs=[vmem] * 4,
         out_specs=(vmem,) * CHIPS,
         compiler_params=pltpu.CompilerParams(vmem_limit_bytes=VMEM_BYTES),
+        cost_estimate=pl.CostEstimate(flops=0, bytes_accessed=2_000_000, transcendentals=0),
         name="chips",
-    )(own, other)
+    )(attn, part_qkv, lax.ppermute(attn, "dp", pairs), lax.ppermute(part_qkv, "dp", pairs))
     return parts[0], *(lax.ppermute(parts[step], "dp", chip_shift(step)) for step in (1, 2, 3))
 
 
@@ -421,7 +394,7 @@
 
 def weight_out_kernel(*refs):
     parts, (mine_ref, other_ref, sent_ref) = refs[:CHIPS], refs[CHIPS:]
-    _, core = place()
+    core = lax.axis_index("dp") % CORES
     total, mine, other = None, [], []
     for ref in parts:
         qkv = ref[2 * ROWS :].astype(jnp.float32)
@@ -493,9 +466,9 @@
     head_out, attn_sent, grads_sent = attention(block_list[0], block_count[0], order, head_rows, upstreams[0])
     attn = lax.all_to_all(attn_sent, "seq", 0, 0, tiled=True)
 
-    own, sent, grads_sent = shares(attn, weight_qkv(head_out, all_nodes), grads_sent)
+    part_qkv, grads_sent = weight_qkv(head_out, all_nodes, grads_sent)
     grads = lax.all_to_all(grads_sent, "seq", 0, 0, tiled=True)
-    parts = weight_out(over_dp(own, sent), *upstreams)
+    parts = weight_out(over_dp(attn, part_qkv), *upstreams)
     grad_qkv, grad_out = fold(lax.all_to_all(parts, "seq", 0, 0, tiled=True))
 
     mixed, grad_nodes = finish(features, upstream, attn, grads, w_qkv, w_out)

time: 130 us -> 127 us (0.977); the launches traced: 128 us -> 127 us
  Pallas kernels: 49.5 us -> 45.6 us
  waiting for transfers between devices: 17.4 us -> 19.7 us
    pallas_call x5 -> x4, Pallas kernels: 26.8 us -> 22.3 us  [the longest x1 8.61 us: project(): pl.pallas_call(project_kernel, grid=(H // FEW,), out_shape=(jax.ShapeDtyp...]
    all_to_all x1, waiting for transfers between devices: 0.01 us -> 2.32 us  [shards(): grad_qkv, grad_out = fold(lax.all_to_all(parts, 'seq', 0, 0, tiled=True))]
    unnamed x31 -> x33, local copies, waits for them, and re-layouts: 5.89 us -> 5.93 us
  transfers between devices with their start and end apart: 13 -> 14, of which waited for: 7 -> 8; matrix products, arithmetic and copies ran while one was open for 3% -> 3% of each run, Pallas kernels for 37% -> 35%
where the time goes in v3:
time: 127 us
  Pallas kernels  45.6 us (36%)
  starting transfers between devices  38 us (30%)
  waiting for transfers between devices  19.7 us (16%)
  between operations  14.2 us (11%)
  local copies, waits for them, and re-layouts  5.93 us (5%)
  other arithmetic  3.42 us (3%)
    pallas_call x1, Pallas kernels, attention(): pl.pallas_call(attention_kernel, out_shape=(jax.ShapeDtypeStruct((NODES,...  16.3 us
    pallas_call x1, Pallas kernels, project(): pl.pallas_call(project_kernel, grid=(H // FEW,), out_shape=(jax.ShapeDtyp...  8.61 us
    all_to_all x1, starting transfers between devices, shards(): lax.all_to_all(sent, 'seq', 0, 0, tiled=True).reshape(NODES, WIDE)  7.96 us
    all_to_all x1, starting transfers between devices, shards(): grad_qkv, grad_out = fold(lax.all_to_all(parts, 'seq', 0, 0, tiled=True))  6.96 us
    pallas_call x1, Pallas kernels, finish(): pl.pallas_call(finish_kernel, grid=(H // STEP,), out_shape=(jax.ShapeDtyp...  6.49 us
    all_to_all x1, starting transfers between devices, shards(): attn = lax.all_to_all(attn_sent, 'seq', 0, 0, tiled=True)  5.96 us
    unnamed x33, local copies, waits for them, and re-layouts  5.93 us
    ppermute x3, waiting for transfers between devices, batches_of(): moved = [lax.ppermute(block, 'dp', chip_shift(step)) for step in (1, 2, 3)]  5.9 us
  transfers between devices with their start and end apart: 14, of which 8 were waited for; matrix products, arithmetic and copies ran while one was open for 3% of the time, Pallas kernels for 35%

profile of v3, /device:TPU:0, one launch (start us, length us, event | category | flops | bytes accessed | tf_op | source)
XLA Modules:
  0.0 126.8 jit_solution(16383024691646068888)
XLA Ops:
  7.2 0.0 all-gather.3.cloned.1.call-start
  7.2 0.7 all-gather.3.cloned.1.call-update
  7.9 0.0 copy-start.1
  7.9 0.0 copy-start.15
  7.9 0.0 copy-start.14
  7.9 8.6 %project.1 = (bf16[16,128,256]{2,1,0:T(8,128)(2,1)}, bf16[128,1024]{1,0:T(8,128)(2,1)}) custom-call(bf16[128,1024]{1,0:T(8,128)(2,1)} %bitcast.19, bf16[128,1024]{1,0:T(8,128)(2,1)} %bitcast.13, bf16[1024,3072]{1,0:T(8,128)(2,1)} %w_qkv_ref.3, bf16[1024,1024]{1,0:T(8,128)(2,1)} %w_out_ref.3), custom_call_target="tpu_custom_call" | custom-call | flops 1073741824 | bytes 9500000 | tf_op jit(solution)/shard_map/project/pallas_call | solution.py:225
  16.5 8.0 %all-to-all-start = ((bf16[16,128,256]{2,1,0:T(8,128)(2,1)}), bf16[16,128,256]{2,1,0:T(8,128)(2,1)S(1)}, u32[]{:S(2)}, u32[]{:S(2)}) async-start(bf16[16,128,256]{2,1,0:T(8,128)(2,1)} %get-tuple-element.18.refs_4_), calls=%async_computation | async-start | bytes 2097152 | tf_op jit(solution)/shard_map/all_to_all | solution.py:464
  24.5 0.0 copy-done.1
  24.5 1.6 %collective-permute-start = (bf16[128,1024]{1,0:T(8,128)(2,1)S(1)}, bf16[128,1024]{1,0:T(8,128)(2,1)S(1)}, u32[]{:S(2)}, u32[]{:S(2)}) collective-permute-start(bf16[128,1024]{1,0:T(8,128)(2,1)S(1)} %bitcast.16), channel_id=1, source_target_pairs={{0,32},{16,48},{32,64},{48,80},{64,96},{80,112},{96,0},{112,16},{1... | collective-permute-start | bytes 786440 | tf_op jit(solution)/shard_map/ppermute | solution.py:390
  26.2 2.9 %collective-permute-start.1 = (bf16[128,1024]{1,0:T(8,128)(2,1)S(1)}, bf16[128,1024]{1,0:T(8,128)(2,1)S(1)}, u32[]{:S(2)}, u32[]{:S(2)}) collective-permute-start(bf16[128,1024]{1,0:T(8,128)(2,1)S(1)} %bitcast.17), channel_id=1, source_target_pairs={{0,64},{16,80},{32,96},{48,112},{64,0},{80,16},{96,32},{112,48},{1... | collective-permute-start | bytes 786440 | tf_op jit(solution)/shard_map/ppermute | solution.py:390
  29.1 1.3 %collective-permute-start.2 = (bf16[128,1024]{1,0:T(8,128)(2,1)S(1)}, bf16[128,1024]{1,0:T(8,128)(2,1)S(1)}, u32[]{:S(2)}, u32[]{:S(2)}) collective-permute-start(bf16[128,1024]{1,0:T(8,128)(2,1)S(1)} %bitcast.18), channel_id=1, source_target_pairs={{0,96},{16,112},{32,0},{48,16},{64,32},{80,48},{96,64},{112,80},{1... | collective-permute-start | bytes 786440 | tf_op jit(solution)/shard_map/ppermute | solution.py:390
  30.4 0.0 copy-done.15
  30.4 0.6 fusion.2
  31.1 1.4 %and_select_fusion = s32[2]{0:T(128)S(1)} fusion(s32[1]{0:T(128)} %bitcast.5, s32[1]{0:T(128)} %bitcast.4), kind=kLoop, calls=%fused_computation.6 | loop fusion | flops 34 | bytes 16 | tf_op jit(solution)/shard_map/jit(floor_divide)/jit(_where)/select_n | solution.py:178
  32.4 0.6 pad_add_fusion.bounds_ref
  33.0 0.0 copy-done.14
  33.0 0.7 copy.13
  33.7 0.2 convert_reduce_fusion
  33.9 0.6 select_reduce_fusion.ranked_ref
  34.5 0.0 collective-permute-done.refs_1_
  34.5 0.0 copy-start.7
  34.5 5.9 %collective-permute-done.1.refs_2_ = bf16[128,1024]{1,0:T(8,128)(2,1)S(1)} collective-permute-done((bf16[128,1024]{1,0:T(8,128)(2,1)S(1)}, bf16[128,1024]{1,0:T(8,128)(2,1)S(1)}, u32[]{:S(2)}, u32[]{:S(2)}) %collective-permute-start.1) | collective-permute-done | bytes 262176 | tf_op jit(solution)/shard_map/ppermute | solution.py:390
  40.4 0.0 copy-start.8
  40.4 0.0 collective-permute-done.2.refs_3_
  40.4 0.0 copy-done.7
  40.4 0.7 copy-done.8
  41.1 0.7 copy-done.9
  41.8 2.3 %stacked.1.after_ref.refs_4_ = bf16[512,1024]{1,0:T(8,128)(2,1)} custom-call(bf16[128,1024]{1,0:T(8,128)(2,1)} %bitcast.14, bf16[128,1024]{1,0:T(8,128)(2,1)} %copy-done.7, bf16[128,1024]{1,0:T(8,128)(2,1)} %copy-done.8, bf16[128,1024]{1,0:T(8,128)(2,1)} %copy-done.9, bf16[16,128,256]{2,1,0:T(8,128)(2,1)} %get-tuple-element.18.refs_4_), custom_call_target="tpu_custom_call" | custom-call | bytes 2097152 | tf_op jit(solution)/shard_map/stacked/pallas_call | solution.py:314
  44.1 0.0 collective-permute-start.8
  44.1 1.0 all-to-all-done
  45.1 1.0 copy-done.4
  46.1 16.3 %clustered_attention.1 = (bf16[2048,256]{1,0:T(8,128)(2,1)}, bf16[16,64,128]{2,1,0:T(8,128)(2,1)}, bf16[16,64,384]{2,1,0:T(8,128)(2,1)}) custom-call(s32[32,8]{1,0:T(8,128)} %bitcast.22, s32[32]{0:T(128)} %bitcast.25, s32[32]{0:T(128)} %select_reduce_fusion.ranked_ref, s32[3]{0:T(128)} %pad_add_fusion.bounds_ref, s32[1,2048]{1,0:T(1,128)} %order_ref.1, ...), custom_call_target="tpu_custom_call" | custom-call | flops 10000000000 | bytes 4000000 | tf_op jit(solution)/shard_map/clustered_attention/pallas_call | solution.py:186
  62.4 6.0 %all-to-all-start.1 = ((bf16[16,64,128]{2,1,0:T(8,128)(2,1)}), bf16[16,64,128]{2,1,0:T(8,128)(2,1)S(1)}, u32[]{:S(2)}, u32[]{:S(2)}) async-start(bf16[16,64,128]{2,1,0:T(8,128)(2,1)} %get-tuple-element.19), calls=%async_computation.1 | async-start | bytes 524288 | tf_op jit(solution)/shard_map/all_to_all | solution.py:467
  68.4 3.0 %all-gather.3.cloned.1.call-done = bf16[1,2048,1024]{2,1,0:T(8,128)(2,1)} async-done(((bf16[1,128,1024]{2,1,0:T(8,128)(2,1)}), bf16[1,2048,1024]{2,1,0:T(8,128)(2,1)}) %all-gather.3.cloned.1.call-update) | async-done | bytes 4194320 | tf_op jit(solution)/shard_map/all_gather | solution.py:462
  71.3 5.1 %weight_qkv.1 = (bf16[8,192,128]{2,1,0:T(8,128)(2,1)}, bf16[16,64,384]{2,1,0:T(8,128)(2,1)}) custom-call(bf16[2048,256]{1,0:T(8,128)(2,1)} %get-tuple-element.20.out_ref, bf16[2048,1024]{1,0:T(8,128)(2,1)} %bitcast.12, bf16[16,64,384]{2,1,0:T(8,128)(2,1)} %get-tuple-element.21.grads_ref), custom_call_target="tpu_custom_call", output_to_operand_aliasing={{1}: (2, {})} | custom-call | flops 805306368 | bytes 6000000 | tf_op jit(solution)/shard_map/weight_qkv/pallas_call | solution.py:340
  76.4 0.5 all-to-all-done.1.attn_ref
  76.9 4.8 %all-to-all-start.2 = ((bf16[16,64,384]{2,1,0:T(8,128)(2,1)}), bf16[16,64,384]{2,1,0:T(8,128)(2,1)S(1)}, u32[]{:S(2)}, u32[]{:S(2)}) async-start(bf16[16,64,384]{2,1,0:T(8,128)(2,1)} %get-tuple-element.22), calls=%async_computation.2 | async-start | bytes 1572864 | tf_op jit(solution)/shard_map/all_to_all | solution.py:470
  81.7 0.3 collective-permute-start.4
  82.0 0.5 collective-permute-start.3
  82.5 1.6 %collective-permute-done.3.other_attn_ref = bf16[16,64,128]{2,1,0:T(8,128)(2,1)S(1)} collective-permute-done((bf16[16,64,128]{2,1,0:T(8,128)(2,1)S(1)}, bf16[16,64,128]{2,1,0:T(8,128)(2,1)S(1)}, u32[]{:S(2)}, u32[]{:S(2)}) %collective-permute-start.3) | collective-permute-done | bytes 262176 | tf_op jit(solution)/shard_map/ppermute | solution.py:381
  84.1 0.0 collective-permute-done.4.other_qkv_ref
  84.1 0.0 copy-done.2
  84.1 0.7 copy-done.10
  84.8 0.7 copy-done.6
  85.5 2.1 %chips.1 = (bf16[448,128]{1,0:T(8,128)(2,1)}, bf16[448,128]{1,0:T(8,128)(2,1)}, bf16[448,128]{1,0:T(8,128)(2,1)}, bf16[448,128]{1,0:T(8,128)(2,1)}) custom-call(bf16[16,64,128]{2,1,0:T(8,128)(2,1)} %copy-done.2, bf16[8,192,128]{2,1,0:T(8,128)(2,1)} %get-tuple-element.25.qkv_ref, bf16[16,64,128]{2,1,0:T(8,128)(2,1)} %copy-done.10, bf16[8,192,128]{2,1,0:T(8,128)(2,1)} %copy-done.6), custom_call_target="tpu_custom_call" | custom-call | bytes 2000000 | tf_op jit(solution)/shard_map/chips/pallas_call | solution.py:373
  87.6 1.5 %collective-permute-start.5 = (bf16[448,128]{1,0:T(8,128)(2,1)}, bf16[448,128]{1,0:T(8,128)(2,1)S(1)}, u32[]{:S(2)}, u32[]{:S(2)}) collective-permute-start(bf16[448,128]{1,0:T(8,128)(2,1)} %get-tuple-element.27), channel_id=1, source_target_pairs={{0,32},{16,48},{32,64},{48,80},{64,96},{80,112},{96,0},{112,16},{1... | collective-permute-start | bytes 344072 | tf_op jit(solution)/shard_map/ppermute | solution.py:382
  89.1 3.1 %collective-permute-start.6 = (bf16[448,128]{1,0:T(8,128)(2,1)}, bf16[448,128]{1,0:T(8,128)(2,1)S(1)}, u32[]{:S(2)}, u32[]{:S(2)}) collective-permute-start(bf16[448,128]{1,0:T(8,128)(2,1)} %get-tuple-element.28), channel_id=1, source_target_pairs={{0,64},{16,80},{32,96},{48,112},{64,0},{80,16},{96,32},{112,48},{1... | collective-permute-start | bytes 344072 | tf_op jit(solution)/shard_map/ppermute | solution.py:382
  92.2 1.1 collective-permute-start.7
  93.2 0.0 collective-permute-done.8.refs_5_
  93.2 1.1 collective-permute-done.5.refs_1_
  94.4 3.6 %collective-permute-done.6.refs_2_ = bf16[448,128]{1,0:T(8,128)(2,1)S(1)} collective-permute-done((bf16[448,128]{1,0:T(8,128)(2,1)}, bf16[448,128]{1,0:T(8,128)(2,1)S(1)}, u32[]{:S(2)}, u32[]{:S(2)}) %collective-permute-start.6) | collective-permute-done | bytes 114720 | tf_op jit(solution)/shard_map/ppermute | solution.py:382
  98.0 0.0 collective-permute-done.7.refs_3_
  98.0 0.0 copy-done.5
  98.0 0.0 copy-done.11
  98.0 0.6 copy-done.12
  98.7 0.0 copy-done.13
  98.7 3.1 %weight_out.1 = bf16[16,16,640]{2,1,0:T(8,128)(2,1)} custom-call(bf16[448,128]{1,0:T(8,128)(2,1)} %get-tuple-element.26.refs_0_, bf16[448,128]{1,0:T(8,128)(2,1)} %copy-done.11, bf16[448,128]{1,0:T(8,128)(2,1)} %copy-done.12, bf16[448,128]{1,0:T(8,128)(2,1)} %copy-done.13, bf16[512,1024]{1,0:T(8,128)(2,1)} %stacked.1.after_ref.refs_4_, ...), custom_call_target="tpu_custom_call" | custom-call | flops 268435456 | bytes 3000000 | tf_op jit(solution)/shard_map/weight_out/pallas_call | solution.py:424
  101.8 0.0 all-to-all-done.2.grads_ref
  101.8 7.0 %all-to-all-start.3 = ((bf16[16,16,640]{2,1,0:T(8,128)(2,1)}), bf16[16,16,640]{2,1,0:T(8,128)(2,1)S(1)}, u32[]{:S(2)}, u32[]{:S(2)}) async-start(bf16[16,16,640]{2,1,0:T(8,128)(2,1)} %weight_out.1), calls=%async_computation.3 | async-start | bytes 655360 | tf_op jit(solution)/shard_map/all_to_all | solution.py:472
  108.7 0.0 copy-done
  108.8 6.5 %finish.1 = (bf16[128,1024]{1,0:T(8,128)(2,1)}, bf16[128,1024]{1,0:T(8,128)(2,1)}) custom-call(bf16[128,1024]{1,0:T(8,128)(2,1)} %bitcast.20, bf16[128,1024]{1,0:T(8,128)(2,1)} %bitcast.15, bf16[16,64,128]{2,1,0:T(8,128)(2,1)} %copy-done.2, bf16[16,64,384]{2,1,0:T(8,128)(2,1)} %copy-done, bf16[1024,3072]{1,0:T(8,128)(2,1)} %w_qkv_ref.3, ...), custom_call_target="tpu_custom_call" | custom-call | flops 1073741824 | bytes 10000000 | tf_op jit(solution)/shard_map/finish/pallas_call | solution.py:284
  115.2 2.3 %all-to-all-done.3.parts_ref = bf16[16,16,640]{2,1,0:T(8,128)(2,1)S(1)} async-done(((bf16[16,16,640]{2,1,0:T(8,128)(2,1)}), bf16[16,16,640]{2,1,0:T(8,128)(2,1)S(1)}, u32[]{:S(2)}, u32[]{:S(2)}) %all-to-all-start.3) | async-done | bytes 327712 | tf_op jit(solution)/shard_map/all_to_all | solution.py:472
  117.6 0.7 copy-done.3
  118.3 1.7 %fold.1 = (f32[8,3072]{1,0:T(8,128)}, f32[8,1024]{1,0:T(8,128)}) custom-call(bf16[16,16,640]{2,1,0:T(8,128)(2,1)} %copy-done.3), custom_call_target="tpu_custom_call" | custom-call | tf_op jit(solution)/shard_map/fold/pallas_call | solution.py:448
  (11 shorter events, 0.0 us)
Async XLA Ops:
  7.2 64.2 %all-gather.3.cloned.1.call-start = ((), (), s32[]{:S(2)}) async-start(), calls=%async_computation.4 | async-start | bytes 4456448 | tf_op jit(solution)/shard_map/all_gather | solution.py:462
  7.9 16.6 %copy-start.1 = (bf16[1,128,1024]{2,1,0:T(8,128)(2,1)S(1)}, bf16[1,128,1024]{2,1,0:T(8,128)(2,1)}, u32[]{:S(2)}) copy-start(bf16[1,128,1024]{2,1,0:T(8,128)(2,1)} %param.10) | copy-start | bytes 786436
  7.9 22.5 %copy-start.15 = (s32[1,32]{1,0:T(1,128)S(1)}, s32[1,32]{1,0:T(1,128)}, u32[]{:S(2)}) copy-start(s32[1,32]{1,0:T(1,128)} %param.13) | copy-start | bytes 388
  7.9 25.1 %copy-start.14 = (s32[1,32,8]{1,2,0:T(8,128)S(1)}, s32[1,32,8]{1,2,0:T(8,128)}, u32[]{:S(2)}) copy-start(s32[1,32,8]{1,2,0:T(8,128)} %param.12) | copy-start | bytes 3076
  16.5 28.6 %all-to-all-start = ((bf16[16,128,256]{2,1,0:T(8,128)(2,1)}), bf16[16,128,256]{2,1,0:T(8,128)(2,1)S(1)}, u32[]{:S(2)}, u32[]{:S(2)}) async-start(bf16[16,128,256]{2,1,0:T(8,128)(2,1)} %get-tuple-element.18.refs_4_), calls=%async_computation | async-start | bytes 2097152 | tf_op jit(solution)/shard_map/all_to_all | solution.py:464
  24.5 10.0 %collective-permute-start = (bf16[128,1024]{1,0:T(8,128)(2,1)S(1)}, bf16[128,1024]{1,0:T(8,128)(2,1)S(1)}, u32[]{:S(2)}, u32[]{:S(2)}) collective-permute-start(bf16[128,1024]{1,0:T(8,128)(2,1)S(1)} %bitcast.16), channel_id=1, source_target_pairs={{0,32},{16,48},{32,64},{48,80},{64,96},{80,112},{96,0},{112,16},{1... | collective-permute-start | bytes 786440 | tf_op jit(solution)/shard_map/ppermute | solution.py:390
  26.2 14.3 %collective-permute-start.1 = (bf16[128,1024]{1,0:T(8,128)(2,1)S(1)}, bf16[128,1024]{1,0:T(8,128)(2,1)S(1)}, u32[]{:S(2)}, u32[]{:S(2)}) collective-permute-start(bf16[128,1024]{1,0:T(8,128)(2,1)S(1)} %bitcast.17), channel_id=1, source_target_pairs={{0,64},{16,80},{32,96},{48,112},{64,0},{80,16},{96,32},{112,48},{1... | collective-permute-start | bytes 786440 | tf_op jit(solution)/shard_map/ppermute | solution.py:390
  29.1 11.4 %collective-permute-start.2 = (bf16[128,1024]{1,0:T(8,128)(2,1)S(1)}, bf16[128,1024]{1,0:T(8,128)(2,1)S(1)}, u32[]{:S(2)}, u32[]{:S(2)}) collective-permute-start(bf16[128,1024]{1,0:T(8,128)(2,1)S(1)} %bitcast.18), channel_id=1, source_target_pairs={{0,96},{16,112},{32,0},{48,16},{64,32},{80,48},{96,64},{112,80},{1... | collective-permute-start | bytes 786440 | tf_op jit(solution)/shard_map/ppermute | solution.py:390
  34.5 5.9 %copy-start.7 = (bf16[128,1024]{1,0:T(8,128)(2,1)}, bf16[128,1024]{1,0:T(8,128)(2,1)S(1)}, u32[]{:S(2)}) copy-start(bf16[128,1024]{1,0:T(8,128)(2,1)S(1)} %collective-permute-done.refs_1_) | copy-start | bytes 786436
  40.4 0.7 copy-start.8
  41.1 0.7 copy-start.9
  44.1 49.1 %collective-permute-start.8 = (bf16[512,1024]{1,0:T(8,128)(2,1)}, bf16[512,1024]{1,0:T(8,128)(2,1)S(1)}, u32[]{:S(2)}, u32[]{:S(2)}) collective-permute-start(bf16[512,1024]{1,0:T(8,128)(2,1)} %stacked.1.after_ref.refs_4_), channel_id=1, source_target_pairs={{0,16},{16,0},{32,48},{48,32},{64,80},{80,64},{96,112},{112,96},{1... | collective-permute-start | bytes 3145736 | tf_op jit(solution)/shard_map/ppermute | solution.py:392
  45.1 1.0 copy-start.4
  62.4 14.5 %all-to-all-start.1 = ((bf16[16,64,128]{2,1,0:T(8,128)(2,1)}), bf16[16,64,128]{2,1,0:T(8,128)(2,1)S(1)}, u32[]{:S(2)}, u32[]{:S(2)}) async-start(bf16[16,64,128]{2,1,0:T(8,128)(2,1)} %get-tuple-element.19), calls=%async_computation.1 | async-start | bytes 524288 | tf_op jit(solution)/shard_map/all_to_all | solution.py:467
  76.9 7.2 %copy-start.2 = (bf16[16,64,128]{2,1,0:T(8,128)(2,1)}, bf16[16,64,128]{2,1,0:T(8,128)(2,1)S(1)}, u32[]{:S(2)}) copy-start(bf16[16,64,128]{2,1,0:T(8,128)(2,1)S(1)} %all-to-all-done.1.attn_ref) | copy-start | bytes 786436
  76.9 24.9 %all-to-all-start.2 = ((bf16[16,64,384]{2,1,0:T(8,128)(2,1)}), bf16[16,64,384]{2,1,0:T(8,128)(2,1)S(1)}, u32[]{:S(2)}, u32[]{:S(2)}) async-start(bf16[16,64,384]{2,1,0:T(8,128)(2,1)} %get-tuple-element.22), calls=%async_computation.2 | async-start | bytes 1572864 | tf_op jit(solution)/shard_map/all_to_all | solution.py:470
  81.7 2.4 %collective-permute-start.4 = (bf16[8,192,128]{2,1,0:T(8,128)(2,1)}, bf16[8,192,128]{2,1,0:T(8,128)(2,1)S(1)}, u32[]{:S(2)}, u32[]{:S(2)}) collective-permute-start(bf16[8,192,128]{2,1,0:T(8,128)(2,1)} %get-tuple-element.25.qkv_ref), channel_id=1, source_target_pairs={{0,16},{16,0},{32,48},{48,32},{64,80},{80,64},{96,112},{112,96},{1... | collective-permute-start | bytes 1179656 | tf_op jit(solution)/shard_map/ppermute | solution.py:381
  82.0 2.1 %collective-permute-start.3 = (bf16[16,64,128]{2,1,0:T(8,128)(2,1)S(1)}, bf16[16,64,128]{2,1,0:T(8,128)(2,1)S(1)}, u32[]{:S(2)}, u32[]{:S(2)}) collective-permute-start(bf16[16,64,128]{2,1,0:T(8,128)(2,1)S(1)} %all-to-all-done.1.attn_ref), channel_id=1, source_target_pairs={{0,16},{16,0},{32,48},{48,32},{64,80},{80,64},{96,112},{112,96},{1... | collective-permute-start | bytes 786440 | tf_op jit(solution)/shard_map/ppermute | solution.py:381
  84.1 0.7 copy-start.10
  84.8 0.8 copy-start.6
  87.6 6.8 %collective-permute-start.5 = (bf16[448,128]{1,0:T(8,128)(2,1)}, bf16[448,128]{1,0:T(8,128)(2,1)S(1)}, u32[]{:S(2)}, u32[]{:S(2)}) collective-permute-start(bf16[448,128]{1,0:T(8,128)(2,1)} %get-tuple-element.27), channel_id=1, source_target_pairs={{0,32},{16,48},{32,64},{48,80},{64,96},{80,112},{96,0},{112,16},{1... | collective-permute-start | bytes 344072 | tf_op jit(solution)/shard_map/ppermute | solution.py:382
  89.1 8.9 %collective-permute-start.6 = (bf16[448,128]{1,0:T(8,128)(2,1)}, bf16[448,128]{1,0:T(8,128)(2,1)S(1)}, u32[]{:S(2)}, u32[]{:S(2)}) collective-permute-start(bf16[448,128]{1,0:T(8,128)(2,1)} %get-tuple-element.28), channel_id=1, source_target_pairs={{0,64},{16,80},{32,96},{48,112},{64,0},{80,16},{96,32},{112,48},{1... | collective-permute-start | bytes 344072 | tf_op jit(solution)/shard_map/ppermute | solution.py:382
  92.2 5.8 %collective-permute-start.7 = (bf16[448,128]{1,0:T(8,128)(2,1)}, bf16[448,128]{1,0:T(8,128)(2,1)S(1)}, u32[]{:S(2)}, u32[]{:S(2)}) collective-permute-start(bf16[448,128]{1,0:T(8,128)(2,1)} %get-tuple-element.29), channel_id=1, source_target_pairs={{0,96},{16,112},{32,0},{48,16},{64,32},{80,48},{96,64},{112,80},{1... | collective-permute-start | bytes 344072 | tf_op jit(solution)/shard_map/ppermute | solution.py:382
  93.2 4.8 %copy-start.5 = (bf16[512,1024]{1,0:T(8,128)(2,1)}, bf16[512,1024]{1,0:T(8,128)(2,1)S(1)}, u32[]{:S(2)}) copy-start(bf16[512,1024]{1,0:T(8,128)(2,1)S(1)} %collective-permute-done.8.refs_5_) | copy-start | bytes 3145732
  94.4 3.7 %copy-start.11 = (bf16[448,128]{1,0:T(8,128)(2,1)}, bf16[448,128]{1,0:T(8,128)(2,1)S(1)}, u32[]{:S(2)}) copy-start(bf16[448,128]{1,0:T(8,128)(2,1)S(1)} %collective-permute-done.5.refs_1_) | copy-start | bytes 344068
  98.0 0.7 copy-start.12
  98.0 0.7 copy-start.13
  101.8 7.0 %copy-start = (bf16[16,64,384]{2,1,0:T(8,128)(2,1)}, bf16[16,64,384]{2,1,0:T(8,128)(2,1)S(1)}, u32[]{:S(2)}) copy-start(bf16[16,64,384]{2,1,0:T(8,128)(2,1)S(1)} %all-to-all-done.2.grads_ref) | copy-start | bytes 2359300
  101.8 15.8 %all-to-all-start.3 = ((bf16[16,16,640]{2,1,0:T(8,128)(2,1)}), bf16[16,16,640]{2,1,0:T(8,128)(2,1)S(1)}, u32[]{:S(2)}, u32[]{:S(2)}) async-start(bf16[16,16,640]{2,1,0:T(8,128)(2,1)} %weight_out.1), calls=%async_computation.3 | async-start | bytes 655360 | tf_op jit(solution)/shard_map/all_to_all | solution.py:472
  117.6 0.7 copy-start.3
Sparse Core Ops, SparseCore 0:
  10.1 61.1 all-gather.2

commit v4 on v3

--- a/solution.py
+++ b/solution.py
@@ -225,17 +225,15 @@
     return pl.pallas_call(
         project_kernel,
         grid=(H // FEW,),
-        out_shape=(
-            jax.ShapeDtypeStruct((H, ROWS, WIDE), jnp.bfloat16),
-            jax.ShapeDtypeStruct((ROWS, D), jnp.bfloat16),
-        ),
+        out_shape=jax.ShapeDtypeStruct((H, ROWS, WIDE), jnp.bfloat16),
         in_specs=[
             whole,
             whole,
             pl.BlockSpec((D, 3 * FEW * HD), lambda i: (0, i)),
             pl.BlockSpec((FEW * HD, D), lambda i: (i, 0)),
         ],
-        out_specs=(pl.BlockSpec((FEW, ROWS, WIDE), lambda i: (i, 0, 0)), whole),
+        out_specs=pl.BlockSpec((FEW, ROWS, WIDE), lambda i: (i, 0, 0)),
+        scratch_shapes=[pltpu.VMEM((ROWS, D), jnp.bfloat16)],
         compiler_params=pltpu.CompilerParams(vmem_limit_bytes=VMEM_BYTES),
         cost_estimate=pl.CostEstimate(flops=2 * ROWS * D * 4 * D, bytes_accessed=9_500_000, transcendentals=ROWS),
         name="project",
@@ -379,7 +377,8 @@
         cost_estimate=pl.CostEstimate(flops=0, bytes_accessed=2_000_000, transcendentals=0),
         name="chips",
     )(attn, part_qkv, lax.ppermute(attn, "dp", pairs), lax.ppermute(part_qkv, "dp", pairs))
-    return parts[0], *(lax.ppermute(parts[step], "dp", chip_shift(step)) for step in (1, 2, 3))
+    moved = {step: lax.ppermute(parts[step], "dp", chip_shift(step)) for step in (2, 1, 3)}
+    return parts[0], moved[2], moved[1], moved[3]
 
 
 def chip_shift(step):
@@ -393,7 +392,7 @@
 
 
 def weight_out_kernel(*refs):
-    parts, (mine_ref, other_ref, sent_ref) = refs[:CHIPS], refs[CHIPS:]
+    parts, (mine_ref, other_ref, sent_ref) = (refs[0], refs[2], refs[1], refs[3]), refs[CHIPS:]
     core = lax.axis_index("dp") % CORES
     total, mine, other = None, [], []
     for ref in parts:
@@ -460,7 +459,7 @@
 def shards(nodes, w_qkv, w_out, cotangent, order, block_list, block_count):
     features, upstream = nodes[0], cotangent[0]
     all_nodes = lax.all_gather(features, "seq", axis=0, tiled=True)
-    sent, _ = project(features, upstream, w_qkv, w_out)
+    sent = project(features, upstream, w_qkv, w_out)
     head_rows = lax.all_to_all(sent, "seq", 0, 0, tiled=True).reshape(NODES, WIDE)
     upstreams = batches_of(upstream, sent)
     head_out, attn_sent, grads_sent = attention(block_list[0], block_count[0], order, head_rows, upstreams[0])

time: 127 us -> 127 us (level)
    ppermute x3, waiting for transfers between devices: 4.76 us -> 3.42 us  [over_dp(): lax.ppermute(parts[step], 'dp', chip_shift(step))]
where the time goes in v4:
time: 127 us; the launch traced here: 126 us
  Pallas kernels  45.3 us (36%)
  starting transfers between devices  38.3 us (30%)
  waiting for transfers between devices  19 us (15%)
  between operations  14.2 us (11%)
  local copies, waits for them, and re-layouts  5.94 us (5%)
  other arithmetic  3.4 us (3%)
    pallas_call x1, Pallas kernels, attention(): pl.pallas_call(attention_kernel, out_shape=(jax.ShapeDtypeStruct((NODES,...  16 us
    pallas_call x1, Pallas kernels, project(): pl.pallas_call(project_kernel, grid=(H // FEW,), out_shape=jax.ShapeDtype...  8.62 us
    all_to_all x1, starting transfers between devices, shards(): lax.all_to_all(sent, 'seq', 0, 0, tiled=True).reshape(NODES, WIDE)  7.96 us
    all_to_all x1, starting transfers between devices, shards(): grad_qkv, grad_out = fold(lax.all_to_all(parts, 'seq', 0, 0, tiled=True))  6.96 us
    pallas_call x1, Pallas kernels, finish(): pl.pallas_call(finish_kernel, grid=(H // STEP,), out_shape=(jax.ShapeDtyp...  6.49 us
    ppermute x3, starting transfers between devices, over_dp(): lax.ppermute(parts[step], 'dp', chip_shift(step))  6.25 us
    all_to_all x1, starting transfers between devices, shards(): attn = lax.all_to_all(attn_sent, 'seq', 0, 0, tiled=True)  5.95 us
    unnamed x33, local copies, waits for them, and re-layouts  5.94 us
  transfers between devices with their start and end apart: 14, of which 8 were waited for; matrix products, arithmetic and copies ran while one was open for 3% of the time, Pallas kernels for 35%

profile of v4, /device:TPU:0, one launch (start us, length us, event | category | flops | bytes accessed | tf_op | source)
XLA Modules:
  0.0 126.1 jit_solution(9847560289108379292)
XLA Ops:
  7.2 0.0 all-gather.3.cloned.1.call-start
  7.2 0.7 all-gather.3.cloned.1.call-update
  7.9 0.0 copy-start.1
  7.9 0.0 copy-start.15
  7.9 0.0 copy-start.14
  7.9 8.6 %project.1.refs_4_ = bf16[16,128,256]{2,1,0:T(8,128)(2,1)} custom-call(bf16[128,1024]{1,0:T(8,128)(2,1)} %bitcast.19, bf16[128,1024]{1,0:T(8,128)(2,1)} %bitcast.13, bf16[1024,3072]{1,0:T(8,128)(2,1)} %w_qkv_ref.3, bf16[1024,1024]{1,0:T(8,128)(2,1)} %w_out_ref.3), custom_call_target="tpu_custom_call" | custom-call | flops 1073741824 | bytes 9500000 | tf_op jit(solution)/shard_map/project/pallas_call | solution.py:225
  16.6 8.0 %all-to-all-start = ((bf16[16,128,256]{2,1,0:T(8,128)(2,1)}), bf16[16,128,256]{2,1,0:T(8,128)(2,1)S(1)}, u32[]{:S(2)}, u32[]{:S(2)}) async-start(bf16[16,128,256]{2,1,0:T(8,128)(2,1)} %project.1.refs_4_), calls=%async_computation | async-start | bytes 2097152 | tf_op jit(solution)/shard_map/all_to_all | solution.py:463
  24.5 0.0 copy-done.1
  24.5 1.6 %collective-permute-start = (bf16[128,1024]{1,0:T(8,128)(2,1)S(1)}, bf16[128,1024]{1,0:T(8,128)(2,1)S(1)}, u32[]{:S(2)}, u32[]{:S(2)}) collective-permute-start(bf16[128,1024]{1,0:T(8,128)(2,1)S(1)} %bitcast.16), channel_id=1, source_target_pairs={{0,32},{16,48},{32,64},{48,80},{64,96},{80,112},{96,0},{112,16},{1... | collective-permute-start | bytes 786440 | tf_op jit(solution)/shard_map/ppermute | solution.py:389
  26.2 2.9 %collective-permute-start.1 = (bf16[128,1024]{1,0:T(8,128)(2,1)S(1)}, bf16[128,1024]{1,0:T(8,128)(2,1)S(1)}, u32[]{:S(2)}, u32[]{:S(2)}) collective-permute-start(bf16[128,1024]{1,0:T(8,128)(2,1)S(1)} %bitcast.17), channel_id=1, source_target_pairs={{0,64},{16,80},{32,96},{48,112},{64,0},{80,16},{96,32},{112,48},{1... | collective-permute-start | bytes 786440 | tf_op jit(solution)/shard_map/ppermute | solution.py:389
  29.1 1.3 %collective-permute-start.2 = (bf16[128,1024]{1,0:T(8,128)(2,1)S(1)}, bf16[128,1024]{1,0:T(8,128)(2,1)S(1)}, u32[]{:S(2)}, u32[]{:S(2)}) collective-permute-start(bf16[128,1024]{1,0:T(8,128)(2,1)S(1)} %bitcast.18), channel_id=1, source_target_pairs={{0,96},{16,112},{32,0},{48,16},{64,32},{80,48},{96,64},{112,80},{1... | collective-permute-start | bytes 786440 | tf_op jit(solution)/shard_map/ppermute | solution.py:389
  30.4 0.0 copy-done.15
  30.4 0.6 fusion.2
  31.1 1.4 %and_select_fusion = s32[2]{0:T(128)S(1)} fusion(s32[1]{0:T(128)} %bitcast.5, s32[1]{0:T(128)} %bitcast.4), kind=kLoop, calls=%fused_computation.6 | loop fusion | flops 34 | bytes 16 | tf_op jit(solution)/shard_map/jit(floor_divide)/jit(_where)/select_n | solution.py:178
  32.4 0.6 pad_add_fusion.bounds_ref
  33.0 0.0 copy-done.14
  33.0 0.7 copy.13
  33.7 0.2 convert_reduce_fusion
  33.9 0.6 select_reduce_fusion.ranked_ref
  34.5 0.0 collective-permute-done.refs_1_
  34.5 0.0 copy-start.7
  34.5 5.9 %collective-permute-done.1.refs_2_ = bf16[128,1024]{1,0:T(8,128)(2,1)S(1)} collective-permute-done((bf16[128,1024]{1,0:T(8,128)(2,1)S(1)}, bf16[128,1024]{1,0:T(8,128)(2,1)S(1)}, u32[]{:S(2)}, u32[]{:S(2)}) %collective-permute-start.1) | collective-permute-done | bytes 262176 | tf_op jit(solution)/shard_map/ppermute | solution.py:389
  40.4 0.0 copy-start.8
  40.4 0.0 collective-permute-done.2.refs_3_
  40.4 0.0 copy-done.7
  40.5 0.7 copy-done.8
  41.1 0.7 copy-done.9
  41.8 2.3 %stacked.1.after_ref.refs_4_ = bf16[512,1024]{1,0:T(8,128)(2,1)} custom-call(bf16[128,1024]{1,0:T(8,128)(2,1)} %bitcast.14, bf16[128,1024]{1,0:T(8,128)(2,1)} %copy-done.7, bf16[128,1024]{1,0:T(8,128)(2,1)} %copy-done.8, bf16[128,1024]{1,0:T(8,128)(2,1)} %copy-done.9, bf16[16,128,256]{2,1,0:T(8,128)(2,1)} %project.1.refs_4_), custom_call_target="tpu_custom_call" | custom-call | bytes 2097152 | tf_op jit(solution)/shard_map/stacked/pallas_call | solution.py:312
  44.1 0.0 collective-permute-start.8
  44.1 1.0 all-to-all-done
  45.1 1.0 copy-done.4
  46.1 16.0 %clustered_attention.1 = (bf16[2048,256]{1,0:T(8,128)(2,1)}, bf16[16,64,128]{2,1,0:T(8,128)(2,1)}, bf16[16,64,384]{2,1,0:T(8,128)(2,1)}) custom-call(s32[32,8]{1,0:T(8,128)} %bitcast.22, s32[32]{0:T(128)} %bitcast.25, s32[32]{0:T(128)} %select_reduce_fusion.ranked_ref, s32[3]{0:T(128)} %pad_add_fusion.bounds_ref, s32[1,2048]{1,0:T(1,128)} %order_ref.1, ...), custom_call_target="tpu_custom_call" | custom-call | flops 10000000000 | bytes 4000000 | tf_op jit(solution)/shard_map/clustered_attention/pallas_call | solution.py:186
  62.1 5.9 %all-to-all-start.1 = ((bf16[16,64,128]{2,1,0:T(8,128)(2,1)}), bf16[16,64,128]{2,1,0:T(8,128)(2,1)S(1)}, u32[]{:S(2)}, u32[]{:S(2)}) async-start(bf16[16,64,128]{2,1,0:T(8,128)(2,1)} %get-tuple-element.17), calls=%async_computation.1 | async-start | bytes 524288 | tf_op jit(solution)/shard_map/all_to_all | solution.py:466
  68.0 3.3 %all-gather.3.cloned.1.call-done = bf16[1,2048,1024]{2,1,0:T(8,128)(2,1)} async-done(((bf16[1,128,1024]{2,1,0:T(8,128)(2,1)}), bf16[1,2048,1024]{2,1,0:T(8,128)(2,1)}) %all-gather.3.cloned.1.call-update) | async-done | bytes 4194320 | tf_op jit(solution)/shard_map/all_gather | solution.py:461
  71.3 5.1 %weight_qkv.1 = (bf16[8,192,128]{2,1,0:T(8,128)(2,1)}, bf16[16,64,384]{2,1,0:T(8,128)(2,1)}) custom-call(bf16[2048,256]{1,0:T(8,128)(2,1)} %get-tuple-element.18.out_ref, bf16[2048,1024]{1,0:T(8,128)(2,1)} %bitcast.12, bf16[16,64,384]{2,1,0:T(8,128)(2,1)} %get-tuple-element.19.grads_ref), custom_call_target="tpu_custom_call", output_to_operand_aliasing={{1}: (2, {})} | custom-call | flops 805306368 | bytes 6000000 | tf_op jit(solution)/shard_map/weight_qkv/pallas_call | solution.py:338
  76.4 0.7 all-to-all-done.1.attn_ref
  77.2 4.5 %all-to-all-start.2 = ((bf16[16,64,384]{2,1,0:T(8,128)(2,1)}), bf16[16,64,384]{2,1,0:T(8,128)(2,1)S(1)}, u32[]{:S(2)}, u32[]{:S(2)}) async-start(bf16[16,64,384]{2,1,0:T(8,128)(2,1)} %get-tuple-element.20), calls=%async_computation.2 | async-start | bytes 1572864 | tf_op jit(solution)/shard_map/all_to_all | solution.py:469
  81.7 0.3 collective-permute-start.4
  82.0 0.5 collective-permute-start.3
  82.5 1.6 %collective-permute-done.3.other_attn_ref = bf16[16,64,128]{2,1,0:T(8,128)(2,1)S(1)} collective-permute-done((bf16[16,64,128]{2,1,0:T(8,128)(2,1)S(1)}, bf16[16,64,128]{2,1,0:T(8,128)(2,1)S(1)}, u32[]{:S(2)}, u32[]{:S(2)}) %collective-permute-start.3) | collective-permute-done | bytes 262176 | tf_op jit(solution)/shard_map/ppermute | solution.py:379
  84.1 0.0 collective-permute-done.4.other_qkv_ref
  84.1 0.0 copy-done.2
  84.1 0.7 copy-done.10
  84.8 0.8 copy-done.6
  85.5 2.1 %chips.1 = (bf16[448,128]{1,0:T(8,128)(2,1)}, bf16[448,128]{1,0:T(8,128)(2,1)}, bf16[448,128]{1,0:T(8,128)(2,1)}, bf16[448,128]{1,0:T(8,128)(2,1)}) custom-call(bf16[16,64,128]{2,1,0:T(8,128)(2,1)} %copy-done.2, bf16[8,192,128]{2,1,0:T(8,128)(2,1)} %get-tuple-element.23.qkv_ref, bf16[16,64,128]{2,1,0:T(8,128)(2,1)} %copy-done.10, bf16[8,192,128]{2,1,0:T(8,128)(2,1)} %copy-done.6), custom_call_target="tpu_custom_call" | custom-call | bytes 2000000 | tf_op jit(solution)/shard_map/chips/pallas_call | solution.py:371
  87.6 3.0 %collective-permute-start.5 = (bf16[448,128]{1,0:T(8,128)(2,1)}, bf16[448,128]{1,0:T(8,128)(2,1)S(1)}, u32[]{:S(2)}, u32[]{:S(2)}) collective-permute-start(bf16[448,128]{1,0:T(8,128)(2,1)} %get-tuple-element.25), channel_id=1, source_target_pairs={{0,64},{16,80},{32,96},{48,112},{64,0},{80,16},{96,32},{112,48},{1... | collective-permute-start | bytes 344072 | tf_op jit(solution)/shard_map/ppermute | solution.py:380
  90.6 0.6 collective-permute-start.6
  91.2 2.7 %collective-permute-start.7 = (bf16[448,128]{1,0:T(8,128)(2,1)}, bf16[448,128]{1,0:T(8,128)(2,1)S(1)}, u32[]{:S(2)}, u32[]{:S(2)}) collective-permute-start(bf16[448,128]{1,0:T(8,128)(2,1)} %get-tuple-element.27), channel_id=1, source_target_pairs={{0,96},{16,112},{32,0},{48,16},{64,32},{80,48},{96,64},{112,80},{1... | collective-permute-start | bytes 344072 | tf_op jit(solution)/shard_map/ppermute | solution.py:380
  93.9 0.0 collective-permute-done.8.refs_5_
  93.9 1.3 %collective-permute-done.5.refs_1_ = bf16[448,128]{1,0:T(8,128)(2,1)S(1)} collective-permute-done((bf16[448,128]{1,0:T(8,128)(2,1)}, bf16[448,128]{1,0:T(8,128)(2,1)S(1)}, u32[]{:S(2)}, u32[]{:S(2)}) %collective-permute-start.5) | collective-permute-done | bytes 114720 | tf_op jit(solution)/shard_map/ppermute | solution.py:380
  95.2 2.1 %collective-permute-done.6.refs_2_ = bf16[448,128]{1,0:T(8,128)(2,1)S(1)} collective-permute-done((bf16[448,128]{1,0:T(8,128)(2,1)}, bf16[448,128]{1,0:T(8,128)(2,1)S(1)}, u32[]{:S(2)}, u32[]{:S(2)}) %collective-permute-start.6) | collective-permute-done | bytes 114720 | tf_op jit(solution)/shard_map/ppermute | solution.py:380
  97.3 0.0 collective-permute-done.7.refs_3_
  97.3 0.0 copy-done.5
  97.3 0.0 copy-done.11
  97.3 0.6 copy-done.12
  97.9 0.1 copy-done.13
  98.0 3.1 %weight_out.1 = bf16[16,16,640]{2,1,0:T(8,128)(2,1)} custom-call(bf16[448,128]{1,0:T(8,128)(2,1)} %get-tuple-element.24.refs_0_, bf16[448,128]{1,0:T(8,128)(2,1)} %copy-done.11, bf16[448,128]{1,0:T(8,128)(2,1)} %copy-done.12, bf16[448,128]{1,0:T(8,128)(2,1)} %copy-done.13, bf16[512,1024]{1,0:T(8,128)(2,1)} %stacked.1.after_ref.refs_4_, ...), custom_call_target="tpu_custom_call" | custom-call | flops 268435456 | bytes 3000000 | tf_op jit(solution)/shard_map/weight_out/pallas_call | solution.py:423
  101.1 0.0 all-to-all-done.2.grads_ref
  101.1 7.0 %all-to-all-start.3 = ((bf16[16,16,640]{2,1,0:T(8,128)(2,1)}), bf16[16,16,640]{2,1,0:T(8,128)(2,1)S(1)}, u32[]{:S(2)}, u32[]{:S(2)}) async-start(bf16[16,16,640]{2,1,0:T(8,128)(2,1)} %weight_out.1), calls=%async_computation.3 | async-start | bytes 655360 | tf_op jit(solution)/shard_map/all_to_all | solution.py:471
  108.0 0.0 copy-done
  108.0 6.5 %finish.1 = (bf16[128,1024]{1,0:T(8,128)(2,1)}, bf16[128,1024]{1,0:T(8,128)(2,1)}) custom-call(bf16[128,1024]{1,0:T(8,128)(2,1)} %bitcast.20, bf16[128,1024]{1,0:T(8,128)(2,1)} %bitcast.15, bf16[16,64,128]{2,1,0:T(8,128)(2,1)} %copy-done.2, bf16[16,64,384]{2,1,0:T(8,128)(2,1)} %copy-done, bf16[1024,3072]{1,0:T(8,128)(2,1)} %w_qkv_ref.3, ...), custom_call_target="tpu_custom_call" | custom-call | flops 1073741824 | bytes 10000000 | tf_op jit(solution)/shard_map/finish/pallas_call | solution.py:282
  114.5 2.3 %all-to-all-done.3.parts_ref = bf16[16,16,640]{2,1,0:T(8,128)(2,1)S(1)} async-done(((bf16[16,16,640]{2,1,0:T(8,128)(2,1)}), bf16[16,16,640]{2,1,0:T(8,128)(2,1)S(1)}, u32[]{:S(2)}, u32[]{:S(2)}) %all-to-all-start.3) | async-done | bytes 327712 | tf_op jit(solution)/shard_map/all_to_all | solution.py:471
  116.9 0.7 copy-done.3
  117.6 1.7 %fold.1 = (f32[8,3072]{1,0:T(8,128)}, f32[8,1024]{1,0:T(8,128)}) custom-call(bf16[16,16,640]{2,1,0:T(8,128)(2,1)} %copy-done.3), custom_call_target="tpu_custom_call" | custom-call | tf_op jit(solution)/shard_map/fold/pallas_call | solution.py:447
  (11 shorter events, 0.0 us)
Async XLA Ops:
  7.2 64.2 %all-gather.3.cloned.1.call-start = ((), (), s32[]{:S(2)}) async-start(), calls=%async_computation.4 | async-start | bytes 4456448 | tf_op jit(solution)/shard_map/all_gather | solution.py:461
  7.9 16.6 %copy-start.1 = (bf16[1,128,1024]{2,1,0:T(8,128)(2,1)S(1)}, bf16[1,128,1024]{2,1,0:T(8,128)(2,1)}, u32[]{:S(2)}) copy-start(bf16[1,128,1024]{2,1,0:T(8,128)(2,1)} %param.10) | copy-start | bytes 786436
  7.9 22.5 %copy-start.15 = (s32[1,32]{1,0:T(1,128)S(1)}, s32[1,32]{1,0:T(1,128)}, u32[]{:S(2)}) copy-start(s32[1,32]{1,0:T(1,128)} %param.13) | copy-start | bytes 388
  7.9 25.1 %copy-start.14 = (s32[1,32,8]{1,2,0:T(8,128)S(1)}, s32[1,32,8]{1,2,0:T(8,128)}, u32[]{:S(2)}) copy-start(s32[1,32,8]{1,2,0:T(8,128)} %param.12) | copy-start | bytes 3076
  16.6 28.6 %all-to-all-start = ((bf16[16,128,256]{2,1,0:T(8,128)(2,1)}), bf16[16,128,256]{2,1,0:T(8,128)(2,1)S(1)}, u32[]{:S(2)}, u32[]{:S(2)}) async-start(bf16[16,128,256]{2,1,0:T(8,128)(2,1)} %project.1.refs_4_), calls=%async_computation | async-start | bytes 2097152 | tf_op jit(solution)/shard_map/all_to_all | solution.py:463
  24.5 10.0 %collective-permute-start = (bf16[128,1024]{1,0:T(8,128)(2,1)S(1)}, bf16[128,1024]{1,0:T(8,128)(2,1)S(1)}, u32[]{:S(2)}, u32[]{:S(2)}) collective-permute-start(bf16[128,1024]{1,0:T(8,128)(2,1)S(1)} %bitcast.16), channel_id=1, source_target_pairs={{0,32},{16,48},{32,64},{48,80},{64,96},{80,112},{96,0},{112,16},{1... | collective-permute-start | bytes 786440 | tf_op jit(solution)/shard_map/ppermute | solution.py:389
  26.2 14.3 %collective-permute-start.1 = (bf16[128,1024]{1,0:T(8,128)(2,1)S(1)}, bf16[128,1024]{1,0:T(8,128)(2,1)S(1)}, u32[]{:S(2)}, u32[]{:S(2)}) collective-permute-start(bf16[128,1024]{1,0:T(8,128)(2,1)S(1)} %bitcast.17), channel_id=1, source_target_pairs={{0,64},{16,80},{32,96},{48,112},{64,0},{80,16},{96,32},{112,48},{1... | collective-permute-start | bytes 786440 | tf_op jit(solution)/shard_map/ppermute | solution.py:389
  29.1 11.4 %collective-permute-start.2 = (bf16[128,1024]{1,0:T(8,128)(2,1)S(1)}, bf16[128,1024]{1,0:T(8,128)(2,1)S(1)}, u32[]{:S(2)}, u32[]{:S(2)}) collective-permute-start(bf16[128,1024]{1,0:T(8,128)(2,1)S(1)} %bitcast.18), channel_id=1, source_target_pairs={{0,96},{16,112},{32,0},{48,16},{64,32},{80,48},{96,64},{112,80},{1... | collective-permute-start | bytes 786440 | tf_op jit(solution)/shard_map/ppermute | solution.py:389
  34.5 5.9 %copy-start.7 = (bf16[128,1024]{1,0:T(8,128)(2,1)}, bf16[128,1024]{1,0:T(8,128)(2,1)S(1)}, u32[]{:S(2)}) copy-start(bf16[128,1024]{1,0:T(8,128)(2,1)S(1)} %collective-permute-done.refs_1_) | copy-start | bytes 786436
  40.4 0.7 copy-start.8
  41.1 0.7 copy-start.9
  44.1 49.7 %collective-permute-start.8 = (bf16[512,1024]{1,0:T(8,128)(2,1)}, bf16[512,1024]{1,0:T(8,128)(2,1)S(1)}, u32[]{:S(2)}, u32[]{:S(2)}) collective-permute-start(bf16[512,1024]{1,0:T(8,128)(2,1)} %stacked.1.after_ref.refs_4_), channel_id=1, source_target_pairs={{0,16},{16,0},{32,48},{48,32},{64,80},{80,64},{96,112},{112,96},{1... | collective-permute-start | bytes 3145736 | tf_op jit(solution)/shard_map/ppermute | solution.py:391
  45.1 1.0 copy-start.4
  62.1 15.1 %all-to-all-start.1 = ((bf16[16,64,128]{2,1,0:T(8,128)(2,1)}), bf16[16,64,128]{2,1,0:T(8,128)(2,1)S(1)}, u32[]{:S(2)}, u32[]{:S(2)}) async-start(bf16[16,64,128]{2,1,0:T(8,128)(2,1)} %get-tuple-element.17), calls=%async_computation.1 | async-start | bytes 524288 | tf_op jit(solution)/shard_map/all_to_all | solution.py:466
  77.2 6.9 %copy-start.2 = (bf16[16,64,128]{2,1,0:T(8,128)(2,1)}, bf16[16,64,128]{2,1,0:T(8,128)(2,1)S(1)}, u32[]{:S(2)}) copy-start(bf16[16,64,128]{2,1,0:T(8,128)(2,1)S(1)} %all-to-all-done.1.attn_ref) | copy-start | bytes 786436
  77.2 23.9 %all-to-all-start.2 = ((bf16[16,64,384]{2,1,0:T(8,128)(2,1)}), bf16[16,64,384]{2,1,0:T(8,128)(2,1)S(1)}, u32[]{:S(2)}, u32[]{:S(2)}) async-start(bf16[16,64,384]{2,1,0:T(8,128)(2,1)} %get-tuple-element.20), calls=%async_computation.2 | async-start | bytes 1572864 | tf_op jit(solution)/shard_map/all_to_all | solution.py:469
  81.7 2.4 %collective-permute-start.4 = (bf16[8,192,128]{2,1,0:T(8,128)(2,1)}, bf16[8,192,128]{2,1,0:T(8,128)(2,1)S(1)}, u32[]{:S(2)}, u32[]{:S(2)}) collective-permute-start(bf16[8,192,128]{2,1,0:T(8,128)(2,1)} %get-tuple-element.23.qkv_ref), channel_id=1, source_target_pairs={{0,16},{16,0},{32,48},{48,32},{64,80},{80,64},{96,112},{112,96},{1... | collective-permute-start | bytes 1179656 | tf_op jit(solution)/shard_map/ppermute | solution.py:379
  82.0 2.1 %collective-permute-start.3 = (bf16[16,64,128]{2,1,0:T(8,128)(2,1)S(1)}, bf16[16,64,128]{2,1,0:T(8,128)(2,1)S(1)}, u32[]{:S(2)}, u32[]{:S(2)}) collective-permute-start(bf16[16,64,128]{2,1,0:T(8,128)(2,1)S(1)} %all-to-all-done.1.attn_ref), channel_id=1, source_target_pairs={{0,16},{16,0},{32,48},{48,32},{64,80},{80,64},{96,112},{112,96},{1... | collective-permute-start | bytes 786440 | tf_op jit(solution)/shard_map/ppermute | solution.py:379
  84.1 0.7 copy-start.10
  84.8 0.8 copy-start.6
  87.6 7.6 %collective-permute-start.5 = (bf16[448,128]{1,0:T(8,128)(2,1)}, bf16[448,128]{1,0:T(8,128)(2,1)S(1)}, u32[]{:S(2)}, u32[]{:S(2)}) collective-permute-start(bf16[448,128]{1,0:T(8,128)(2,1)} %get-tuple-element.25), channel_id=1, source_target_pairs={{0,64},{16,80},{32,96},{48,112},{64,0},{80,16},{96,32},{112,48},{1... | collective-permute-start | bytes 344072 | tf_op jit(solution)/shard_map/ppermute | solution.py:380
  90.6 6.7 %collective-permute-start.6 = (bf16[448,128]{1,0:T(8,128)(2,1)}, bf16[448,128]{1,0:T(8,128)(2,1)S(1)}, u32[]{:S(2)}, u32[]{:S(2)}) collective-permute-start(bf16[448,128]{1,0:T(8,128)(2,1)} %get-tuple-element.26), channel_id=1, source_target_pairs={{0,32},{16,48},{32,64},{48,80},{64,96},{80,112},{96,0},{112,16},{1... | collective-permute-start | bytes 344072 | tf_op jit(solution)/shard_map/ppermute | solution.py:380
  91.2 6.1 %collective-permute-start.7 = (bf16[448,128]{1,0:T(8,128)(2,1)}, bf16[448,128]{1,0:T(8,128)(2,1)S(1)}, u32[]{:S(2)}, u32[]{:S(2)}) collective-permute-start(bf16[448,128]{1,0:T(8,128)(2,1)} %get-tuple-element.27), channel_id=1, source_target_pairs={{0,96},{16,112},{32,0},{48,16},{64,32},{80,48},{96,64},{112,80},{1... | collective-permute-start | bytes 344072 | tf_op jit(solution)/shard_map/ppermute | solution.py:380
  93.9 3.4 %copy-start.5 = (bf16[512,1024]{1,0:T(8,128)(2,1)}, bf16[512,1024]{1,0:T(8,128)(2,1)S(1)}, u32[]{:S(2)}) copy-start(bf16[512,1024]{1,0:T(8,128)(2,1)S(1)} %collective-permute-done.8.refs_5_) | copy-start | bytes 3145732
  95.2 2.1 %copy-start.11 = (bf16[448,128]{1,0:T(8,128)(2,1)}, bf16[448,128]{1,0:T(8,128)(2,1)S(1)}, u32[]{:S(2)}) copy-start(bf16[448,128]{1,0:T(8,128)(2,1)S(1)} %collective-permute-done.5.refs_1_) | copy-start | bytes 344068
  97.3 0.7 copy-start.12
  97.3 0.7 copy-start.13
  101.1 7.0 %copy-start = (bf16[16,64,384]{2,1,0:T(8,128)(2,1)}, bf16[16,64,384]{2,1,0:T(8,128)(2,1)S(1)}, u32[]{:S(2)}) copy-start(bf16[16,64,384]{2,1,0:T(8,128)(2,1)S(1)} %all-to-all-done.2.grads_ref) | copy-start | bytes 2359300
  101.1 15.8 %all-to-all-start.3 = ((bf16[16,16,640]{2,1,0:T(8,128)(2,1)}), bf16[16,16,640]{2,1,0:T(8,128)(2,1)S(1)}, u32[]{:S(2)}, u32[]{:S(2)}) async-start(bf16[16,16,640]{2,1,0:T(8,128)(2,1)} %weight_out.1), calls=%async_computation.3 | async-start | bytes 655360 | tf_op jit(solution)/shard_map/all_to_all | solution.py:471
  116.9 0.7 copy-start.3
Sparse Core Ops, SparseCore 0:
  10.1 61.1 all-gather.2

commit v5 on v3

--- a/solution.py
+++ b/solution.py
@@ -322,7 +322,7 @@
     )(*blocks, after)
 
 
-def weight_qkv_kernel(out_ref, nodes_ref, grads_ref, sent_ref, through_ref):
+def weight_qkv_kernel(out_ref, nodes_ref, sent_ref):
     total = None
     for t in range(NODES // CHUNK):
         rows = slice(t * CHUNK, (t + 1) * CHUNK)
@@ -334,29 +334,24 @@
         sent_ref[i] = total[:, i * ROWS : (i + 1) * ROWS].astype(jnp.bfloat16)
 
 
-def weight_qkv(head_out, all_nodes, grads):
-    vmem = pl.BlockSpec(memory_space=pltpu.VMEM)
-    anywhere = pl.BlockSpec(memory_space=pl.ANY)
+def weight_qkv(head_out, all_nodes):
+    vmem = pl.BlockSpec(memory_space=pltpu.VMEM)
     return pl.pallas_call(
         weight_qkv_kernel,
-        out_shape=(
-            jax.ShapeDtypeStruct((DP, 3 * HD, ROWS), jnp.bfloat16),
-            jax.ShapeDtypeStruct(grads.shape, grads.dtype),
-        ),
-        in_specs=[vmem, vmem, anywhere],
-        out_specs=(vmem, anywhere),
-        input_output_aliases={2: 1},
+        out_shape=jax.ShapeDtypeStruct((DP, 3 * HD, ROWS), jnp.bfloat16),
+        in_specs=[vmem, vmem],
+        out_specs=vmem,
         compiler_params=pltpu.CompilerParams(vmem_limit_bytes=VMEM_BYTES),
         cost_estimate=pl.CostEstimate(flops=2 * NODES * D * 3 * HD, bytes_accessed=6_000_000, transcendentals=0),
         name="weight_qkv",
-    )(head_out, all_nodes, grads)
-
-
-def chips_kernel(attn_ref, qkv_ref, other_attn_ref, other_qkv_ref, *sent_refs):
+    )(head_out, all_nodes)
+
+
+def chips_kernel(attn_ref, qkv_ref, other_attn_ref, other_qkv_ref, grads_ref, *sent_refs):
     me = lax.axis_index("dp")
     y, core = me // CORES, me % CORES
     first = core == 0
-    for step, ref in enumerate(sent_refs):
+    for step, ref in enumerate(sent_refs[:CHIPS]):
         i = ((y + step) % CHIPS) * CORES + core
         for k in range(2):
             own, other = attn_ref[2 * i + k], other_attn_ref[2 * i + k]
@@ -366,20 +361,22 @@
         ref[2 * ROWS :] = total.astype(jnp.bfloat16)
 
 
-def over_dp(attn, part_qkv):
+def over_dp(attn, part_qkv, grads):
     pairs = [(i, i ^ 1) for i in range(DP)]
     vmem = pl.BlockSpec(memory_space=pltpu.VMEM)
+    anywhere = pl.BlockSpec(memory_space=pl.ANY)
     shape = jax.ShapeDtypeStruct((2 * ROWS + 3 * HD, ROWS), jnp.bfloat16)
-    parts = pl.pallas_call(
+    *parts, grads = pl.pallas_call(
         chips_kernel,
-        out_shape=(shape,) * CHIPS,
-        in_specs=[vmem] * 4,
-        out_specs=(vmem,) * CHIPS,
+        out_shape=(shape,) * CHIPS + (jax.ShapeDtypeStruct(grads.shape, grads.dtype),),
+        in_specs=[vmem] * 4 + [anywhere],
+        out_specs=(vmem,) * CHIPS + (anywhere,),
+        input_output_aliases={4: CHIPS},
         compiler_params=pltpu.CompilerParams(vmem_limit_bytes=VMEM_BYTES),
         cost_estimate=pl.CostEstimate(flops=0, bytes_accessed=2_000_000, transcendentals=0),
         name="chips",
-    )(attn, part_qkv, lax.ppermute(attn, "dp", pairs), lax.ppermute(part_qkv, "dp", pairs))
-    return parts[0], *(lax.ppermute(parts[step], "dp", chip_shift(step)) for step in (1, 2, 3))
+    )(attn, part_qkv, lax.ppermute(attn, "dp", pairs), lax.ppermute(part_qkv, "dp", pairs), grads)
+    return (parts[0], *(lax.ppermute(parts[step], "dp", chip_shift(step)) for step in (1, 2, 3))), grads
 
 
 def chip_shift(step):
@@ -393,7 +390,7 @@
 
 
 def weight_out_kernel(*refs):
-    parts, (mine_ref, other_ref, sent_ref) = refs[:CHIPS], refs[CHIPS:]
+    parts, (mine_ref, other_ref, _, sent_ref) = refs[:CHIPS], refs[CHIPS:]
     core = lax.axis_index("dp") % CORES
     total, mine, other = None, [], []
     for ref in parts:
@@ -419,17 +416,17 @@
         ).astype(jnp.bfloat16)
 
 
-def weight_out(parts, mine, other):
+def weight_out(parts, mine, other, after):
     vmem = pl.BlockSpec(memory_space=pltpu.VMEM)
     return pl.pallas_call(
         weight_out_kernel,
         out_shape=jax.ShapeDtypeStruct((SEQ, 16, D // 2 + 2 * HD), jnp.bfloat16),
-        in_specs=[vmem] * (CHIPS + 2),
+        in_specs=[vmem] * (CHIPS + 2) + [pl.BlockSpec(memory_space=pl.ANY)],
         out_specs=vmem,
         compiler_params=pltpu.CompilerParams(vmem_limit_bytes=VMEM_BYTES),
         cost_estimate=pl.CostEstimate(flops=2 * DP * ROWS * D * ROWS, bytes_accessed=3_000_000, transcendentals=0),
         name="weight_out",
-    )(*parts, mine, other)
+    )(*parts, mine, other, after)
 
 
 def fold_kernel(parts_ref, qkv_ref, out_ref):
@@ -466,9 +463,9 @@
     head_out, attn_sent, grads_sent = attention(block_list[0], block_count[0], order, head_rows, upstreams[0])
     attn = lax.all_to_all(attn_sent, "seq", 0, 0, tiled=True)
 
-    part_qkv, grads_sent = weight_qkv(head_out, all_nodes, grads_sent)
+    exchanged, grads_sent = over_dp(attn, weight_qkv(head_out, all_nodes), grads_sent)
     grads = lax.all_to_all(grads_sent, "seq", 0, 0, tiled=True)
-    parts = weight_out(over_dp(attn, part_qkv), *upstreams)
+    parts = weight_out(exchanged, *upstreams, grads)
     grad_qkv, grad_out = fold(lax.all_to_all(parts, "seq", 0, 0, tiled=True))
 
     mixed, grad_nodes = finish(features, upstream, attn, grads, w_qkv, w_out)

time: 127 us -> 131 us (1.031); the launches traced: 127 us -> 129 us
  waiting for transfers between devices: 19.7 us -> 25.2 us
  starting transfers between devices: 38 us -> 36 us
    all_to_all x1, waiting for transfers between devices: 0.01 us -> 4.52 us  [shards(): grads = lax.all_to_all(grads_sent, 'seq', 0, 0, tiled=True)]
    all_to_all x1, starting transfers between devices: 6.96 us -> 3.54 us  [shards(): grad_qkv, grad_out = fold(lax.all_to_all(parts, 'seq', 0, 0, tiled=True))]
    all_gather x1, waiting for transfers between devices: 2.99 us -> 4.44 us  [shards(): all_nodes = lax.all_gather(features, 'seq', axis=0, tiled=True)]
    unnamed x33 -> x35, local copies, waits for them, and re-layouts: 5.93 us -> 5.52 us
  transfers between devices with their start and end apart: 14 -> 14, of which waited for: 8 -> 7; matrix products, arithmetic and copies ran while one was open for 3% -> 3% of each run, Pallas kernels for 35% -> 31%
where the time goes in v5:
time: 131 us; the launch traced here: 129 us
  Pallas kernels  45 us (34%)
  starting transfers between devices  36 us (27%)
  waiting for transfers between devices  25.2 us (19%)
  between operations  14.2 us (11%)
  local copies, waits for them, and re-layouts  5.52 us (4%)
  other arithmetic  3.42 us (3%)
    pallas_call x1, Pallas kernels, attention(): pl.pallas_call(attention_kernel, out_shape=(jax.ShapeDtypeStruct((NODES,...  15.7 us
    pallas_call x1, Pallas kernels, project(): pl.pallas_call(project_kernel, grid=(H // FEW,), out_shape=(jax.ShapeDtyp...  8.61 us
    all_to_all x1, starting transfers between devices, shards(): lax.all_to_all(sent, 'seq', 0, 0, tiled=True).reshape(NODES, WIDE)  7.96 us
    ppermute x3, starting transfers between devices, over_dp(): lax.ppermute(parts[step], 'dp', chip_shift(step))  6.75 us
    pallas_call x1, Pallas kernels, finish(): pl.pallas_call(finish_kernel, grid=(H // STEP,), out_shape=(jax.ShapeDtyp...  6.5 us
    all_to_all x1, starting transfers between devices, shards(): attn = lax.all_to_all(attn_sent, 'seq', 0, 0, tiled=True)  6.08 us
    ppermute x3, waiting for transfers between devices, batches_of(): moved = [lax.ppermute(block, 'dp', chip_shift(step)) for step in (1, 2, 3)]  5.9 us
    ppermute x3, starting transfers between devices, batches_of(): moved = [lax.ppermute(block, 'dp', chip_shift(step)) for step in (1, 2, 3)]  5.89 us
  transfers between devices with their start and end apart: 14, of which 7 were waited for; matrix products, arithmetic and copies ran while one was open for 3% of the time, Pallas kernels for 31%

profile of v5, /device:TPU:0, one launch (start us, length us, event | category | flops | bytes accessed | tf_op | source)
XLA Modules:
  0.0 129.2 jit_solution(12609573178653372376)
XLA Ops:
  7.2 0.0 all-gather.3.cloned.1.call-start
  7.2 0.7 all-gather.3.cloned.1.call-update
  7.9 0.0 copy-start.2
  7.9 0.0 copy-start.16
  7.9 0.0 copy-start.15
  7.9 8.6 %project.1 = (bf16[16,128,256]{2,1,0:T(8,128)(2,1)}, bf16[128,1024]{1,0:T(8,128)(2,1)}) custom-call(bf16[128,1024]{1,0:T(8,128)(2,1)} %bitcast.19, bf16[128,1024]{1,0:T(8,128)(2,1)} %bitcast.13, bf16[1024,3072]{1,0:T(8,128)(2,1)} %w_qkv_ref.3, bf16[1024,1024]{1,0:T(8,128)(2,1)} %w_out_ref.3), custom_call_target="tpu_custom_call" | custom-call | flops 1073741824 | bytes 9500000 | tf_op jit(solution)/shard_map/project/pallas_call | solution.py:225
  16.5 8.0 %all-to-all-start = ((bf16[16,128,256]{2,1,0:T(8,128)(2,1)}), bf16[16,128,256]{2,1,0:T(8,128)(2,1)S(1)}, u32[]{:S(2)}, u32[]{:S(2)}) async-start(bf16[16,128,256]{2,1,0:T(8,128)(2,1)} %get-tuple-element.17.refs_4_), calls=%async_computation | async-start | bytes 2097152 | tf_op jit(solution)/shard_map/all_to_all | solution.py:461
  24.5 0.0 copy-done.2
  24.5 1.6 %collective-permute-start = (bf16[128,1024]{1,0:T(8,128)(2,1)S(1)}, bf16[128,1024]{1,0:T(8,128)(2,1)S(1)}, u32[]{:S(2)}, u32[]{:S(2)}) collective-permute-start(bf16[128,1024]{1,0:T(8,128)(2,1)S(1)} %bitcast.16), channel_id=1, source_target_pairs={{0,32},{16,48},{32,64},{48,80},{64,96},{80,112},{96,0},{112,16},{1... | collective-permute-start | bytes 786440 | tf_op jit(solution)/shard_map/ppermute | solution.py:387
  26.2 2.9 %collective-permute-start.1 = (bf16[128,1024]{1,0:T(8,128)(2,1)S(1)}, bf16[128,1024]{1,0:T(8,128)(2,1)S(1)}, u32[]{:S(2)}, u32[]{:S(2)}) collective-permute-start(bf16[128,1024]{1,0:T(8,128)(2,1)S(1)} %bitcast.17), channel_id=1, source_target_pairs={{0,64},{16,80},{32,96},{48,112},{64,0},{80,16},{96,32},{112,48},{1... | collective-permute-start | bytes 786440 | tf_op jit(solution)/shard_map/ppermute | solution.py:387
  29.1 1.3 %collective-permute-start.2 = (bf16[128,1024]{1,0:T(8,128)(2,1)S(1)}, bf16[128,1024]{1,0:T(8,128)(2,1)S(1)}, u32[]{:S(2)}, u32[]{:S(2)}) collective-permute-start(bf16[128,1024]{1,0:T(8,128)(2,1)S(1)} %bitcast.18), channel_id=1, source_target_pairs={{0,96},{16,112},{32,0},{48,16},{64,32},{80,48},{96,64},{112,80},{1... | collective-permute-start | bytes 786440 | tf_op jit(solution)/shard_map/ppermute | solution.py:387
  30.4 0.0 copy-done.16
  30.4 0.6 fusion.2
  31.1 1.4 %and_select_fusion = s32[2]{0:T(128)S(1)} fusion(s32[1]{0:T(128)} %bitcast.5, s32[1]{0:T(128)} %bitcast.4), kind=kLoop, calls=%fused_computation.6 | loop fusion | flops 34 | bytes 16 | tf_op jit(solution)/shard_map/jit(floor_divide)/jit(_where)/select_n | solution.py:178
  32.4 0.6 pad_add_fusion.bounds_ref
  33.0 0.0 copy-done.15
  33.0 0.7 copy.13
  33.7 0.2 convert_reduce_fusion
  33.9 0.6 select_reduce_fusion.ranked_ref
  34.5 0.0 collective-permute-done.refs_1_
  34.5 5.9 %collective-permute-done.1.refs_2_ = bf16[128,1024]{1,0:T(8,128)(2,1)S(1)} collective-permute-done((bf16[128,1024]{1,0:T(8,128)(2,1)S(1)}, bf16[128,1024]{1,0:T(8,128)(2,1)S(1)}, u32[]{:S(2)}, u32[]{:S(2)}) %collective-permute-start.1) | collective-permute-done | bytes 262176 | tf_op jit(solution)/shard_map/ppermute | solution.py:387
  40.4 0.0 collective-permute-done.2.refs_3_
  40.4 0.0 copy-done.8
  40.4 0.7 copy-done.9
  41.1 0.7 copy-done.10
  41.8 2.3 %stacked.1.after_ref.refs_4_ = bf16[512,1024]{1,0:T(8,128)(2,1)} custom-call(bf16[128,1024]{1,0:T(8,128)(2,1)} %bitcast.14, bf16[128,1024]{1,0:T(8,128)(2,1)} %copy-done.8, bf16[128,1024]{1,0:T(8,128)(2,1)} %copy-done.9, bf16[128,1024]{1,0:T(8,128)(2,1)} %copy-done.10, bf16[16,128,256]{2,1,0:T(8,128)(2,1)} %get-tuple-element.17.refs_4_), custom_call_target="tpu_custom_call" | custom-call | bytes 2097152 | tf_op jit(solution)/shard_map/stacked/pallas_call | solution.py:314
  44.1 1.0 all-to-all-done
  45.1 1.0 copy-done.6
  46.1 15.7 %clustered_attention.1 = (bf16[2048,256]{1,0:T(8,128)(2,1)}, bf16[16,64,128]{2,1,0:T(8,128)(2,1)}, bf16[16,64,384]{2,1,0:T(8,128)(2,1)}) custom-call(s32[32,8]{1,0:T(8,128)} %bitcast.22, s32[32]{0:T(128)} %bitcast.25, s32[32]{0:T(128)} %select_reduce_fusion.ranked_ref, s32[3]{0:T(128)} %pad_add_fusion.bounds_ref, s32[1,2048]{1,0:T(1,128)} %order_ref.1, ...), custom_call_target="tpu_custom_call" | custom-call | flops 10000000000 | bytes 4000000 | tf_op jit(solution)/shard_map/clustered_attention/pallas_call | solution.py:186
  61.8 6.1 %all-to-all-start.1 = ((bf16[16,64,128]{2,1,0:T(8,128)(2,1)}), bf16[16,64,128]{2,1,0:T(8,128)(2,1)S(1)}, u32[]{:S(2)}, u32[]{:S(2)}) async-start(bf16[16,64,128]{2,1,0:T(8,128)(2,1)} %get-tuple-element.18), calls=%async_computation.1 | async-start | bytes 524288 | tf_op jit(solution)/shard_map/all_to_all | solution.py:464
  67.8 4.4 %all-gather.3.cloned.1.call-done = bf16[1,2048,1024]{2,1,0:T(8,128)(2,1)} async-done(((bf16[1,128,1024]{2,1,0:T(8,128)(2,1)}), bf16[1,2048,1024]{2,1,0:T(8,128)(2,1)}) %all-gather.3.cloned.1.call-update) | async-done | bytes 4194320 | tf_op jit(solution)/shard_map/all_gather | solution.py:459
  72.3 5.1 %weight_qkv.1.qkv_ref = bf16[8,192,128]{2,1,0:T(8,128)(2,1)} custom-call(bf16[2048,256]{1,0:T(8,128)(2,1)} %get-tuple-element.19.out_ref, bf16[2048,1024]{1,0:T(8,128)(2,1)} %bitcast.12), custom_call_target="tpu_custom_call" | custom-call | flops 805306368 | bytes 6000000 | tf_op jit(solution)/shard_map/weight_qkv/pallas_call | solution.py:339
  77.4 0.0 collective-permute-start.4
  77.4 0.0 copy-done.1
  77.4 0.5 collective-permute-start.8
  77.9 0.0 all-to-all-done.1.attn_ref
  77.9 0.3 collective-permute-start.3
  78.2 2.8 %collective-permute-done.3.other_attn_ref = bf16[16,64,128]{2,1,0:T(8,128)(2,1)S(1)} collective-permute-done((bf16[16,64,128]{2,1,0:T(8,128)(2,1)S(1)}, bf16[16,64,128]{2,1,0:T(8,128)(2,1)S(1)}, u32[]{:S(2)}, u32[]{:S(2)}) %collective-permute-start.3) | collective-permute-done | bytes 262176 | tf_op jit(solution)/shard_map/ppermute | solution.py:378
  81.0 0.0 collective-permute-done.4.other_qkv_ref
  81.0 0.0 copy-done.3
  81.0 0.7 copy-done.11
  81.7 0.1 copy-done.7
  81.8 2.1 %chips.1 = (bf16[448,128]{1,0:T(8,128)(2,1)}, bf16[448,128]{1,0:T(8,128)(2,1)}, bf16[448,128]{1,0:T(8,128)(2,1)}, bf16[448,128]{1,0:T(8,128)(2,1)}, bf16[16,64,384]{2,1,0:T(8,128)(2,1)}) custom-call(bf16[16,64,128]{2,1,0:T(8,128)(2,1)} %copy-done.3, bf16[8,192,128]{2,1,0:T(8,128)(2,1)} %weight_qkv.1.qkv_ref, ...), custom_call_target="tpu_custom_call", output_to_operand_aliasing={{4}: (4, {})} | custom-call | bytes 2000000 | tf_op jit(solution)/shard_map/chips/pallas_call | solution.py:369
  83.9 4.9 %all-to-all-start.2 = ((bf16[16,64,384]{2,1,0:T(8,128)(2,1)}), bf16[16,64,384]{2,1,0:T(8,128)(2,1)S(1)}, u32[]{:S(2)}, u32[]{:S(2)}) async-start(bf16[16,64,384]{2,1,0:T(8,128)(2,1)} %get-tuple-element.21), calls=%async_computation.2 | async-start | bytes 1572864 | tf_op jit(solution)/shard_map/all_to_all | solution.py:467
  88.8 1.5 %collective-permute-start.5 = (bf16[448,128]{1,0:T(8,128)(2,1)}, bf16[448,128]{1,0:T(8,128)(2,1)S(1)}, u32[]{:S(2)}, u32[]{:S(2)}) collective-permute-start(bf16[448,128]{1,0:T(8,128)(2,1)} %get-tuple-element.25), channel_id=1, source_target_pairs={{0,32},{16,48},{32,64},{48,80},{64,96},{80,112},{96,0},{112,16},{1... | collective-permute-start | bytes 344072 | tf_op jit(solution)/shard_map/ppermute | solution.py:379
  90.4 3.2 %collective-permute-start.6 = (bf16[448,128]{1,0:T(8,128)(2,1)}, bf16[448,128]{1,0:T(8,128)(2,1)S(1)}, u32[]{:S(2)}, u32[]{:S(2)}) collective-permute-start(bf16[448,128]{1,0:T(8,128)(2,1)} %get-tuple-element.26), channel_id=1, source_target_pairs={{0,64},{16,80},{32,96},{48,112},{64,0},{80,16},{96,32},{112,48},{1... | collective-permute-start | bytes 344072 | tf_op jit(solution)/shard_map/ppermute | solution.py:379
  93.6 2.0 %collective-permute-start.7 = (bf16[448,128]{1,0:T(8,128)(2,1)}, bf16[448,128]{1,0:T(8,128)(2,1)S(1)}, u32[]{:S(2)}, u32[]{:S(2)}) collective-permute-start(bf16[448,128]{1,0:T(8,128)(2,1)} %get-tuple-element.27), channel_id=1, source_target_pairs={{0,96},{16,112},{32,0},{48,16},{64,32},{80,48},{96,64},{112,80},{1... | collective-permute-start | bytes 344072 | tf_op jit(solution)/shard_map/ppermute | solution.py:379
  95.6 0.0 collective-permute-done.8.refs_5_
  95.6 0.0 collective-permute-done.5.refs_1_
  95.6 0.0 copy-start.12
  95.6 3.5 %collective-permute-done.6.refs_2_ = bf16[448,128]{1,0:T(8,128)(2,1)S(1)} collective-permute-done((bf16[448,128]{1,0:T(8,128)(2,1)}, bf16[448,128]{1,0:T(8,128)(2,1)S(1)}, u32[]{:S(2)}, u32[]{:S(2)}) %collective-permute-start.6) | collective-permute-done | bytes 114720 | tf_op jit(solution)/shard_map/ppermute | solution.py:379
  99.2 0.0 collective-permute-done.7.refs_3_
  99.2 4.5 %all-to-all-done.2.grads_ref.refs_6_ = bf16[16,64,384]{2,1,0:T(8,128)(2,1)S(1)} async-done(((bf16[16,64,384]{2,1,0:T(8,128)(2,1)}), bf16[16,64,384]{2,1,0:T(8,128)(2,1)S(1)}, u32[]{:S(2)}, u32[]{:S(2)}) %all-to-all-start.2) | async-done | bytes 786464 | tf_op jit(solution)/shard_map/all_to_all | solution.py:467
  103.7 0.0 copy-done.5
  103.7 0.0 copy-done.12
  103.7 0.0 copy-done.13
  103.7 0.0 copy-done.14
  103.7 0.9 copy-done
  104.6 3.1 %weight_out.1 = bf16[16,16,640]{2,1,0:T(8,128)(2,1)} custom-call(bf16[448,128]{1,0:T(8,128)(2,1)} %get-tuple-element.24.refs_0_, bf16[448,128]{1,0:T(8,128)(2,1)} %copy-done.12, bf16[448,128]{1,0:T(8,128)(2,1)} %copy-done.13, bf16[448,128]{1,0:T(8,128)(2,1)} %copy-done.14, bf16[512,1024]{1,0:T(8,128)(2,1)} %stacked.1.after_ref.refs_4_, ...), custom_call_target="tpu_custom_call" | custom-call | flops 268435456 | bytes 3000000 | tf_op jit(solution)/shard_map/weight_out/pallas_call | solution.py:421
  107.6 3.5 %all-to-all-start.3 = ((bf16[16,16,640]{2,1,0:T(8,128)(2,1)}), bf16[16,16,640]{2,1,0:T(8,128)(2,1)S(1)}, u32[]{:S(2)}, u32[]{:S(2)}) async-start(bf16[16,16,640]{2,1,0:T(8,128)(2,1)} %weight_out.1), calls=%async_computation.3 | async-start | bytes 655360 | tf_op jit(solution)/shard_map/all_to_all | solution.py:469
  111.2 6.5 %finish.1 = (bf16[128,1024]{1,0:T(8,128)(2,1)}, bf16[128,1024]{1,0:T(8,128)(2,1)}) custom-call(bf16[128,1024]{1,0:T(8,128)(2,1)} %bitcast.20, bf16[128,1024]{1,0:T(8,128)(2,1)} %bitcast.15, bf16[16,64,128]{2,1,0:T(8,128)(2,1)} %copy-done.3, bf16[16,64,384]{2,1,0:T(8,128)(2,1)} %copy-done, bf16[1024,3072]{1,0:T(8,128)(2,1)} %w_qkv_ref.3, ...), custom_call_target="tpu_custom_call" | custom-call | flops 1073741824 | bytes 10000000 | tf_op jit(solution)/shard_map/finish/pallas_call | solution.py:284
  117.7 2.3 %all-to-all-done.3.parts_ref = bf16[16,16,640]{2,1,0:T(8,128)(2,1)S(1)} async-done(((bf16[16,16,640]{2,1,0:T(8,128)(2,1)}), bf16[16,16,640]{2,1,0:T(8,128)(2,1)S(1)}, u32[]{:S(2)}, u32[]{:S(2)}) %all-to-all-start.3) | async-done | bytes 327712 | tf_op jit(solution)/shard_map/all_to_all | solution.py:469
  120.0 0.7 copy-done.4
  120.7 1.7 %fold.1 = (f32[8,3072]{1,0:T(8,128)}, f32[8,1024]{1,0:T(8,128)}) custom-call(bf16[16,16,640]{2,1,0:T(8,128)(2,1)} %copy-done.4), custom_call_target="tpu_custom_call" | custom-call | tf_op jit(solution)/shard_map/fold/pallas_call | solution.py:445
  (13 shorter events, 0.0 us)
Async XLA Ops:
  7.2 65.1 %all-gather.3.cloned.1.call-start = ((), (), s32[]{:S(2)}) async-start(), calls=%async_computation.4 | async-start | bytes 4456448 | tf_op jit(solution)/shard_map/all_gather | solution.py:459
  7.9 16.6 %copy-start.2 = (bf16[1,128,1024]{2,1,0:T(8,128)(2,1)S(1)}, bf16[1,128,1024]{2,1,0:T(8,128)(2,1)}, u32[]{:S(2)}) copy-start(bf16[1,128,1024]{2,1,0:T(8,128)(2,1)} %param.10) | copy-start | bytes 786436
  7.9 22.5 %copy-start.16 = (s32[1,32]{1,0:T(1,128)S(1)}, s32[1,32]{1,0:T(1,128)}, u32[]{:S(2)}) copy-start(s32[1,32]{1,0:T(1,128)} %param.13) | copy-start | bytes 388
  7.9 25.1 %copy-start.15 = (s32[1,32,8]{1,2,0:T(8,128)S(1)}, s32[1,32,8]{1,2,0:T(8,128)}, u32[]{:S(2)}) copy-start(s32[1,32,8]{1,2,0:T(8,128)} %param.12) | copy-start | bytes 3076
  16.5 28.6 %all-to-all-start = ((bf16[16,128,256]{2,1,0:T(8,128)(2,1)}), bf16[16,128,256]{2,1,0:T(8,128)(2,1)S(1)}, u32[]{:S(2)}, u32[]{:S(2)}) async-start(bf16[16,128,256]{2,1,0:T(8,128)(2,1)} %get-tuple-element.17.refs_4_), calls=%async_computation | async-start | bytes 2097152 | tf_op jit(solution)/shard_map/all_to_all | solution.py:461
  24.5 10.0 %collective-permute-start = (bf16[128,1024]{1,0:T(8,128)(2,1)S(1)}, bf16[128,1024]{1,0:T(8,128)(2,1)S(1)}, u32[]{:S(2)}, u32[]{:S(2)}) collective-permute-start(bf16[128,1024]{1,0:T(8,128)(2,1)S(1)} %bitcast.16), channel_id=1, source_target_pairs={{0,32},{16,48},{32,64},{48,80},{64,96},{80,112},{96,0},{112,16},{1... | collective-permute-start | bytes 786440 | tf_op jit(solution)/shard_map/ppermute | solution.py:387
  26.2 14.3 %collective-permute-start.1 = (bf16[128,1024]{1,0:T(8,128)(2,1)S(1)}, bf16[128,1024]{1,0:T(8,128)(2,1)S(1)}, u32[]{:S(2)}, u32[]{:S(2)}) collective-permute-start(bf16[128,1024]{1,0:T(8,128)(2,1)S(1)} %bitcast.17), channel_id=1, source_target_pairs={{0,64},{16,80},{32,96},{48,112},{64,0},{80,16},{96,32},{112,48},{1... | collective-permute-start | bytes 786440 | tf_op jit(solution)/shard_map/ppermute | solution.py:387
  29.1 11.4 %collective-permute-start.2 = (bf16[128,1024]{1,0:T(8,128)(2,1)S(1)}, bf16[128,1024]{1,0:T(8,128)(2,1)S(1)}, u32[]{:S(2)}, u32[]{:S(2)}) collective-permute-start(bf16[128,1024]{1,0:T(8,128)(2,1)S(1)} %bitcast.18), channel_id=1, source_target_pairs={{0,96},{16,112},{32,0},{48,16},{64,32},{80,48},{96,64},{112,80},{1... | collective-permute-start | bytes 786440 | tf_op jit(solution)/shard_map/ppermute | solution.py:387
  34.5 5.9 %copy-start.8 = (bf16[128,1024]{1,0:T(8,128)(2,1)}, bf16[128,1024]{1,0:T(8,128)(2,1)S(1)}, u32[]{:S(2)}) copy-start(bf16[128,1024]{1,0:T(8,128)(2,1)S(1)} %collective-permute-done.refs_1_) | copy-start | bytes 786436
  40.4 0.7 copy-start.9
  41.1 0.7 copy-start.10
  45.1 1.0 copy-start.6
  61.8 15.6 %copy-start.1 = (bf16[512,1024]{1,0:T(8,128)(2,1)S(1)}, bf16[512,1024]{1,0:T(8,128)(2,1)}, u32[]{:S(2)}) copy-start(bf16[512,1024]{1,0:T(8,128)(2,1)} %stacked.1.after_ref.refs_4_) | copy-start | bytes 3145732
  61.8 16.1 %all-to-all-start.1 = ((bf16[16,64,128]{2,1,0:T(8,128)(2,1)}), bf16[16,64,128]{2,1,0:T(8,128)(2,1)S(1)}, u32[]{:S(2)}, u32[]{:S(2)}) async-start(bf16[16,64,128]{2,1,0:T(8,128)(2,1)} %get-tuple-element.18), calls=%async_computation.1 | async-start | bytes 524288 | tf_op jit(solution)/shard_map/all_to_all | solution.py:464
  77.4 3.6 %collective-permute-start.4 = (bf16[8,192,128]{2,1,0:T(8,128)(2,1)}, bf16[8,192,128]{2,1,0:T(8,128)(2,1)S(1)}, u32[]{:S(2)}, u32[]{:S(2)}) collective-permute-start(bf16[8,192,128]{2,1,0:T(8,128)(2,1)} %weight_qkv.1.qkv_ref), channel_id=1, source_target_pairs={{0,16},{16,0},{32,48},{48,32},{64,80},{80,64},{96,112},{112,96},{1... | collective-permute-start | bytes 1179656 | tf_op jit(solution)/shard_map/ppermute | solution.py:378
  77.4 18.2 %collective-permute-start.8 = (bf16[512,1024]{1,0:T(8,128)(2,1)S(1)}, bf16[512,1024]{1,0:T(8,128)(2,1)S(1)}, u32[]{:S(2)}, u32[]{:S(2)}) collective-permute-start(bf16[512,1024]{1,0:T(8,128)(2,1)S(1)} %copy-done.1), channel_id=1, source_target_pairs={{0,16},{16,0},{32,48},{48,32},{64,80},{80,64},{96,112},{112,96},{1... | collective-permute-start | bytes 3145736 | tf_op jit(solution)/shard_map/ppermute | solution.py:389
  77.9 3.1 %copy-start.3 = (bf16[16,64,128]{2,1,0:T(8,128)(2,1)}, bf16[16,64,128]{2,1,0:T(8,128)(2,1)S(1)}, u32[]{:S(2)}) copy-start(bf16[16,64,128]{2,1,0:T(8,128)(2,1)S(1)} %all-to-all-done.1.attn_ref) | copy-start | bytes 786436
  77.9 3.1 %collective-permute-start.3 = (bf16[16,64,128]{2,1,0:T(8,128)(2,1)S(1)}, bf16[16,64,128]{2,1,0:T(8,128)(2,1)S(1)}, u32[]{:S(2)}, u32[]{:S(2)}) collective-permute-start(bf16[16,64,128]{2,1,0:T(8,128)(2,1)S(1)} %all-to-all-done.1.attn_ref), channel_id=1, source_target_pairs={{0,16},{16,0},{32,48},{48,32},{64,80},{80,64},{96,112},{112,96},{1... | collective-permute-start | bytes 786440 | tf_op jit(solution)/shard_map/ppermute | solution.py:378
  81.0 0.7 copy-start.11
  81.0 0.8 copy-start.7
  83.9 19.8 %all-to-all-start.2 = ((bf16[16,64,384]{2,1,0:T(8,128)(2,1)}), bf16[16,64,384]{2,1,0:T(8,128)(2,1)S(1)}, u32[]{:S(2)}, u32[]{:S(2)}) async-start(bf16[16,64,384]{2,1,0:T(8,128)(2,1)} %get-tuple-element.21), calls=%async_computation.2 | async-start | bytes 1572864 | tf_op jit(solution)/shard_map/all_to_all | solution.py:467
  88.8 6.8 %collective-permute-start.5 = (bf16[448,128]{1,0:T(8,128)(2,1)}, bf16[448,128]{1,0:T(8,128)(2,1)S(1)}, u32[]{:S(2)}, u32[]{:S(2)}) collective-permute-start(bf16[448,128]{1,0:T(8,128)(2,1)} %get-tuple-element.25), channel_id=1, source_target_pairs={{0,32},{16,48},{32,64},{48,80},{64,96},{80,112},{96,0},{112,16},{1... | collective-permute-start | bytes 344072 | tf_op jit(solution)/shard_map/ppermute | solution.py:379
  90.4 8.8 %collective-permute-start.6 = (bf16[448,128]{1,0:T(8,128)(2,1)}, bf16[448,128]{1,0:T(8,128)(2,1)S(1)}, u32[]{:S(2)}, u32[]{:S(2)}) collective-permute-start(bf16[448,128]{1,0:T(8,128)(2,1)} %get-tuple-element.26), channel_id=1, source_target_pairs={{0,64},{16,80},{32,96},{48,112},{64,0},{80,16},{96,32},{112,48},{1... | collective-permute-start | bytes 344072 | tf_op jit(solution)/shard_map/ppermute | solution.py:379
  93.6 5.6 %collective-permute-start.7 = (bf16[448,128]{1,0:T(8,128)(2,1)}, bf16[448,128]{1,0:T(8,128)(2,1)S(1)}, u32[]{:S(2)}, u32[]{:S(2)}) collective-permute-start(bf16[448,128]{1,0:T(8,128)(2,1)} %get-tuple-element.27), channel_id=1, source_target_pairs={{0,96},{16,112},{32,0},{48,16},{64,32},{80,48},{96,64},{112,80},{1... | collective-permute-start | bytes 344072 | tf_op jit(solution)/shard_map/ppermute | solution.py:379
  95.6 8.1 %copy-start.5 = (bf16[512,1024]{1,0:T(8,128)(2,1)}, bf16[512,1024]{1,0:T(8,128)(2,1)S(1)}, u32[]{:S(2)}) copy-start(bf16[512,1024]{1,0:T(8,128)(2,1)S(1)} %collective-permute-done.8.refs_5_) | copy-start | bytes 3145732
  95.6 8.1 %copy-start.12 = (bf16[448,128]{1,0:T(8,128)(2,1)}, bf16[448,128]{1,0:T(8,128)(2,1)S(1)}, u32[]{:S(2)}) copy-start(bf16[448,128]{1,0:T(8,128)(2,1)S(1)} %collective-permute-done.5.refs_1_) | copy-start | bytes 344068
  99.2 4.5 %copy-start.13 = (bf16[448,128]{1,0:T(8,128)(2,1)}, bf16[448,128]{1,0:T(8,128)(2,1)S(1)}, u32[]{:S(2)}) copy-start(bf16[448,128]{1,0:T(8,128)(2,1)S(1)} %collective-permute-done.6.refs_2_) | copy-start | bytes 344068
  99.2 4.5 %copy-start.14 = (bf16[448,128]{1,0:T(8,128)(2,1)}, bf16[448,128]{1,0:T(8,128)(2,1)S(1)}, u32[]{:S(2)}) copy-start(bf16[448,128]{1,0:T(8,128)(2,1)S(1)} %collective-permute-done.7.refs_3_) | copy-start | bytes 344068
  103.7 0.9 copy-start
  107.6 12.3 %all-to-all-start.3 = ((bf16[16,16,640]{2,1,0:T(8,128)(2,1)}), bf16[16,16,640]{2,1,0:T(8,128)(2,1)S(1)}, u32[]{:S(2)}, u32[]{:S(2)}) async-start(bf16[16,16,640]{2,1,0:T(8,128)(2,1)} %weight_out.1), calls=%async_computation.3 | async-start | bytes 655360 | tf_op jit(solution)/shard_map/all_to_all | solution.py:469
  120.0 0.7 copy-start.4
Sparse Core Ops, SparseCore 0:
  10.1 62.0 all-gather.2
